TPU v7x, 32 devices: a whole 2x2x4 slice. The times are simulated.
32 devices in a mesh: member: 8 (over z, y), tile: 4 (over x, core).
Axes of the slice: x: 2, y: 2, z: 4, core: 2. Of those that a mesh axis runs over, the one named last changes fastest.
Arguments:
- realization_array: float32 [8, 4, 256, 512], P('member', None, 'tile'), may hold values from -6 to 6
- water_depth: float32 [256, 512], P('tile'), may hold values from 0.5 to 4
- wet_mask: int32 [256, 512], P('tile'), may hold values 0 or 1
- obs_cell: int32 [16384], P('tile'), may hold values from 0 to 32767, as said below
- obs_value: float32 [16384], P('tile'), may hold values from -8 to 8
- obs_error: float32 [16384], P('tile'), may hold values from 0.05 to 0.5
- celer_gain: float32 [16384], P('tile'), may hold values from 0.5 to 2
- obs_list: int32 [4, 128, 64], P('tile', 'member'), may hold values from 3584 to 8639, as said below
- obs_count: int32 [4, 128], P('tile', 'member'), may hold values from 32 to 64, as said below
Outputs:
- analysis: float32 [8, 4, 256, 512], P('member', None, 'tile')
Inputs may be any that keep to these rules, and one draw needn't show every extreme that they name: `obs_cell`: observation o of a tile lies in cells o * S to o * S + S - 1 of that tile, S = 8. `obs_list`: the entries of one patch's list are distinct and name only observations of existing tiles. `obs_count`: some patch has a full list.
All inputs are finite; a program needn't handle non-finite values. No bound on the sum of `wet_mask` on one device may be relied on, other than what follows from the above.
Results may differ from a plain program's by a relative error of at most 0.0003.
Values sent between devices are 32-bit elements; how exact they have to be, the bound alone decides.
No kernel may reach another device: no remote copies, remote signals or barrier semaphores. Data moves between devices by JAX's collectives and lax.ppermute only.
A program may use at most 128 MiB of HBM per device.

v0:
```python
import functools

import jax
import jax.numpy as jnp
from jax import lax
from jax.experimental import pallas as pl
from jax.experimental.pallas import tpu as pltpu
from jax.sharding import PartitionSpec as P

REGION_POINTS = 256
STEPS = 4
NS_ITERS = 14
CELLS_PER_OBS = 8
LANES = 128

FRICTION = 0.98
PRESSURE = 0.25
DIVERGE = 0.25
FORCING = 0.05
UPWIND = 0.4
DAMPING = 0.02
HIGH = lax.Precision.HIGHEST

PAD = 8


def iota(shape, dim):
    return lax.broadcasted_iota(jnp.int32, shape, dim)


def forecast_kernel(
    sizes,
    state_ref,
    depth_ref,
    mask_ref,
    cell_ref,
    gain_ref,
    low_ref,
    high_ref,
    out_ref,
    s_ref,
    u_ref,
    v_ref,
    e_ref,
    h_ref,
    w_ref,
    flux_ref,
    part_ref,
    cell_win,
    gain_win,
    level_ref,
):
    members, own_rows, halo, obs_halo = sizes
    rows, width = depth_ref.shape
    total = rows + 2 * halo
    first = PAD + halo
    fields = (s_ref, u_ref, v_ref, e_ref, h_ref, w_ref)
    for i, field in enumerate(fields):
        field[PAD : PAD + halo, :] = low_ref[i * halo : (i + 1) * halo, :]
        field[first + rows : first + rows + halo, :] = high_ref[i * halo : (i + 1) * halo, :]
        if i < 4:
            field[first : first + rows, :] = state_ref[i]
    h_ref[first : first + rows, :] = depth_ref[...]
    w_ref[first : first + rows, :] = mask_ref[...].astype(jnp.float32)
    edge = jnp.zeros((PAD, width), jnp.float32)
    for field in (s_ref, e_ref, flux_ref):
        field[0:PAD, :] = edge
        field[PAD + total : PAD + total + PAD, :] = edge

    column = iota((8, width), 1)
    not_first = column > 0
    not_last = column < width - 1

    def next_col(x):
        return jnp.where(not_last, pltpu.roll(x, width - 1, 1), 0.0)

    def prev_col(x):
        return jnp.where(not_first, pltpu.roll(x, 1, 1), 0.0)

    for step in range(STEPS):
        for block in range(total // 8):
            r = PAD + 8 * block
            here = pl.ds(r, 8)
            s, e, w, h = s_ref[here, :], e_ref[here, :], w_ref[here, :], h_ref[here, :]
            slope = s_ref[pl.ds(r + 1, 8), :] - s_ref[pl.ds(r - 1, 8), :]
            u = w * (FRICTION * u_ref[here, :] - PRESSURE * slope)
            u_ref[here, :] = u
            flux_ref[here, :] = h * u
            v = w * (FRICTION * v_ref[here, :] - PRESSURE * (next_col(s) - prev_col(s)))
            v_ref[here, :] = v
            flux = h * v
            part_ref[here, :] = s - DIVERGE * (next_col(flux) - prev_col(flux)) + FORCING * e
        for block in reversed(range(total // 8)):
            r = PAD + 8 * block
            here = pl.ds(r, 8)
            w = w_ref[here, :]
            rise = flux_ref[pl.ds(r + 1, 8), :] - flux_ref[pl.ds(r - 1, 8), :]
            s_ref[here, :] = w * (part_ref[here, :] - DIVERGE * rise)
            e = e_ref[here, :]
            e_ref[here, :] = w * (e - UPWIND * (e - e_ref[pl.ds(r - 1, 8), :]) - DAMPING * e)

    span = obs_halo // LANES
    inner = cell_ref.shape[0]
    window = inner + 2 * span
    base = 6 * halo
    for j, (win, own) in enumerate(((cell_win, cell_ref), (gain_win, gain_ref))):
        win[span : span + inner, :] = own[...].astype(jnp.float32)
        for i in range(span):
            lanes = slice(i * LANES, (i + 1) * LANES)
            win[i : i + 1, :] = low_ref[base + j : base + j + 1, lanes]
            win[span + inner + i : span + inner + i + 1, :] = high_ref[base + j : base + j + 1, lanes]
    cell = cell_win[0:window, :]
    half = width // CELLS_PER_OBS
    top = first - obs_halo // half
    equiv = jnp.zeros((window, LANES), jnp.float32)
    lane_cell = (iota((window, LANES), 1) % CELLS_PER_OBS).astype(jnp.float32)
    group = LANES // CELLS_PER_OBS
    for q in range(width // LANES):
        level_ref[...] = s_ref[top : top + 2 * window, q * LANES : (q + 1) * LANES]
        for parity in range(2):
            shift = parity * half + q * group
            spread = (iota((LANES, LANES), 0) == iota((LANES, LANES), 1) // CELLS_PER_OBS + shift).astype(jnp.float32)
            gather = (iota((LANES, LANES), 1) == iota((LANES, LANES), 0) // CELLS_PER_OBS + shift).astype(jnp.float32)
            offset = jnp.dot(cell, spread, preferred_element_type=jnp.float32, precision=HIGH)
            level = level_ref[pl.ds(parity, window, stride=2), :]
            chosen = jnp.where(jnp.abs(offset - lane_cell) < 0.5, level, 0.0)
            equiv = equiv + jnp.dot(chosen, gather, preferred_element_type=jnp.float32, precision=HIGH)
    equiv = equiv * gain_win[0:window, :]

    pieces = width // LANES
    for j in range(members):
        source = first + j * own_rows
        for i in range(4):
            for q in range(pieces):
                target = (i * pieces + q) * own_rows
                out_ref[j, target : target + own_rows, :] = fields[i][
                    source : source + own_rows, q * LANES : (q + 1) * LANES
                ]
        out_ref[j, 4 * pieces * own_rows : 4 * pieces * own_rows + window, :] = equiv


def group_matmul(left, right, starts, members):
    total = None
    for k in range(members):
        column = jnp.take_along_axis(left, starts + k, axis=1, mode="promise_in_bounds")
        term = column * right[k : k + 1, :]
        total = term if total is None else total + term
    return total


def analysis_kernel(
    sizes,
    recv_ref,
    spot_ref,
    damp_ref,
    live_ref,
    value_ref,
    error_ref,
    low_ref,
    high_ref,
    out_ref,
    value_win,
    error_win,
    table_ref,
):
    members, own_rows, halo, obs_halo, pieces = sizes
    stride = recv_ref.shape[0] // members
    body_rows = 4 * pieces * own_rows
    span = obs_halo // LANES
    inner = value_ref.shape[0]
    window = inner + 2 * span
    base = 6 * halo + 2
    for j, (win, own) in enumerate(((value_win, value_ref), (error_win, error_ref))):
        win[span : span + inner, :] = own[...]
        for i in range(span):
            lanes = slice(i * LANES, (i + 1) * LANES)
            win[i : i + 1, :] = low_ref[base + j : base + j + 1, lanes]
            win[span + inner + i : span + inner + i + 1, :] = high_ref[base + j : base + j + 1, lanes]

    spot = spot_ref[...]
    pairs = spot.shape[0]
    row, lane = spot // LANES, spot % LANES
    rows_of = [jnp.broadcast_to(row[i : i + 1, :], (members, LANES)) for i in range(pairs)]
    lanes_of = [jnp.broadcast_to(lane[i : i + 1, :], (members, LANES)) for i in range(pairs)]
    picked = [jnp.zeros((members, LANES), jnp.float32) for i in range(pairs)]
    value = jnp.zeros((pairs, LANES), jnp.float32)
    error = jnp.zeros((pairs, LANES), jnp.float32)
    for r in range(window):
        source = recv_ref[pl.ds(body_rows + r, members, stride=stride), :]
        for i in range(pairs):
            got = jnp.take_along_axis(source, lanes_of[i], axis=1, mode="promise_in_bounds")
            picked[i] = jnp.where(rows_of[i] == r, got, picked[i])
        hit = row == r
        for name, win in (("value", value_win), ("error", error_win)):
            line = jnp.broadcast_to(win[r : r + 1, :], (pairs, LANES))
            got = jnp.take_along_axis(line, lane, axis=1, mode="promise_in_bounds")
            if name == "value":
                value = jnp.where(hit, got, value)
            else:
                error = jnp.where(hit, got, error)
    precision = jnp.where(live_ref[...] > 0.0, 1.0 / (damp_ref[...] * error), 0.0)

    left_half = iota((members, LANES), 1) < LANES // 2
    weighted, spreads, innovations = [], [], []
    for i in range(pairs):
        mean = jnp.sum(picked[i], axis=0, keepdims=True) * (1.0 / members)
        spread = picked[i] - mean
        scaled = spread * precision[i : i + 1, :]
        innovation = jnp.broadcast_to(value[i : i + 1, :] - mean, (members, LANES))
        weighted += [jnp.where(left_half, scaled, 0.0), jnp.where(left_half, 0.0, scaled)]
        spreads += [spread, spread]
        innovations += [innovation, innovation]
    every = lax.dot_general(
        jnp.concatenate(weighted, axis=0),
        jnp.concatenate(spreads + innovations, axis=0),
        (((1,), (1,)), ((), ())),
        preferred_element_type=jnp.float32,
        precision=HIGH,
    )
    lane_at = iota((members, LANES), 1)
    patch_at = lane_at // members
    gram = jnp.zeros((members, LANES), jnp.float32)
    proj = jnp.zeros((members, LANES), jnp.float32)
    for p in range(2 * pairs):
        mine = patch_at == p
        block = every[p * members : (p + 1) * members, :]
        gram = jnp.where(mine, block[:, :LANES], gram)
        proj = jnp.where(mine, block[:, LANES:], proj)

    starts = lane_at - lane_at % members
    eye = (lane_at % members == iota((members, LANES), 0)).astype(jnp.float32)
    amat = gram + (members - 1.0) * eye
    trace = group_matmul(
        jnp.broadcast_to(jnp.sum(amat * eye, axis=0, keepdims=True), (members, LANES)),
        jnp.ones((members, LANES), jnp.float32),
        starts,
        members,
    )

    def iterate(sweep, carry):
        current, inverse = carry
        factor = 1.5 * eye - 0.5 * group_matmul(inverse, current, starts, members)
        return (
            group_matmul(current, factor, starts, members),
            group_matmul(factor, inverse, starts, members),
        )

    current, inverse = lax.fori_loop(0, NS_ITERS, iterate, (amat / trace, eye), unroll=members <= 8)
    root = inverse / jnp.sqrt(trace)
    wbar = group_matmul(root, group_matmul(root, proj, starts, members), starts, members)
    wtot = ((members - 1.0) ** 0.5) * root + wbar
    mix = wtot - jnp.sum(wtot, axis=0, keepdims=True) * (1.0 / members) + 1.0 / members
    table_ref[...] = mix.T

    def analyse(m, carry):
        for side in range(2):
            coefs = table_ref[pl.ds(side * members + m, own_rows, stride=2 * members), :]
            columns = [
                jnp.broadcast_to(coefs[:, k : k + 1], (own_rows, LANES)) for k in range(members)
            ]
            for i in range(4):
                for q in range(side * pieces // 2, (side + 1) * pieces // 2):
                    start = (i * pieces + q) * own_rows
                    total = None
                    for k in range(members):
                        term = columns[k] * recv_ref[pl.ds(k * stride + start, own_rows), :]
                        total = term if total is None else total + term
                    out_ref[m, i, :, q * LANES : (q + 1) * LANES] = total
        return carry

    if members <= 8:
        for m in range(members):
            analyse(m, 0)
    else:
        lax.fori_loop(0, members, analyse, 0)


def exchange(low, high):
    count = lax.axis_size("tile")
    forward = [(i, i + 1) for i in range(count - 1)]
    backward = [(target, source) for source, target in forward]
    return lax.ppermute(low, "tile", forward), lax.ppermute(high, "tile", backward)


def vmem_specs(count):
    return [pl.BlockSpec(memory_space=pltpu.VMEM)] * count


def body(
    realization_array,
    water_depth,
    wet_mask,
    obs_cell,
    obs_value,
    obs_error,
    celer_gain,
    obs_list,
    obs_count,
):
    members = lax.axis_size("member")
    rows, width = water_depth.shape
    obs_tile = obs_cell.shape[0]
    radius = obs_tile // 8
    halo = radius * CELLS_PER_OBS // width + 2 * STEPS
    per_dev, slots = obs_list.shape[1:]
    own_rows = per_dev * REGION_POINTS // width
    pieces = width // LANES
    state = realization_array[0]
    wet_float = wet_mask.astype(jnp.float32)
    offset = (obs_cell % CELLS_PER_OBS).astype(jnp.float32)

    def edge(rows_of, obs_of):
        grid = jnp.concatenate([state, water_depth[None], wet_float[None]], axis=0)[:, rows_of, :]
        obs = jnp.stack([x[obs_of] for x in (offset, celer_gain, obs_value, obs_error)])
        return jnp.concatenate(
            [grid.reshape(6 * halo, width), obs.reshape(4 * radius // width, width)], axis=0
        )

    low, high = exchange(
        edge(slice(rows - halo, rows), slice(obs_tile - radius, obs_tile)),
        edge(slice(0, halo), slice(0, radius)),
    )

    window = (obs_tile + 2 * radius) // LANES
    packet = 4 * pieces * own_rows + window
    grid = (rows + 2 * halo + 2 * PAD, width)
    panel = (obs_tile // LANES, LANES)
    sends = pl.pallas_call(
        functools.partial(forecast_kernel, (members, own_rows, halo, radius)),
        out_shape=jax.ShapeDtypeStruct((members, packet, LANES), jnp.float32),
        in_specs=vmem_specs(7),
        out_specs=pl.BlockSpec(memory_space=pltpu.VMEM),
        scratch_shapes=[pltpu.VMEM(grid, jnp.float32)] * 8
        + [pltpu.VMEM((window, LANES), jnp.float32)] * 2
        + [pltpu.VMEM((2 * window, LANES), jnp.float32)],
        compiler_params=pltpu.CompilerParams(vmem_limit_bytes=24 * 2**20),
        name="forecast",
    )(
        state,
        water_depth,
        wet_mask,
        offset.reshape(panel),
        celer_gain.reshape(panel),
        low,
        high,
    )
    received = lax.all_to_all(sends, "member", split_axis=0, concat_axis=0, tiled=True)

    pairs = per_dev * slots // LANES
    patch_index = lax.axis_index("member") * per_dev + jnp.arange(per_dev, dtype=jnp.int32)
    row_index = patch_index * REGION_POINTS // width
    centre = obs_tile + row_index * obs_tile // rows
    dist = (obs_list[0] - centre[:, None]).astype(jnp.float32) / radius
    damp = 1.0 + 4.0 * dist * dist
    live = jnp.arange(slots, dtype=jnp.int32)[None, :] < obs_count[0][:, None]
    spot = obs_list[0] - (obs_tile - radius)
    analysed = pl.pallas_call(
        functools.partial(analysis_kernel, (members, own_rows, halo, radius, pieces)),
        out_shape=jax.ShapeDtypeStruct((members, 4, own_rows, width), jnp.float32),
        in_specs=vmem_specs(8),
        out_specs=pl.BlockSpec(memory_space=pltpu.VMEM),
        scratch_shapes=[pltpu.VMEM((window, LANES), jnp.float32)] * 2
        + [pltpu.VMEM((LANES, members), jnp.float32)],
        compiler_params=pltpu.CompilerParams(vmem_limit_bytes=24 * 2**20),
        name="analysis",
    )(
        received.reshape(members * packet, LANES),
        spot.reshape(pairs, LANES),
        damp.reshape(pairs, LANES),
        live.astype(jnp.float32).reshape(pairs, LANES),
        obs_value.reshape(panel),
        obs_error.reshape(panel),
        low,
        high,
    )
    result = lax.all_to_all(analysed, "member", split_axis=0, concat_axis=0, tiled=True)
    return jnp.transpose(result, (1, 0, 2, 3)).reshape(1, 4, rows, width)


def solution(mesh):
    return jax.shard_map(
        body,
        mesh=mesh,
        in_specs=(
            P("member", None, "tile", None),
            P("tile", None),
            P("tile", None),
            P("tile"),
            P("tile"),
            P("tile"),
            P("tile"),
            P("tile", "member", None),
            P("tile", "member"),
        ),
        out_specs=P("member", None, "tile", None),
        check_vma=False,
    )
```

profile of v0, /device:TPU:1, one launch (start us, length us, event | category | flops | bytes accessed | tf_op | source)
XLA Modules:
  0.0 62.5 jit_solution(15878689541824503276)
XLA Ops:
  0.0 1.0 %convert_bitcast_fusion = f32[1,64,512]{2,1,0:T(8,128)S(1)} fusion(s32[64,512]{1,0:T(8,128)} %mask_ref.1), kind=kLoop, calls=%fused_computation.4 | loop fusion | flops 32768 | bytes 262144 | tf_op jit(solution)/shard_map/broadcast_in_dim | solution.py:313
  1.0 0.7 %copy-done.3 = f32[4096]{0:T(1024)S(1)} copy-done((f32[4096]{0:T(1024)S(1)}, f32[4096]{0:T(1024)}, u32[]{:S(2)}) %copy-start.3) | copy-done | bytes 16408
  1.7 0.0 copy-done.4
  1.8 1.0 %pad_maximum_fusion = (f32[6,16,512]{2,1,0:T(8,128)S(1)}, f32[6,16,512]{2,1,0:T(8,128)S(1)}) fusion(f32[1,64,512]{2,1,0:T(8,128)S(1)} %convert_bitcast_fusion, f32[1,64,512]{2,1,0:T(8,128)S(1)} %bitcast.28, f32[4,64,512]{2,1,0:T(8,128)} %bitcast.26), kind=kLoop, calls=%fused_computation.1 | loop fusion | flops 196608 | bytes 1179648 | tf_op jit(solution)/shard_map/concatenate | solution.py:313
  2.8 4.6 %collective-permute-start = (f32[100,512]{1,0:T(8,128)S(1)}, f32[100,512]{1,0:T(8,128)S(1)}, u32[]{:S(2)}, u32[]{:S(2)}) collective-permute-start(f32[100,512]{1,0:T(8,128)S(1)} %concatenate.11), channel_id=1, source_target_pairs={{0,1},{1,2},{2,3},{4,5},{5,6},{6,7},{8,9},{9,10},{10,11},{12,13},{... | collective-permute-start | bytes 614408 | tf_op jit(solution)/shard_map/ppermute | solution.py:282
  7.5 2.0 %collective-permute-start.1 = (f32[100,512]{1,0:T(8,128)S(1)}, f32[100,512]{1,0:T(8,128)S(1)}, u32[]{:S(2)}, u32[]{:S(2)}) collective-permute-start(f32[100,512]{1,0:T(8,128)S(1)} %concatenate.12), channel_id=1, source_target_pairs={{1,0},{2,1},{3,2},{5,4},{6,5},{7,6},{9,8},{10,9},{11,10},{13,12},{... | collective-permute-start | bytes 614408 | tf_op jit(solution)/shard_map/ppermute | solution.py:282
  9.6 0.7 %collective-permute-done.low_ref = f32[100,512]{1,0:T(8,128)S(1)} collective-permute-done((f32[100,512]{1,0:T(8,128)S(1)}, f32[100,512]{1,0:T(8,128)S(1)}, u32[]{:S(2)}, u32[]{:S(2)}) %collective-permute-start) | collective-permute-done | bytes 204832 | tf_op jit(solution)/shard_map/ppermute | solution.py:282
  10.2 4.6 %collective-permute-done.1.high_ref = f32[100,512]{1,0:T(8,128)S(1)} collective-permute-done((f32[100,512]{1,0:T(8,128)S(1)}, f32[100,512]{1,0:T(8,128)S(1)}, u32[]{:S(2)}, u32[]{:S(2)}) %collective-permute-start.1) | collective-permute-done | bytes 204832 | tf_op jit(solution)/shard_map/ppermute | solution.py:282
  14.8 3.5 %forecast.1 = f32[8,168,128]{2,1,0:T(8,128)} custom-call(f32[4,64,512]{2,1,0:T(8,128)S(1)} %bitcast.27, f32[64,512]{1,0:T(8,128)S(1)} %copy-done.1, s32[64,512]{1,0:T(8,128)S(1)} %copy-done.2, f32[32,128]{1,0:T(8,128)S(1)} %get-tuple-element.16.cell_ref, f32[32,128]{1,0:T(8,128)S(1)} %bitcast.29, f32[100,512]{1,0:T(8,128)S(1)} %collective-permute-done.low_ref, ...), custom_call_target="tpu_custom_call" | custom-call | tf_op jit(solution)/shard_map/forecast/pallas_call | solution.py:328
  18.3 5.7 %all-to-all-start = ((f32[8,168,128]{2,1,0:T(8,128)}), f32[8,168,128]{2,1,0:T(8,128)S(1)}, u32[]{:S(2)}, u32[]{:S(2)}) async-start(f32[8,168,128]{2,1,0:T(8,128)} %forecast.1), calls=%async_computation | async-start | bytes 1376256 | tf_op jit(solution)/shard_map/all_to_all | solution.py:347
  24.0 0.1 squeeze.8
  24.1 0.1 sub.25
  24.2 0.1 sub.26
  24.3 0.5 broadcast.126
  24.8 0.1 copy-done.8
  24.9 0.7 %reduce.3 = s32[16]{0:T(128)S(1)} reduce(s32[1,16]{1,0:T(1,128)S(1)} %copy-done.8, s32[]{:T(128)} %broadcast.126), dimensions={0}, to_apply=%param.17.reduce_sub_computation.3 | reduce | bytes 132 | tf_op args[8]
  25.6 0.1 lt.32
  25.7 0.1 lt.33
  25.8 0.1 lt.34
  25.8 0.1 lt.30
  25.9 13.3 %all-to-all-done = f32[8,168,128]{2,1,0:T(8,128)S(1)} async-done(((f32[8,168,128]{2,1,0:T(8,128)}), f32[8,168,128]{2,1,0:T(8,128)S(1)}, u32[]{:S(2)}, u32[]{:S(2)}) %all-to-all-start) | async-done | bytes 688160 | tf_op jit(solution)/shard_map/all_to_all | solution.py:347
  39.2 4.5 %analysis.1 = f32[8,4,8,512]{3,2,1,0:T(8,128)S(1)} custom-call(f32[1344,128]{1,0:T(8,128)S(1)} %bitcast.25, s32[8,128]{1,0:T(8,128)S(1)} %broadcast_add_fusion.spot_ref, f32[8,128]{1,0:T(8,128)S(1)} %multiply_add_fusion.damp_ref, f32[8,128]{1,0:T(8,128)S(1)} %compare_convert_fusion.live_ref, f32[32,128]{1,0:T(8,128)S(1)} %bitcast.30, ...), custom_call_target="tpu_custom_call" | custom-call | tf_op jit(solution)/shard_map/analysis/pallas_call | solution.py:357
  43.7 17.9 %all_to_all.10 = f32[8,4,8,512]{3,2,1,0:T(8,128)S(1)} all-to-all(f32[8,4,8,512]{3,2,1,0:T(8,128)S(1)} %analysis.1), channel_id=1, replica_groups=mesh['member'=8,'tile'=4] {'member'}, dimensions={0} | all-to-all | bytes 1048576 | tf_op jit(solution)/shard_map/all_to_all | solution.py:376
  61.6 0.8 %copy_bitcast_fusion = f32[1,4,64,512]{3,2,1,0:T(8,128)} fusion(f32[8,4,8,512]{3,2,1,0:T(8,128)S(1)} %all_to_all.10), kind=kLoop, calls=%fused_computation | loop fusion | bytes 1048576 | tf_op jit(solution)/shard_map/reshape | solution.py:377
  (27 shorter events, 0.2 us)
Async XLA Ops:
  0.0 1.0 %copy-start.6 = (s32[4096]{0:T(1024)S(1)}, s32[4096]{0:T(1024)}, u32[]{:S(2)}) copy-start(s32[4096]{0:T(1024)} %param.12) | copy-start | bytes 49156
  0.0 1.7 %copy-start.1 = (f32[64,512]{1,0:T(8,128)S(1)}, f32[64,512]{1,0:T(8,128)}, u32[]{:S(2)}) copy-start(f32[64,512]{1,0:T(8,128)} %depth_ref.1) | copy-start | bytes 393220
  1.0 0.7 %copy-start.3 = (f32[4096]{0:T(1024)S(1)}, f32[4096]{0:T(1024)}, u32[]{:S(2)}) copy-start(f32[4096]{0:T(1024)} %param.15) | copy-start | bytes 49156
  1.0 0.8 %copy-start.5 = (f32[4096]{0:T(1024)S(1)}, f32[4096]{0:T(1024)}, u32[]{:S(2)}) copy-start(f32[4096]{0:T(1024)} %param.14) | copy-start | bytes 49156
  1.0 0.7 %copy-start.4 = (f32[4096]{0:T(1024)S(1)}, f32[4096]{0:T(1024)}, u32[]{:S(2)}) copy-start(f32[4096]{0:T(1024)} %param.13) | copy-start | bytes 49156
  2.8 12.1 %copy-start = (f32[1,4,64,512]{3,2,1,0:T(8,128)S(1)}, f32[1,4,64,512]{3,2,1,0:T(8,128)}, u32[]{:S(2)}) copy-start(f32[1,4,64,512]{3,2,1,0:T(8,128)} %param.9) | copy-start | bytes 1572868
  2.8 7.4 %collective-permute-start = (f32[100,512]{1,0:T(8,128)S(1)}, f32[100,512]{1,0:T(8,128)S(1)}, u32[]{:S(2)}, u32[]{:S(2)}) collective-permute-start(f32[100,512]{1,0:T(8,128)S(1)} %concatenate.11), channel_id=1, source_target_pairs={{0,1},{1,2},{2,3},{4,5},{5,6},{6,7},{8,9},{9,10},{10,11},{12,13},{... | collective-permute-start | bytes 614408 | tf_op jit(solution)/shard_map/ppermute | solution.py:282
  7.5 7.4 %copy-start.2 = (s32[64,512]{1,0:T(8,128)S(1)}, s32[64,512]{1,0:T(8,128)}, u32[]{:S(2)}) copy-start(s32[64,512]{1,0:T(8,128)} %mask_ref.1) | copy-start | bytes 393220
  7.5 7.3 %collective-permute-start.1 = (f32[100,512]{1,0:T(8,128)S(1)}, f32[100,512]{1,0:T(8,128)S(1)}, u32[]{:S(2)}, u32[]{:S(2)}) collective-permute-start(f32[100,512]{1,0:T(8,128)S(1)} %concatenate.12), channel_id=1, source_target_pairs={{1,0},{2,1},{3,2},{5,4},{6,5},{7,6},{9,8},{10,9},{11,10},{13,12},{... | collective-permute-start | bytes 614408 | tf_op jit(solution)/shard_map/ppermute | solution.py:282
  18.3 5.7 %copy-start.7 = (s32[1,16,64]{2,1,0:T(8,128)S(1)}, s32[1,16,64]{2,1,0:T(8,128)}, u32[]{:S(2)}) copy-start(s32[1,16,64]{2,1,0:T(8,128)} %param.16) | copy-start | bytes 12292
  18.3 20.9 %all-to-all-start = ((f32[8,168,128]{2,1,0:T(8,128)}), f32[8,168,128]{2,1,0:T(8,128)S(1)}, u32[]{:S(2)}, u32[]{:S(2)}) async-start(f32[8,168,128]{2,1,0:T(8,128)} %forecast.1), calls=%async_computation | async-start | bytes 1376256 | tf_op jit(solution)/shard_map/all_to_all | solution.py:347
  24.3 0.7 %copy-start.8 = (s32[1,16]{1,0:T(1,128)S(1)}, s32[1,16]{1,0:T(1,128)}, u32[]{:S(2)}) copy-start(s32[1,16]{1,0:T(1,128)} %param.17) | copy-start | bytes 196
where the time goes:
time: 63.6 us; the launch traced here: 62.5 us
  waiting for transfers between devices  18.5 us (29%)
  blocking collectives  17.9 us (28%)
  starting transfers between devices  12.4 us (19%)
  Pallas kernels  8 us (13%)
  local copies, waits for them, and re-layouts  2.87 us (5%)
  other arithmetic  2.67 us (4%)
    all_to_all x1, blocking collectives, body(): lax.all_to_all(analysed, 'member', split_axis=0, concat_axis=0, tiled=True)  17.9 us
    all_to_all x1, waiting for transfers between devices, body(): lax.all_to_all(sends, 'member', split_axis=0, concat_axis=0, tiled=True)  13.3 us
    all_to_all x1, starting transfers between devices, body(): lax.all_to_all(sends, 'member', split_axis=0, concat_axis=0, tiled=True)  5.69 us
    ppermute x1, starting transfers between devices, exchange(): lax.ppermute(low, 'tile', forward)  4.64 us
    ppermute x1, waiting for transfers between devices, exchange(): lax.ppermute(high, 'tile', backward)  4.58 us
    pallas_call x1, Pallas kernels, body(): pl.pallas_call(functools.partial(analysis_kernel, (members, own_rows, hal...  4.49 us
    pallas_call x1, Pallas kernels, body(): pl.pallas_call(functools.partial(forecast_kernel, (members, own_rows, hal...  3.5 us
    ppermute x1, starting transfers between devices, exchange(): lax.ppermute(high, 'tile', backward)  2.05 us
  transfers between devices with their start and end apart: 3, of which 3 were waited for; matrix products, arithmetic and copies ran while one was open for 3% of the time, Pallas kernels for 0%

commit v1 on v0

v1 whole, which is shorter than its diff:
```python
import functools

import jax
import jax.numpy as jnp
from jax import lax
from jax.experimental import pallas as pl
from jax.experimental.pallas import tpu as pltpu
from jax.sharding import PartitionSpec as P

REGION_POINTS = 256
STEPS = 4
NS_ITERS = 14
CELLS_PER_OBS = 8
LANES = 128

FRICTION = 0.98
PRESSURE = 0.25
DIVERGE = 0.25
FORCING = 0.05
UPWIND = 0.4
DAMPING = 0.02
HIGH = lax.Precision.HIGHEST

PAD = 8


def iota(shape, dim):
    return lax.broadcasted_iota(jnp.int32, shape, dim)


def edge_kernel(halo, *refs):
    grids, obs, outs = refs[:3], refs[3:7], refs[7:9]
    wet_ref, cell_ref, sems = refs[9:]
    rows = grids[1].shape[0]
    inner = obs[0].shape[0]
    even = lax.axis_index("tile") % 2 == 0
    copies = []

    def fetch(source, target):
        copies.append(pltpu.make_async_copy(source, target, sems.at[len(copies)]))
        copies[-1].start()

    for side, out in enumerate(outs):
        is_last = even if side == 0 else jnp.logical_not(even)
        start = pl.multiple_of(jnp.where(is_last, rows - halo, 0), 8)
        for i in range(6):
            source = (grids[0].at[i] if i < 4 else grids[i - 3]).at[pl.ds(start, halo), :]
            fetch(source, out.at[pl.ds(i * halo, halo), :] if i < 5 else wet_ref.at[side])
        start = pl.multiple_of(jnp.where(is_last, inner - 8, 0), 8)
        for j in range(4):
            target = out.at[pl.ds(6 * halo, 8), pl.ds(j * LANES, LANES)] if j else cell_ref.at[side]
            fetch(obs[j].at[pl.ds(start, 8), :], target)
    for copy in copies:
        copy.wait()
    for side, out in enumerate(outs):
        out[5 * halo : 6 * halo, :] = wet_ref[side].astype(jnp.float32)
        out[6 * halo : 6 * halo + 8, 0:LANES] = (cell_ref[side] % CELLS_PER_OBS).astype(jnp.float32)


def side_by_side(x, pairs):
    return jnp.concatenate([x[:pairs], x[pairs:]], axis=1)


def window_parts(win, own, near_ref, far_ref, base, j, even):
    inner = own.shape[0]
    span = (win.shape[0] - inner) // 2
    lanes = slice(j * LANES, (j + 1) * LANES)
    near, far = near_ref[base : base + 8, lanes], far_ref[base : base + 8, lanes]
    win[0:span, :] = jnp.where(even, far, near)[8 - span :, :]
    win[span : span + inner, :] = own
    win[span + inner :, :] = jnp.where(even, near, far)[:span, :]


def forecast_kernel(
    sizes,
    state_ref,
    depth_ref,
    mask_ref,
    cell_ref,
    gain_ref,
    near_ref,
    far_ref,
    out_ref,
    equiv_ref,
    s_ref,
    u_ref,
    v_ref,
    e_ref,
    h_ref,
    w_ref,
    flux_ref,
    part_ref,
    cell_win,
    gain_win,
):
    members, own_rows, halo, obs_halo = sizes
    even = lax.axis_index("tile") % 2 == 0
    rows, width = depth_ref.shape
    pieces = width // LANES
    total = rows + 2 * halo
    first = PAD + halo
    own = pl.ds(first, rows)
    fields = (s_ref, u_ref, v_ref, e_ref, h_ref, w_ref)
    near_at = pl.multiple_of(jnp.where(even, first + rows, PAD), 8)
    far_at = pl.multiple_of(jnp.where(even, PAD, first + rows), 8)
    edge = jnp.zeros((PAD, LANES), jnp.float32)
    for q in range(pieces):
        lanes = slice(q * LANES, (q + 1) * LANES)
        for i, field in enumerate(fields):
            field[q, pl.ds(near_at, halo), :] = near_ref[i * halo : (i + 1) * halo, lanes]
            field[q, pl.ds(far_at, halo), :] = far_ref[i * halo : (i + 1) * halo, lanes]
            if i < 4:
                field[q, own, :] = state_ref[i, :, lanes]
        h_ref[q, own, :] = depth_ref[:, lanes]
        w_ref[q, own, :] = mask_ref[:, lanes].astype(jnp.float32)
        for field in (s_ref, e_ref, flux_ref):
            field[q, 0:PAD, :] = edge
            field[q, PAD + total : PAD + total + PAD, :] = edge

    lane = iota((8, LANES), 1)
    at_first, at_last = lane == 0, lane == LANES - 1

    def across(x):
        ahead = [pltpu.roll(piece, LANES - 1, 1) for piece in x] + [0.0]
        behind = [0.0] + [pltpu.roll(piece, 1, 1) for piece in x]
        return [
            jnp.where(at_last, ahead[q + 1], ahead[q]) - jnp.where(at_first, behind[q], behind[q + 1])
            for q in range(pieces)
        ]

    for step in range(STEPS):
        for block in range(total // 8):
            r = PAD + 8 * block
            here, below, above = pl.ds(r, 8), pl.ds(r + 1, 8), pl.ds(r - 1, 8)
            s = [s_ref[q, here, :] for q in range(pieces)]
            slope = across(s)
            flux = []
            for q in range(pieces):
                w, h = w_ref[q, here, :], h_ref[q, here, :]
                u = w * (FRICTION * u_ref[q, here, :] - PRESSURE * (s_ref[q, below, :] - s_ref[q, above, :]))
                u_ref[q, here, :] = u
                flux_ref[q, here, :] = h * u
                v = w * (FRICTION * v_ref[q, here, :] - PRESSURE * slope[q])
                v_ref[q, here, :] = v
                flux.append(h * v)
            rise = across(flux)
            for q in range(pieces):
                part_ref[q, here, :] = s[q] - DIVERGE * rise[q] + FORCING * e_ref[q, here, :]
        for block in reversed(range(total // 8)):
            r = PAD + 8 * block
            here, below, above = pl.ds(r, 8), pl.ds(r + 1, 8), pl.ds(r - 1, 8)
            for q in range(pieces):
                w = w_ref[q, here, :]
                rise = flux_ref[q, below, :] - flux_ref[q, above, :]
                s_ref[q, here, :] = w * (part_ref[q, here, :] - DIVERGE * rise)
                e = e_ref[q, here, :]
                e_ref[q, here, :] = w * (e - UPWIND * (e - e_ref[q, above, :]) - DAMPING * e)

    window = cell_win.shape[0]
    base = 6 * halo
    offsets = (cell_ref[...] % CELLS_PER_OBS).astype(jnp.float32)
    window_parts(cell_win, offsets, near_ref, far_ref, base, 0, even)
    window_parts(gain_win, gain_ref[...], near_ref, far_ref, base, 1, even)
    half = width // CELLS_PER_OBS
    top = first - obs_halo // half
    column = iota((LANES, 2 * width), 1)
    cell_at = column // (2 * LANES) * LANES + column % LANES
    parity = column // LANES % 2
    spread = jnp.where(
        iota((LANES, 2 * width), 0) == parity * half + cell_at // CELLS_PER_OBS, 1.0, 0.0
    ).astype(jnp.bfloat16)
    offset = jnp.dot(cell_win[...].astype(jnp.bfloat16), spread, preferred_element_type=jnp.float32)
    level = jnp.concatenate(
        [s_ref[q, pl.ds(top + side, window, stride=2), :] for q in range(pieces) for side in range(2)], axis=1
    )
    place = (iota((window, 2 * width), 1) % CELLS_PER_OBS).astype(jnp.float32)
    rest = jnp.where(jnp.abs(offset - place) < 0.5, level, 0.0)
    equiv = jnp.zeros((window, LANES), jnp.float32)
    parts = []
    for i in range(3):
        parts.append(rest.astype(jnp.bfloat16))
        rest = rest - parts[-1].astype(jnp.float32)
    for part in reversed(parts):
        equiv = equiv + lax.dot_general(
            part, spread, (((1,), (1,)), ((), ())), preferred_element_type=jnp.float32
        )
    equiv_ref[...] = equiv * gain_win[...]

    for j in range(members):
        source = first + j * own_rows
        for i in range(4):
            for q in range(pieces):
                target = (i * pieces + q) * own_rows
                out_ref[j, target : target + own_rows, :] = fields[i][q, source : source + own_rows, :]


def group_columns(left, starts, members):
    return [jnp.take_along_axis(left, starts + k, axis=1, mode="promise_in_bounds") for k in range(members)]


def group_matmul(columns, right):
    terms = [column * right[k : k + 1, :] for k, column in enumerate(columns)]
    while len(terms) > 1:
        terms = [a + b for a, b in zip(terms[::2], terms[1::2])]
    return terms[0]


def relative(index, members):
    bits = members.bit_length() - 1
    return sum(((index >> i) & 1) << (bits - 1 - i) for i in range(bits))


def weight_kernel(
    sizes,
    equiv_ref,
    spot_ref,
    damp_ref,
    live_ref,
    value_ref,
    error_ref,
    near_ref,
    far_ref,
    mix_ref,
    value_win,
    error_win,
):
    members, halo = sizes
    window = value_win.shape[0]
    even = lax.axis_index("tile") % 2 == 0
    window_parts(value_win, value_ref[...], near_ref, far_ref, 6 * halo, 2, even)
    window_parts(error_win, error_ref[...], near_ref, far_ref, 6 * halo, 3, even)

    spot = spot_ref[...]
    pairs = spot.shape[0]
    row, lane = spot // LANES, spot % LANES
    rows_of = [jnp.broadcast_to(row[i : i + 1, :], (members, LANES)) for i in range(pairs)]
    lanes_of = [jnp.broadcast_to(lane[i : i + 1, :], (members, LANES)) for i in range(pairs)]
    picked = [jnp.zeros((members, LANES), jnp.float32) for i in range(pairs)]
    value = jnp.zeros((pairs, LANES), jnp.float32)
    error = jnp.zeros((pairs, LANES), jnp.float32)
    for r in range(window):
        source = equiv_ref[pl.ds(r, members, stride=window), :]
        for i in range(pairs):
            got = jnp.take_along_axis(source, lanes_of[i], axis=1, mode="promise_in_bounds")
            picked[i] = jnp.where(rows_of[i] == r, got, picked[i])
        hit = row == r
        line = jnp.broadcast_to(value_win[r : r + 1, :], spot.shape)
        value = jnp.where(hit, jnp.take_along_axis(line, lane, axis=1, mode="promise_in_bounds"), value)
        line = jnp.broadcast_to(error_win[r : r + 1, :], spot.shape)
        error = jnp.where(hit, jnp.take_along_axis(line, lane, axis=1, mode="promise_in_bounds"), error)
    precision = jnp.where(live_ref[...] > 0.0, 1.0 / (damp_ref[...] * error), 0.0)

    left_half = iota((members, LANES), 1) < LANES // 2
    weighted, spreads, innovations = [], [], []
    for i in range(pairs):
        mean = jnp.sum(picked[i], axis=0, keepdims=True) * (1.0 / members)
        spread = picked[i] - mean
        scaled = spread * precision[i : i + 1, :]
        innovation = jnp.broadcast_to(value[i : i + 1, :] - mean, (members, LANES))
        weighted.append(scaled)
        spreads.append(spread)
        innovations.append(innovation)
    every = lax.dot_general(
        jnp.concatenate(
            [jnp.where(left_half, x, 0.0) for x in weighted] + [jnp.where(left_half, 0.0, x) for x in weighted],
            axis=0,
        ),
        jnp.concatenate(spreads + spreads + innovations + innovations, axis=0),
        (((1,), (1,)), ((), ())),
        preferred_element_type=jnp.float32,
        precision=HIGH,
    )
    lane_at = iota((members, LANES), 1)
    patch_at = lane_at // members
    gram = jnp.zeros((members, LANES), jnp.float32)
    proj = jnp.zeros((members, LANES), jnp.float32)
    for p in range(2 * pairs):
        mine = patch_at == p
        block = every[p * members : (p + 1) * members, :]
        gram = jnp.where(mine, block[:, :LANES], gram)
        proj = jnp.where(mine, block[:, LANES:], proj)

    starts = lane_at - lane_at % members
    eye = (lane_at % members == iota((members, LANES), 0)).astype(jnp.float32)
    amat = gram + (members - 1.0) * eye
    diagonal = jnp.broadcast_to(jnp.sum(amat * eye, axis=0, keepdims=True), (members, LANES))
    trace = functools.reduce(jnp.add, group_columns(diagonal, starts, members))

    def iterate(sweep, carry):
        product, inverse = carry
        columns = group_columns(product, starts, members)
        square = group_matmul(columns, product)
        cube = group_matmul(columns, square)
        return (
            2.25 * product - 1.5 * square + 0.25 * cube,
            1.5 * inverse - 0.5 * group_matmul(columns, inverse),
        )

    product, inverse = lax.fori_loop(0, NS_ITERS, iterate, (amat / trace, eye), unroll=members <= 8)
    root = inverse / jnp.sqrt(trace)
    columns = group_columns(root, starts, members)
    wbar = group_matmul(columns, group_matmul(columns, proj))
    wtot = ((members - 1.0) ** 0.5) * root + wbar
    mix = wtot - jnp.sum(wtot, axis=0, keepdims=True) * (1.0 / members) + 1.0 / members
    mix_ref[...] = mix


def mix_kernel(sizes, recv_ref, mix_ref, out_ref, table_ref):
    members, own_rows, pieces = sizes
    stride = recv_ref.shape[0] // members
    me = lax.axis_index("member")
    table_ref[...] = mix_ref[...].T
    bases = [pl.multiple_of((me ^ relative(k, members)) * stride, 8) for k in range(members)]

    def analyse(m, carry):
        target = me ^ relative(m, members)
        for side in range(2):
            coefs = table_ref[pl.ds(side * members + m, own_rows, stride=2 * members), :]
            columns = [
                jnp.broadcast_to(coefs[:, k : k + 1], (own_rows, LANES)) for k in range(members)
            ]
            for i in range(4):
                for q in range(side * pieces // 2, (side + 1) * pieces // 2):
                    start = (i * pieces + q) * own_rows
                    total = None
                    for k in range(members):
                        term = columns[k] * recv_ref[pl.ds(bases[k] + start, own_rows), :]
                        total = term if total is None else total + term
                    out_ref[target, i, :, q * LANES : (q + 1) * LANES] = total
        return carry

    if members <= 8:
        for m in range(members):
            analyse(m, 0)
    else:
        lax.fori_loop(0, members, analyse, 0)


def gather_members(block):
    members = lax.axis_size("member")
    held = block[None]
    distance = members // 2
    while distance:
        pairs = [(i, i ^ distance) for i in range(members)]
        held = jnp.concatenate([held, lax.ppermute(held, "member", pairs)], axis=0)
        distance //= 2
    return held


def swaps(near, far):
    count = lax.axis_size("tile")

    def pairs(start):
        twos = [(i, i + 1) for i in range(start, count - 1, 2)]
        return twos + [(b, a) for a, b in twos]

    far = lax.ppermute(far, "tile", pairs(1))
    near = lax.ppermute(near, "tile", pairs(0))
    return near, far


def vmem_specs(count):
    return [pl.BlockSpec(memory_space=pltpu.VMEM)] * count


def body(
    realization_array,
    water_depth,
    wet_mask,
    obs_cell,
    obs_value,
    obs_error,
    celer_gain,
    obs_list,
    obs_count,
):
    members = lax.axis_size("member")
    rows, width = water_depth.shape
    obs_tile = obs_cell.shape[0]
    radius = obs_tile // 8
    halo = radius * CELLS_PER_OBS // width + 2 * STEPS
    per_dev, slots = obs_list.shape[1:]
    own_rows = per_dev * REGION_POINTS // width
    pieces = width // LANES
    state = realization_array[0]
    panel = (obs_tile // LANES, LANES)
    pairs = per_dev * slots // LANES
    edges = pl.pallas_call(
        functools.partial(edge_kernel, halo),
        out_shape=[jax.ShapeDtypeStruct((6 * halo + 8, width), jnp.float32)] * 2,
        in_specs=[pl.BlockSpec(memory_space=pl.ANY)] * 7,
        out_specs=vmem_specs(2),
        scratch_shapes=[
            pltpu.VMEM((2, halo, width), jnp.int32),
            pltpu.VMEM((2, 8, LANES), jnp.int32),
            pltpu.SemaphoreType.DMA((20,)),
        ],
        name="edges",
    )(
        state,
        water_depth,
        wet_mask,
        obs_cell.reshape(panel),
        celer_gain.reshape(panel),
        obs_value.reshape(panel),
        obs_error.reshape(panel),
    )
    near, far = swaps(*edges)

    window = (obs_tile + 2 * radius) // LANES
    packet = 4 * pieces * own_rows
    grid = (pieces, rows + 2 * halo + 2 * PAD, LANES)
    sends, equiv = pl.pallas_call(
        functools.partial(forecast_kernel, (members, own_rows, halo, radius)),
        out_shape=[
            jax.ShapeDtypeStruct((members, packet, LANES), jnp.float32),
            jax.ShapeDtypeStruct((window, LANES), jnp.float32),
        ],
        in_specs=vmem_specs(7),
        out_specs=vmem_specs(2),
        scratch_shapes=[pltpu.VMEM(grid, jnp.float32)] * 8 + [pltpu.VMEM((window, LANES), jnp.float32)] * 2,
        compiler_params=pltpu.CompilerParams(vmem_limit_bytes=24 * 2**20),
        name="forecast",
    )(
        state,
        water_depth,
        wet_mask,
        obs_cell.reshape(panel),
        celer_gain.reshape(panel),
        near,
        far,
    )
    received = lax.all_to_all(sends, "member", split_axis=0, concat_axis=0, tiled=True)
    equivs = gather_members(equiv)

    patch_index = lax.axis_index("member") * per_dev + jnp.arange(per_dev, dtype=jnp.int32)
    row_index = patch_index * REGION_POINTS // width
    centre = obs_tile + row_index * obs_tile // rows
    dist = (obs_list[0] - centre[:, None]).astype(jnp.float32) / radius
    damp = 1.0 + 4.0 * dist * dist
    live = jnp.arange(slots, dtype=jnp.int32)[None, :] < obs_count[0][:, None]
    spot = side_by_side(obs_list[0] - (obs_tile - radius), pairs)
    mix = pl.pallas_call(
        functools.partial(weight_kernel, (members, halo)),
        out_shape=jax.ShapeDtypeStruct((members, LANES), jnp.float32),
        in_specs=vmem_specs(8),
        out_specs=vmem_specs(1)[0],
        scratch_shapes=[pltpu.VMEM((window, LANES), jnp.float32)] * 2,
        compiler_params=pltpu.CompilerParams(vmem_limit_bytes=24 * 2**20),
        name="weights",
    )(
        equivs.reshape(members * window, LANES),
        spot,
        side_by_side(damp, pairs),
        side_by_side(live.astype(jnp.float32), pairs),
        obs_value.reshape(panel),
        obs_error.reshape(panel),
        near,
        far,
    )
    analysed = pl.pallas_call(
        functools.partial(mix_kernel, (members, own_rows, pieces)),
        out_shape=jax.ShapeDtypeStruct((members, 4, own_rows, width), jnp.float32),
        in_specs=vmem_specs(2),
        out_specs=vmem_specs(1)[0],
        scratch_shapes=[pltpu.VMEM((LANES, members), jnp.float32)],
        compiler_params=pltpu.CompilerParams(vmem_limit_bytes=24 * 2**20),
        name="mix",
    )(received.reshape(members * packet, LANES), mix)
    result = lax.all_to_all(analysed, "member", split_axis=0, concat_axis=0, tiled=True)
    return jnp.transpose(result, (1, 0, 2, 3)).reshape(1, 4, rows, width)


def solution(mesh):
    return jax.shard_map(
        body,
        mesh=mesh,
        in_specs=(
            P("member", None, "tile", None),
            P("tile", None),
            P("tile", None),
            P("tile"),
            P("tile"),
            P("tile"),
            P("tile"),
            P("tile", "member", None),
            P("tile", "member"),
        ),
        out_specs=P("member", None, "tile", None),
        check_vma=False,
    )
```

time: 63.6 us -> 61 us (0.959)
  the two profiles are of different devices: /device:TPU:1 before, /device:TPU:0 now
where the time goes in v1:
time: 61 us; the launch traced here: 60.6 us
  blocking collectives  20.5 us (34%)
  waiting for transfers between devices  16.8 us (28%)
  starting transfers between devices  12.5 us (20%)
  Pallas kernels  8.07 us (13%)
  local copies, waits for them, and re-layouts  2.25 us (4%)
    all_to_all x1, blocking collectives, body(): lax.all_to_all(analysed, 'member', split_axis=0, concat_axis=0, tiled=True)  20.5 us
    ppermute x3, waiting for transfers between devices, gather_members(): held = jnp.concatenate([held, lax.ppermute(held, 'member', pairs)], axis=0)  16.8 us
    all_to_all x1, starting transfers between devices, body(): lax.all_to_all(sends, 'member', split_axis=0, concat_axis=0, tiled=True)  6.93 us
    ppermute x3, starting transfers between devices, gather_members(): held = jnp.concatenate([held, lax.ppermute(held, 'member', pairs)], axis=0)  4.39 us
    pallas_call x1, Pallas kernels, body(): pl.pallas_call(functools.partial(weight_kernel, (members, halo)), out_sha...  2.96 us
    pallas_call x1, Pallas kernels, body(): pl.pallas_call(functools.partial(forecast_kernel, (members, own_rows, hal...  2.69 us
    pallas_call x1, Pallas kernels, body(): pl.pallas_call(functools.partial(edge_kernel, halo), out_shape=[jax.Shape...  1.96 us
    unnamed x18, local copies, waits for them, and re-layouts  1.41 us
  transfers between devices with their start and end apart: 6, of which 3 were waited for; matrix products, arithmetic and copies ran while one was open for 1% of the time, Pallas kernels for 5%

profile of v1, /device:TPU:0, one launch (start us, length us, event | category | flops | bytes accessed | tf_op | source)
XLA Modules:
  0.0 60.6 jit_solution(12986389151286412179)
XLA Ops:
  0.0 2.0 %edges.1 = (f32[104,512]{1,0:T(8,128)}, f32[104,512]{1,0:T(8,128)}) custom-call(f32[4,64,512]{2,1,0:T(8,128)} %bitcast.21, f32[64,512]{1,0:T(8,128)} %depth_ref.1, s32[64,512]{1,0:T(8,128)} %mask_ref.1, s32[32,128]{1,0:T(8,128)} %bitcast.29, f32[32,128]{1,0:T(8,128)} %bitcast.31, f32[32,128]{1,0:T(8,128)} %bitcast.33, f32[32,128]{1,0:T(8,128)} %bitcast.35), custom_call_target="tpu_custom_call" | custom-call | tf_op jit(solution)/shard_map/edges/pallas_call | solution.py:388
  2.0 0.0 copy-start.7
  2.0 0.5 collective-permute-start
  2.5 0.7 %collective-permute-start.1 = (f32[104,512]{1,0:T(8,128)}, f32[104,512]{1,0:T(8,128)S(1)}, u32[]{:S(2)}, u32[]{:S(2)}) collective-permute-start(f32[104,512]{1,0:T(8,128)} %get-tuple-element.10), channel_id=1, source_target_pairs={{1,2},{2,1},{5,6},{6,5},{9,10},{10,9},{13,14},{14,13},{17,18},{18,... | collective-permute-start | bytes 638984 | tf_op jit(solution)/shard_map/ppermute | solution.py:357
  3.2 0.0 copy-start.4
  3.3 0.1 multiply_add_fusion
  3.3 0.7 %copy-done.8 = s32[1,16]{1,0:T(1,128)S(1)} copy-done((s32[1,16]{1,0:T(1,128)S(1)}, s32[1,16]{1,0:T(1,128)}, u32[]{:S(2)}) %copy-start.8) | copy-done | bytes 88
  4.0 0.1 fusion.1
  4.1 2.7 %forecast.1 = (f32[8,128,128]{2,1,0:T(8,128)}, f32[40,128]{1,0:T(8,128)S(1)}) custom-call(f32[4,64,512]{2,1,0:T(8,128)S(1)} %bitcast.22, f32[64,512]{1,0:T(8,128)S(1)} %copy-done.1, s32[64,512]{1,0:T(8,128)S(1)} %copy-done.2, s32[32,128]{1,0:T(8,128)S(1)} %bitcast.30, f32[32,128]{1,0:T(8,128)S(1)} %bitcast.32, f32[104,512]{1,0:T(8,128)S(1)} %collective-permute-done.near_ref, ...), custom_call_target="tpu_custom_call" | custom-call | tf_op jit(solution)/shard_map/forecast/pallas_call | solution.py:413
  6.8 6.9 %all-to-all-start = ((f32[8,128,128]{2,1,0:T(8,128)}), f32[8,128,128]{2,1,0:T(8,128)S(1)}, u32[]{:S(2)}, u32[]{:S(2)}) async-start(f32[8,128,128]{2,1,0:T(8,128)} %get-tuple-element.11), calls=%async_computation | async-start | bytes 1048576 | tf_op jit(solution)/shard_map/all_to_all | solution.py:433
  13.8 2.9 %collective-permute-start.2 = (f32[1,40,128]{2,1,0:T(8,128)S(1)}, f32[1,40,128]{2,1,0:T(8,128)S(1)}, u32[]{:S(2)}, u32[]{:S(2)}) collective-permute-start(f32[1,40,128]{2,1,0:T(8,128)S(1)} %bitcast.25), channel_id=1, source_target_pairs={{0,16},{4,20},{8,24},{12,28},{16,0},{20,4},{24,8},{28,12},{1,17},{... | collective-permute-start | bytes 61448 | tf_op jit(solution)/shard_map/ppermute | solution.py:345
  16.7 8.4 %collective-permute-done.2 = f32[1,40,128]{2,1,0:T(8,128)S(1)} collective-permute-done((f32[1,40,128]{2,1,0:T(8,128)S(1)}, f32[1,40,128]{2,1,0:T(8,128)S(1)}, u32[]{:S(2)}, u32[]{:S(2)}) %collective-permute-start.2) | collective-permute-done | bytes 20512 | tf_op jit(solution)/shard_map/ppermute | solution.py:345
  25.1 0.1 pad_maximum_fusion.3
  25.1 5.5 %collective-permute-done.3 = f32[2,40,128]{2,1,0:T(8,128)S(1)} collective-permute-done((f32[2,40,128]{2,1,0:T(8,128)S(1)}, f32[2,40,128]{2,1,0:T(8,128)S(1)}, u32[]{:S(2)}, u32[]{:S(2)}) %collective-permute-start.3) | collective-permute-done | bytes 40992 | tf_op jit(solution)/shard_map/ppermute | solution.py:345
  30.7 1.5 %collective-permute-start.4 = (f32[4,40,128]{2,1,0:T(8,128)S(1)}, f32[4,40,128]{2,1,0:T(8,128)S(1)}, u32[]{:S(2)}, u32[]{:S(2)}) collective-permute-start(f32[4,40,128]{2,1,0:T(8,128)S(1)} %pad_maximum_fusion.1), channel_id=1, source_target_pairs={{0,4},{4,0},{8,12},{12,8},{16,20},{20,16},{24,28},{28,24},{1,5},{5... | collective-permute-start | bytes 245768 | tf_op jit(solution)/shard_map/ppermute | solution.py:345
  32.1 0.1 pad_add_fusion.spot_ref
  32.2 2.9 %collective-permute-done.4 = f32[4,40,128]{2,1,0:T(8,128)S(1)} collective-permute-done((f32[4,40,128]{2,1,0:T(8,128)S(1)}, f32[4,40,128]{2,1,0:T(8,128)S(1)}, u32[]{:S(2)}, u32[]{:S(2)}) %collective-permute-start.4) | collective-permute-done | bytes 81952 | tf_op jit(solution)/shard_map/ppermute | solution.py:345
  35.1 0.7 %copy-done.5 = f32[4096]{0:T(1024)S(1)} copy-done((f32[4096]{0:T(1024)S(1)}, f32[4096]{0:T(1024)}, u32[]{:S(2)}) %copy-start.5) | copy-done | bytes 16408
  35.8 0.0 copy-done.6
  35.9 3.0 %weights.1.mix_ref = f32[8,128]{1,0:T(8,128)S(1)} custom-call(f32[320,128]{1,0:T(8,128)S(1)} %bitcast.24, s32[8,128]{1,0:T(8,128)S(1)} %pad_add_fusion.spot_ref, f32[8,128]{1,0:T(8,128)S(1)} %get-tuple-element.19.damp_ref, f32[8,128]{1,0:T(8,128)S(1)} %get-tuple-element.20.live_ref, f32[32,128]{1,0:T(8,128)S(1)} %bitcast.34, f32[32,128]{1,0:T(8,128)S(1)} %bitcast.36, ...), custom_call_target="tpu_custom_call" | custom-call | tf_op jit(solution)/shard_map/weights/pallas_call | solution.py:443
  38.8 0.0 all-to-all-done
  38.8 0.5 mix.1
  39.3 20.5 %all_to_all.10 = f32[8,4,8,512]{3,2,1,0:T(8,128)S(1)} all-to-all(f32[8,4,8,512]{3,2,1,0:T(8,128)S(1)} %mix.1), channel_id=1, replica_groups=mesh['member'=8,'tile'=4] {'member'}, dimensions={0} | all-to-all | bytes 1048576 | tf_op jit(solution)/shard_map/all_to_all | solution.py:470
  59.8 0.8 %copy_bitcast_fusion = f32[1,4,64,512]{3,2,1,0:T(8,128)} fusion(f32[8,4,8,512]{3,2,1,0:T(8,128)S(1)} %all_to_all.10), kind=kLoop, calls=%fused_computation | loop fusion | bytes 1048576 | tf_op jit(solution)/shard_map/reshape | solution.py:471
  (24 shorter events, 0.1 us)
Async XLA Ops:
  0.0 4.1 %copy-start = (f32[1,4,64,512]{3,2,1,0:T(8,128)S(1)}, f32[1,4,64,512]{3,2,1,0:T(8,128)}, u32[]{:S(2)}) copy-start(f32[1,4,64,512]{3,2,1,0:T(8,128)} %param.9) | copy-start | bytes 1572868
  0.0 4.1 %copy-start.1 = (f32[64,512]{1,0:T(8,128)S(1)}, f32[64,512]{1,0:T(8,128)}, u32[]{:S(2)}) copy-start(f32[64,512]{1,0:T(8,128)} %depth_ref.1) | copy-start | bytes 393220
  0.0 4.1 %copy-start.2 = (s32[64,512]{1,0:T(8,128)S(1)}, s32[64,512]{1,0:T(8,128)}, u32[]{:S(2)}) copy-start(s32[64,512]{1,0:T(8,128)} %mask_ref.1) | copy-start | bytes 393220
  2.0 1.2 %copy-start.7 = (s32[1,16,64]{2,1,0:T(8,128)S(1)}, s32[1,16,64]{2,1,0:T(8,128)}, u32[]{:S(2)}) copy-start(s32[1,16,64]{2,1,0:T(8,128)} %param.16) | copy-start | bytes 12292
  2.0 2.1 %collective-permute-start = (f32[104,512]{1,0:T(8,128)}, f32[104,512]{1,0:T(8,128)S(1)}, u32[]{:S(2)}, u32[]{:S(2)}) collective-permute-start(f32[104,512]{1,0:T(8,128)} %get-tuple-element.9), channel_id=1, source_target_pairs={{0,1},{2,3},{1,0},{3,2},{4,5},{6,7},{5,4},{7,6},{8,9},{10,11},{9,8... | collective-permute-start | bytes 638984 | tf_op jit(solution)/shard_map/ppermute | solution.py:358
  2.5 1.6 %collective-permute-start.1 = (f32[104,512]{1,0:T(8,128)}, f32[104,512]{1,0:T(8,128)S(1)}, u32[]{:S(2)}, u32[]{:S(2)}) collective-permute-start(f32[104,512]{1,0:T(8,128)} %get-tuple-element.10), channel_id=1, source_target_pairs={{1,2},{2,1},{5,6},{6,5},{9,10},{10,9},{13,14},{14,13},{17,18},{18,... | collective-permute-start | bytes 638984 | tf_op jit(solution)/shard_map/ppermute | solution.py:357
  3.2 0.9 %copy-start.4 = (f32[4096]{0:T(1024)S(1)}, f32[4096]{0:T(1024)}, u32[]{:S(2)}) copy-start(f32[4096]{0:T(1024)} %param.15) | copy-start | bytes 49156
  3.3 0.8 %copy-start.3 = (s32[4096]{0:T(1024)S(1)}, s32[4096]{0:T(1024)}, u32[]{:S(2)}) copy-start(s32[4096]{0:T(1024)} %param.12) | copy-start | bytes 49156
  3.3 0.7 %copy-start.8 = (s32[1,16]{1,0:T(1,128)S(1)}, s32[1,16]{1,0:T(1,128)}, u32[]{:S(2)}) copy-start(s32[1,16]{1,0:T(1,128)} %param.17) | copy-start | bytes 196
  6.8 32.0 %all-to-all-start = ((f32[8,128,128]{2,1,0:T(8,128)}), f32[8,128,128]{2,1,0:T(8,128)S(1)}, u32[]{:S(2)}, u32[]{:S(2)}) async-start(f32[8,128,128]{2,1,0:T(8,128)} %get-tuple-element.11), calls=%async_computation | async-start | bytes 1048576 | tf_op jit(solution)/shard_map/all_to_all | solution.py:433
  13.8 11.3 %collective-permute-start.2 = (f32[1,40,128]{2,1,0:T(8,128)S(1)}, f32[1,40,128]{2,1,0:T(8,128)S(1)}, u32[]{:S(2)}, u32[]{:S(2)}) collective-permute-start(f32[1,40,128]{2,1,0:T(8,128)S(1)} %bitcast.25), channel_id=1, source_target_pairs={{0,16},{4,20},{8,24},{12,28},{16,0},{20,4},{24,8},{28,12},{1,17},{... | collective-permute-start | bytes 61448 | tf_op jit(solution)/shard_map/ppermute | solution.py:345
  25.0 5.6 %collective-permute-start.3 = (f32[2,40,128]{2,1,0:T(8,128)S(1)}, f32[2,40,128]{2,1,0:T(8,128)S(1)}, u32[]{:S(2)}, u32[]{:S(2)}) collective-permute-start(f32[2,40,128]{2,1,0:T(8,128)S(1)} %pad_maximum_fusion.2), channel_id=1, source_target_pairs={{0,8},{4,12},{8,0},{12,4},{16,24},{20,28},{24,16},{28,20},{1,9},{5... | collective-permute-start | bytes 122888 | tf_op jit(solution)/shard_map/ppermute | solution.py:345
  30.7 4.4 %collective-permute-start.4 = (f32[4,40,128]{2,1,0:T(8,128)S(1)}, f32[4,40,128]{2,1,0:T(8,128)S(1)}, u32[]{:S(2)}, u32[]{:S(2)}) collective-permute-start(f32[4,40,128]{2,1,0:T(8,128)S(1)} %pad_maximum_fusion.1), channel_id=1, source_target_pairs={{0,4},{4,0},{8,12},{12,8},{16,20},{20,16},{24,28},{28,24},{1,5},{5... | collective-permute-start | bytes 245768 | tf_op jit(solution)/shard_map/ppermute | solution.py:345
  35.1 0.7 %copy-start.5 = (f32[4096]{0:T(1024)S(1)}, f32[4096]{0:T(1024)}, u32[]{:S(2)}) copy-start(f32[4096]{0:T(1024)} %param.13) | copy-start | bytes 49156
  35.1 0.7 %copy-start.6 = (f32[4096]{0:T(1024)S(1)}, f32[4096]{0:T(1024)}, u32[]{:S(2)}) copy-start(f32[4096]{0:T(1024)} %param.14) | copy-start | bytes 49156

commit v2 on v1

--- a/solution.py
+++ b/solution.py
@@ -22,6 +22,7 @@
 HIGH = lax.Precision.HIGHEST
 
 PAD = 8
+PACKED = 2
 
 
 def iota(shape, dim):
@@ -80,20 +81,11 @@
     gain_ref,
     near_ref,
     far_ref,
-    out_ref,
-    equiv_ref,
-    s_ref,
-    u_ref,
-    v_ref,
-    e_ref,
-    h_ref,
-    w_ref,
-    flux_ref,
-    part_ref,
-    cell_win,
-    gain_win,
+    *refs,
 ):
     members, own_rows, halo, obs_halo = sizes
+    out_ref, rest_refs, scratch = refs[0], refs[1 : members + 1], refs[members + 1 :]
+    s_ref, u_ref, v_ref, e_ref, h_ref, w_ref, flux_ref, part_ref, cell_win, gain_win = scratch
     even = lax.axis_index("tile") % 2 == 0
     rows, width = depth_ref.shape
     pieces = width // LANES
@@ -184,14 +176,22 @@
         equiv = equiv + lax.dot_general(
             part, spread, (((1,), (1,)), ((), ())), preferred_element_type=jnp.float32
         )
-    equiv_ref[...] = equiv * gain_win[...]
-
+    equiv = equiv * gain_win[...]
+
+    me = lax.axis_index("member")
     for j in range(members):
         source = first + j * own_rows
-        for i in range(4):
+        for i in range(PACKED):
             for q in range(pieces):
                 target = (i * pieces + q) * own_rows
                 out_ref[j, target : target + own_rows, :] = fields[i][q, source : source + own_rows, :]
+        body_rows = PACKED * pieces * own_rows
+        out_ref[j, body_rows : body_rows + window, :] = equiv
+        source = pl.multiple_of(first + (me ^ j) * own_rows, min(own_rows, 8))
+        for i in range(PACKED, 4):
+            for q in range(pieces):
+                target = ((i - PACKED) * pieces + q) * own_rows
+                rest_refs[j][target : target + own_rows, :] = fields[i][q, pl.ds(source, own_rows), :]
 
 
 def group_columns(left, starts, members):
@@ -205,14 +205,9 @@
     return terms[0]
 
 
-def relative(index, members):
-    bits = members.bit_length() - 1
-    return sum(((index >> i) & 1) << (bits - 1 - i) for i in range(bits))
-
-
 def weight_kernel(
     sizes,
-    equiv_ref,
+    recv_ref,
     spot_ref,
     damp_ref,
     live_ref,
@@ -226,6 +221,7 @@
 ):
     members, halo = sizes
     window = value_win.shape[0]
+    stride = recv_ref.shape[0] // members
     even = lax.axis_index("tile") % 2 == 0
     window_parts(value_win, value_ref[...], near_ref, far_ref, 6 * halo, 2, even)
     window_parts(error_win, error_ref[...], near_ref, far_ref, 6 * halo, 3, even)
@@ -239,7 +235,7 @@
     value = jnp.zeros((pairs, LANES), jnp.float32)
     error = jnp.zeros((pairs, LANES), jnp.float32)
     for r in range(window):
-        source = equiv_ref[pl.ds(r, members, stride=window), :]
+        source = recv_ref[pl.ds(stride - window + r, members, stride=stride), :]
         for i in range(pairs):
             got = jnp.take_along_axis(source, lanes_of[i], axis=1, mode="promise_in_bounds")
             picked[i] = jnp.where(rows_of[i] == r, got, picked[i])
@@ -305,28 +301,34 @@
     mix_ref[...] = mix
 
 
-def mix_kernel(sizes, recv_ref, mix_ref, out_ref, table_ref):
+def mix_kernel(sizes, recv_ref, mix_ref, *refs):
     members, own_rows, pieces = sizes
+    rest_refs, (out_ref, table_ref) = refs[:members], refs[members:]
     stride = recv_ref.shape[0] // members
     me = lax.axis_index("member")
-    table_ref[...] = mix_ref[...].T
-    bases = [pl.multiple_of((me ^ relative(k, members)) * stride, 8) for k in range(members)]
+    order = (iota((members, members), 0) == iota((members, members), 1) ^ me).astype(jnp.float32)
+    table_ref[...] = lax.dot_general(
+        mix_ref[...], order, (((0,), (0,)), ((), ())), preferred_element_type=jnp.float32, precision=HIGH
+    )
+    bases = [pl.multiple_of((me ^ d) * stride, 8) for d in range(members)]
 
     def analyse(m, carry):
-        target = me ^ relative(m, members)
         for side in range(2):
             coefs = table_ref[pl.ds(side * members + m, own_rows, stride=2 * members), :]
-            columns = [
-                jnp.broadcast_to(coefs[:, k : k + 1], (own_rows, LANES)) for k in range(members)
-            ]
+            columns = [jnp.broadcast_to(coefs[:, d : d + 1], (own_rows, LANES)) for d in range(members)]
             for i in range(4):
                 for q in range(side * pieces // 2, (side + 1) * pieces // 2):
-                    start = (i * pieces + q) * own_rows
                     total = None
-                    for k in range(members):
-                        term = columns[k] * recv_ref[pl.ds(bases[k] + start, own_rows), :]
+                    for d in range(members):
+                        if i < PACKED:
+                            start = (i * pieces + q) * own_rows
+                            block = recv_ref[pl.ds(bases[d] + start, own_rows), :]
+                        else:
+                            start = ((i - PACKED) * pieces + q) * own_rows
+                            block = rest_refs[d][start : start + own_rows, :]
+                        term = columns[d] * block
                         total = term if total is None else total + term
-                    out_ref[target, i, :, q * LANES : (q + 1) * LANES] = total
+                    out_ref[m, i, :, q * LANES : (q + 1) * LANES] = total
         return carry
 
     if members <= 8:
@@ -336,14 +338,11 @@
         lax.fori_loop(0, members, analyse, 0)
 
 
-def gather_members(block):
-    members = lax.axis_size("member")
-    held = block[None]
-    distance = members // 2
-    while distance:
-        pairs = [(i, i ^ distance) for i in range(members)]
-        held = jnp.concatenate([held, lax.ppermute(held, "member", pairs)], axis=0)
-        distance //= 2
+def trade(blocks):
+    members = len(blocks)
+    held = list(blocks)
+    for d in reversed(range(1, members)):
+        held[d] = lax.ppermute(blocks[d], "member", [(i, i ^ d) for i in range(members)])
     return held
 
 
@@ -408,16 +407,16 @@
     near, far = swaps(*edges)
 
     window = (obs_tile + 2 * radius) // LANES
-    packet = 4 * pieces * own_rows
+    packet = PACKED * pieces * own_rows + window
     grid = (pieces, rows + 2 * halo + 2 * PAD, LANES)
-    sends, equiv = pl.pallas_call(
+    sends, *rest = pl.pallas_call(
         functools.partial(forecast_kernel, (members, own_rows, halo, radius)),
         out_shape=[
             jax.ShapeDtypeStruct((members, packet, LANES), jnp.float32),
-            jax.ShapeDtypeStruct((window, LANES), jnp.float32),
-        ],
+        ]
+        + [jax.ShapeDtypeStruct(((4 - PACKED) * pieces * own_rows, LANES), jnp.float32)] * members,
         in_specs=vmem_specs(7),
-        out_specs=vmem_specs(2),
+        out_specs=vmem_specs(1 + members),
         scratch_shapes=[pltpu.VMEM(grid, jnp.float32)] * 8 + [pltpu.VMEM((window, LANES), jnp.float32)] * 2,
         compiler_params=pltpu.CompilerParams(vmem_limit_bytes=24 * 2**20),
         name="forecast",
@@ -431,7 +430,8 @@
         far,
     )
     received = lax.all_to_all(sends, "member", split_axis=0, concat_axis=0, tiled=True)
-    equivs = gather_members(equiv)
+    rest = trade(rest)
+    received = received.reshape(members * packet, LANES)
 
     patch_index = lax.axis_index("member") * per_dev + jnp.arange(per_dev, dtype=jnp.int32)
     row_index = patch_index * REGION_POINTS // width
@@ -449,7 +449,7 @@
         compiler_params=pltpu.CompilerParams(vmem_limit_bytes=24 * 2**20),
         name="weights",
     )(
-        equivs.reshape(members * window, LANES),
+        received,
         spot,
         side_by_side(damp, pairs),
         side_by_side(live.astype(jnp.float32), pairs),
@@ -461,12 +461,12 @@
     analysed = pl.pallas_call(
         functools.partial(mix_kernel, (members, own_rows, pieces)),
         out_shape=jax.ShapeDtypeStruct((members, 4, own_rows, width), jnp.float32),
-        in_specs=vmem_specs(2),
+        in_specs=vmem_specs(2 + members),
         out_specs=vmem_specs(1)[0],
         scratch_shapes=[pltpu.VMEM((LANES, members), jnp.float32)],
         compiler_params=pltpu.CompilerParams(vmem_limit_bytes=24 * 2**20),
         name="mix",
-    )(received.reshape(members * packet, LANES), mix)
+    )(received, mix, *rest)
     result = lax.all_to_all(analysed, "member", split_axis=0, concat_axis=0, tiled=True)
     return jnp.transpose(result, (1, 0, 2, 3)).reshape(1, 4, rows, width)
 

time: 61 us -> 51.4 us (0.84)
  the two profiles are of different devices: /device:TPU:0 before, /device:TPU:1 now
where the time goes in v2:
time: 51.4 us; the launch traced here: 51.1 us
  starting transfers between devices  20.3 us (39%)
  blocking collectives  15.5 us (30%)
  Pallas kernels  8.4 us (16%)
  waiting for transfers between devices  4.91 us (10%)
  local copies, waits for them, and re-layouts  1.54 us (3%)
    all_to_all x1, blocking collectives, body(): lax.all_to_all(analysed, 'member', split_axis=0, concat_axis=0, tiled=True)  15.5 us
    ppermute x7, starting transfers between devices, trade(): lax.ppermute(blocks[d], 'member', [(i, i ^ d) for i in range(members)])  9.56 us
    all_to_all x1, starting transfers between devices, body(): lax.all_to_all(sends, 'member', split_axis=0, concat_axis=0, tiled=True)  6.17 us
    ppermute x1, starting transfers between devices, swaps(): far = lax.ppermute(far, 'tile', pairs(1))  4.48 us
    pallas_call x1, Pallas kernels, body(): pl.pallas_call(functools.partial(weight_kernel, (members, halo)), out_sha...  2.96 us
    ppermute x1, waiting for transfers between devices, swaps(): far = lax.ppermute(far, 'tile', pairs(1))  2.85 us
    pallas_call x1, Pallas kernels, body(): pl.pallas_call(functools.partial(forecast_kernel, (members, own_rows, hal...  2.81 us
    pallas_call x1, Pallas kernels, body(): pl.pallas_call(functools.partial(edge_kernel, halo), out_shape=[jax.Shape...  1.98 us
  transfers between devices with their start and end apart: 10, of which 3 were waited for; matrix products, arithmetic and copies ran while one was open for 1% of the time, Pallas kernels for 6%

profile of v2, /device:TPU:1, one launch (start us, length us, event | category | flops | bytes accessed | tf_op | source)
XLA Modules:
  0.0 51.1 jit_solution(11355253796648347828)
XLA Ops:
  0.0 2.0 %edges.1 = (f32[104,512]{1,0:T(8,128)}, f32[104,512]{1,0:T(8,128)}) custom-call(f32[4,64,512]{2,1,0:T(8,128)} %bitcast.21, f32[64,512]{1,0:T(8,128)} %depth_ref.1, s32[64,512]{1,0:T(8,128)} %mask_ref.1, s32[32,128]{1,0:T(8,128)} %bitcast.23, f32[32,128]{1,0:T(8,128)} %bitcast.25, f32[32,128]{1,0:T(8,128)} %bitcast.27, f32[32,128]{1,0:T(8,128)} %bitcast.29), custom_call_target="tpu_custom_call" | custom-call | tf_op jit(solution)/shard_map/edges/pallas_call | solution.py:387
  2.0 0.1 collective-permute-start
  2.1 4.5 %collective-permute-start.1 = (f32[104,512]{1,0:T(8,128)}, f32[104,512]{1,0:T(8,128)S(1)}, u32[]{:S(2)}, u32[]{:S(2)}) collective-permute-start(f32[104,512]{1,0:T(8,128)} %get-tuple-element.17), channel_id=1, source_target_pairs={{1,2},{2,1},{5,6},{6,5},{9,10},{10,9},{13,14},{14,13},{17,18},{18,... | collective-permute-start | bytes 638984 | tf_op jit(solution)/shard_map/ppermute | solution.py:356
  6.7 0.1 multiply_add_fusion
  6.7 0.7 %copy-done.8 = s32[1,16]{1,0:T(1,128)S(1)} copy-done((s32[1,16]{1,0:T(1,128)S(1)}, s32[1,16]{1,0:T(1,128)}, u32[]{:S(2)}) %copy-start.8) | copy-done | bytes 88
  7.4 0.1 fusion.1
  7.5 2.9 %collective-permute-done.1.far_ref = f32[104,512]{1,0:T(8,128)S(1)} collective-permute-done((f32[104,512]{1,0:T(8,128)}, f32[104,512]{1,0:T(8,128)S(1)}, u32[]{:S(2)}, u32[]{:S(2)}) %collective-permute-start.1) | collective-permute-done | bytes 213024 | tf_op jit(solution)/shard_map/ppermute | solution.py:356
  10.4 2.8 %forecast.1 = (f32[8,104,128]{2,1,0:T(8,128)}, f32[64,128]{1,0:T(8,128)S(1)}, f32[64,128]{1,0:T(8,128)S(1)}, f32[64,128]{1,0:T(8,128)S(1)}, f32[64,128]{1,0:T(8,...) custom-call(f32[4,64,512]{2,1,0:T(8,128)S(1)} %bitcast.22, ...), custom_call_target="tpu_custom_call" | custom-call | tf_op jit(solution)/shard_map/forecast/pallas_call | solution.py:412
  13.2 6.2 %all-to-all-start = ((f32[8,104,128]{2,1,0:T(8,128)}), f32[8,104,128]{2,1,0:T(8,128)S(1)}, u32[]{:S(2)}, u32[]{:S(2)}) async-start(f32[8,104,128]{2,1,0:T(8,128)} %get-tuple-element.18), calls=%async_computation | async-start | bytes 851968 | tf_op jit(solution)/shard_map/all_to_all | solution.py:432
  19.4 1.5 %collective-permute-start.2 = (f32[64,128]{1,0:T(8,128)S(1)}, f32[64,128]{1,0:T(8,128)S(1)}, u32[]{:S(2)}, u32[]{:S(2)}) collective-permute-start(f32[64,128]{1,0:T(8,128)S(1)} %get-tuple-element.20), channel_id=1, source_target_pairs={{0,4},{4,0},{8,12},{12,8},{16,20},{20,16},{24,28},{28,24},{1,5},{5... | collective-permute-start | bytes 98312 | tf_op jit(solution)/shard_map/ppermute | solution.py:345
  20.9 1.2 %collective-permute-start.3 = (f32[64,128]{1,0:T(8,128)S(1)}, f32[64,128]{1,0:T(8,128)S(1)}, u32[]{:S(2)}, u32[]{:S(2)}) collective-permute-start(f32[64,128]{1,0:T(8,128)S(1)} %get-tuple-element.21), channel_id=1, source_target_pairs={{0,8},{4,12},{8,0},{12,4},{16,24},{20,28},{24,16},{28,20},{1,9},{5... | collective-permute-start | bytes 98312 | tf_op jit(solution)/shard_map/ppermute | solution.py:345
  22.1 0.1 pad_maximum_fusion
  22.1 0.1 collective-permute-start.4
  22.2 2.3 %collective-permute-start.5 = (f32[64,128]{1,0:T(8,128)S(1)}, f32[64,128]{1,0:T(8,128)S(1)}, u32[]{:S(2)}, u32[]{:S(2)}) collective-permute-start(f32[64,128]{1,0:T(8,128)S(1)} %get-tuple-element.23), channel_id=1, source_target_pairs={{0,16},{4,20},{8,24},{12,28},{16,0},{20,4},{24,8},{28,12},{1,17},{... | collective-permute-start | bytes 98312 | tf_op jit(solution)/shard_map/ppermute | solution.py:345
  24.5 1.2 %collective-permute-start.6 = (f32[64,128]{1,0:T(8,128)S(1)}, f32[64,128]{1,0:T(8,128)S(1)}, u32[]{:S(2)}, u32[]{:S(2)}) collective-permute-start(f32[64,128]{1,0:T(8,128)S(1)} %get-tuple-element.24), channel_id=1, source_target_pairs={{0,20},{4,16},{8,28},{12,24},{16,4},{20,0},{24,12},{28,8},{1,21},{... | collective-permute-start | bytes 98312 | tf_op jit(solution)/shard_map/ppermute | solution.py:345
  25.7 3.0 %collective-permute-start.7 = (f32[64,128]{1,0:T(8,128)S(1)}, f32[64,128]{1,0:T(8,128)S(1)}, u32[]{:S(2)}, u32[]{:S(2)}) collective-permute-start(f32[64,128]{1,0:T(8,128)S(1)} %get-tuple-element.25), channel_id=1, source_target_pairs={{0,24},{4,28},{8,16},{12,20},{16,8},{20,12},{24,0},{28,4},{1,25},{... | collective-permute-start | bytes 98312 | tf_op jit(solution)/shard_map/ppermute | solution.py:345
  28.7 0.3 collective-permute-start.8
  29.0 0.1 pad_add_fusion.spot_ref
  29.1 0.6 %all-to-all-done = f32[8,104,128]{2,1,0:T(8,128)S(1)} async-done(((f32[8,104,128]{2,1,0:T(8,128)}), f32[8,104,128]{2,1,0:T(8,128)S(1)}, u32[]{:S(2)}, u32[]{:S(2)}) %all-to-all-start) | async-done | bytes 426016 | tf_op jit(solution)/shard_map/all_to_all | solution.py:432
  29.7 3.0 %weights.1.mix_ref = f32[8,128]{1,0:T(8,128)S(1)} custom-call(f32[832,128]{1,0:T(8,128)S(1)} %bitcast.19, s32[8,128]{1,0:T(8,128)S(1)} %pad_add_fusion.spot_ref, f32[8,128]{1,0:T(8,128)S(1)} %get-tuple-element.33.damp_ref, f32[8,128]{1,0:T(8,128)S(1)} %get-tuple-element.34.live_ref, f32[32,128]{1,0:T(8,128)S(1)} %bitcast.28, f32[32,128]{1,0:T(8,128)S(1)} %bitcast.30, ...), custom_call_target="tpu_custom_call" | custom-call | tf_op jit(solution)/shard_map/weights/pallas_call | solution.py:443
  32.7 1.4 %collective-permute-done.8.refs_7_ = f32[64,128]{1,0:T(8,128)S(1)} collective-permute-done((f32[64,128]{1,0:T(8,128)S(1)}, f32[64,128]{1,0:T(8,128)S(1)}, u32[]{:S(2)}, u32[]{:S(2)}) %collective-permute-start.8) | collective-permute-done | bytes 32800 | tf_op jit(solution)/shard_map/ppermute | solution.py:345
  34.2 0.7 %mix.1 = f32[8,4,8,512]{3,2,1,0:T(8,128)S(1)} custom-call(f32[832,128]{1,0:T(8,128)S(1)} %bitcast.20, f32[8,128]{1,0:T(8,128)S(1)} %weights.1.mix_ref, f32[64,128]{1,0:T(8,128)S(1)} %get-tuple-element.19.refs_0_, f32[64,128]{1,0:T(8,128)S(1)} %collective-permute-done.2.refs_1_, f32[64,128]{1,0:T(8,128)S(1)} %collective-permute-done.3.refs_2_, ...), custom_call_target="tpu_custom_call" | custom-call | tf_op jit(solution)/shard_map/mix/pallas_call | solution.py:461
  34.8 15.5 %all_to_all.10 = f32[8,4,8,512]{3,2,1,0:T(8,128)S(1)} all-to-all(f32[8,4,8,512]{3,2,1,0:T(8,128)S(1)} %mix.1), channel_id=1, replica_groups=mesh['member'=8,'tile'=4] {'member'}, dimensions={0} | all-to-all | bytes 1048576 | tf_op jit(solution)/shard_map/all_to_all | solution.py:470
  50.3 0.8 %copy_bitcast_fusion = f32[1,4,64,512]{3,2,1,0:T(8,128)} fusion(f32[8,4,8,512]{3,2,1,0:T(8,128)S(1)} %all_to_all.10), kind=kLoop, calls=%fused_computation | loop fusion | bytes 1048576 | tf_op jit(solution)/shard_map/reshape | solution.py:471
  (29 shorter events, 0.1 us)
Async XLA Ops:
  0.0 10.3 %copy-start = (f32[1,4,64,512]{3,2,1,0:T(8,128)S(1)}, f32[1,4,64,512]{3,2,1,0:T(8,128)}, u32[]{:S(2)}) copy-start(f32[1,4,64,512]{3,2,1,0:T(8,128)} %param.9) | copy-start | bytes 1572868
  0.0 10.3 %copy-start.1 = (f32[64,512]{1,0:T(8,128)S(1)}, f32[64,512]{1,0:T(8,128)}, u32[]{:S(2)}) copy-start(f32[64,512]{1,0:T(8,128)} %depth_ref.1) | copy-start | bytes 393220
  0.0 10.3 %copy-start.2 = (s32[64,512]{1,0:T(8,128)S(1)}, s32[64,512]{1,0:T(8,128)}, u32[]{:S(2)}) copy-start(s32[64,512]{1,0:T(8,128)} %mask_ref.1) | copy-start | bytes 393220
  2.0 4.6 %copy-start.7 = (s32[1,16,64]{2,1,0:T(8,128)S(1)}, s32[1,16,64]{2,1,0:T(8,128)}, u32[]{:S(2)}) copy-start(s32[1,16,64]{2,1,0:T(8,128)} %param.16) | copy-start | bytes 12292
  2.0 5.5 %collective-permute-start = (f32[104,512]{1,0:T(8,128)}, f32[104,512]{1,0:T(8,128)S(1)}, u32[]{:S(2)}, u32[]{:S(2)}) collective-permute-start(f32[104,512]{1,0:T(8,128)} %get-tuple-element.16), channel_id=1, source_target_pairs={{0,1},{2,3},{1,0},{3,2},{4,5},{6,7},{5,4},{7,6},{8,9},{10,11},{9,8... | collective-permute-start | bytes 638984 | tf_op jit(solution)/shard_map/ppermute | solution.py:357
  2.1 8.2 %collective-permute-start.1 = (f32[104,512]{1,0:T(8,128)}, f32[104,512]{1,0:T(8,128)S(1)}, u32[]{:S(2)}, u32[]{:S(2)}) collective-permute-start(f32[104,512]{1,0:T(8,128)} %get-tuple-element.17), channel_id=1, source_target_pairs={{1,2},{2,1},{5,6},{6,5},{9,10},{10,9},{13,14},{14,13},{17,18},{18,... | collective-permute-start | bytes 638984 | tf_op jit(solution)/shard_map/ppermute | solution.py:356
  6.6 3.7 %copy-start.4 = (f32[4096]{0:T(1024)S(1)}, f32[4096]{0:T(1024)}, u32[]{:S(2)}) copy-start(f32[4096]{0:T(1024)} %param.15) | copy-start | bytes 49156
  6.7 3.6 %copy-start.3 = (s32[4096]{0:T(1024)S(1)}, s32[4096]{0:T(1024)}, u32[]{:S(2)}) copy-start(s32[4096]{0:T(1024)} %param.12) | copy-start | bytes 49156
  6.7 0.7 %copy-start.8 = (s32[1,16]{1,0:T(1,128)S(1)}, s32[1,16]{1,0:T(1,128)}, u32[]{:S(2)}) copy-start(s32[1,16]{1,0:T(1,128)} %param.17) | copy-start | bytes 196
  13.2 16.5 %all-to-all-start = ((f32[8,104,128]{2,1,0:T(8,128)}), f32[8,104,128]{2,1,0:T(8,128)S(1)}, u32[]{:S(2)}, u32[]{:S(2)}) async-start(f32[8,104,128]{2,1,0:T(8,128)} %get-tuple-element.18), calls=%async_computation | async-start | bytes 851968 | tf_op jit(solution)/shard_map/all_to_all | solution.py:432
  19.4 6.3 %collective-permute-start.2 = (f32[64,128]{1,0:T(8,128)S(1)}, f32[64,128]{1,0:T(8,128)S(1)}, u32[]{:S(2)}, u32[]{:S(2)}) collective-permute-start(f32[64,128]{1,0:T(8,128)S(1)} %get-tuple-element.20), channel_id=1, source_target_pairs={{0,4},{4,0},{8,12},{12,8},{16,20},{20,16},{24,28},{28,24},{1,5},{5... | collective-permute-start | bytes 98312 | tf_op jit(solution)/shard_map/ppermute | solution.py:345
  20.9 7.8 %collective-permute-start.3 = (f32[64,128]{1,0:T(8,128)S(1)}, f32[64,128]{1,0:T(8,128)S(1)}, u32[]{:S(2)}, u32[]{:S(2)}) collective-permute-start(f32[64,128]{1,0:T(8,128)S(1)} %get-tuple-element.21), channel_id=1, source_target_pairs={{0,8},{4,12},{8,0},{12,4},{16,24},{20,28},{24,16},{28,20},{1,9},{5... | collective-permute-start | bytes 98312 | tf_op jit(solution)/shard_map/ppermute | solution.py:345
  22.1 7.6 %copy-start.6 = (f32[4096]{0:T(1024)S(1)}, f32[4096]{0:T(1024)}, u32[]{:S(2)}) copy-start(f32[4096]{0:T(1024)} %param.14) | copy-start | bytes 49156
  22.1 7.6 %copy-start.5 = (f32[4096]{0:T(1024)S(1)}, f32[4096]{0:T(1024)}, u32[]{:S(2)}) copy-start(f32[4096]{0:T(1024)} %param.13) | copy-start | bytes 49156
  22.1 10.5 %collective-permute-start.4 = (f32[64,128]{1,0:T(8,128)S(1)}, f32[64,128]{1,0:T(8,128)S(1)}, u32[]{:S(2)}, u32[]{:S(2)}) collective-permute-start(f32[64,128]{1,0:T(8,128)S(1)} %get-tuple-element.22), channel_id=1, source_target_pairs={{0,12},{4,8},{8,4},{12,0},{16,28},{20,24},{24,20},{28,16},{1,13},{... | collective-permute-start | bytes 98312 | tf_op jit(solution)/shard_map/ppermute | solution.py:345
  22.2 10.4 %collective-permute-start.5 = (f32[64,128]{1,0:T(8,128)S(1)}, f32[64,128]{1,0:T(8,128)S(1)}, u32[]{:S(2)}, u32[]{:S(2)}) collective-permute-start(f32[64,128]{1,0:T(8,128)S(1)} %get-tuple-element.23), channel_id=1, source_target_pairs={{0,16},{4,20},{8,24},{12,28},{16,0},{20,4},{24,8},{28,12},{1,17},{... | collective-permute-start | bytes 98312 | tf_op jit(solution)/shard_map/ppermute | solution.py:345
  24.5 8.2 %collective-permute-start.6 = (f32[64,128]{1,0:T(8,128)S(1)}, f32[64,128]{1,0:T(8,128)S(1)}, u32[]{:S(2)}, u32[]{:S(2)}) collective-permute-start(f32[64,128]{1,0:T(8,128)S(1)} %get-tuple-element.24), channel_id=1, source_target_pairs={{0,20},{4,16},{8,28},{12,24},{16,4},{20,0},{24,12},{28,8},{1,21},{... | collective-permute-start | bytes 98312 | tf_op jit(solution)/shard_map/ppermute | solution.py:345
  25.7 7.0 %collective-permute-start.7 = (f32[64,128]{1,0:T(8,128)S(1)}, f32[64,128]{1,0:T(8,128)S(1)}, u32[]{:S(2)}, u32[]{:S(2)}) collective-permute-start(f32[64,128]{1,0:T(8,128)S(1)} %get-tuple-element.25), channel_id=1, source_target_pairs={{0,24},{4,28},{8,16},{12,20},{16,8},{20,12},{24,0},{28,4},{1,25},{... | collective-permute-start | bytes 98312 | tf_op jit(solution)/shard_map/ppermute | solution.py:345
  28.7 5.5 %collective-permute-start.8 = (f32[64,128]{1,0:T(8,128)S(1)}, f32[64,128]{1,0:T(8,128)S(1)}, u32[]{:S(2)}, u32[]{:S(2)}) collective-permute-start(f32[64,128]{1,0:T(8,128)S(1)} %get-tuple-element.26), channel_id=1, source_target_pairs={{0,28},{4,24},{8,20},{12,16},{16,12},{20,8},{24,4},{28,0},{1,29},{... | collective-permute-start | bytes 98312 | tf_op jit(solution)/shard_map/ppermute | solution.py:345

commit v3 on v2

--- a/solution.py
+++ b/solution.py
@@ -31,31 +31,47 @@
 
 def edge_kernel(halo, *refs):
     grids, obs, outs = refs[:3], refs[3:7], refs[7:9]
-    wet_ref, cell_ref, sems = refs[9:]
+    buf_ref, wet_ref, cell_ref, in_sems, out_sems = refs[9:]
     rows = grids[1].shape[0]
     inner = obs[0].shape[0]
     even = lax.axis_index("tile") % 2 == 0
-    copies = []
+    fetches, stores = [], []
 
     def fetch(source, target):
-        copies.append(pltpu.make_async_copy(source, target, sems.at[len(copies)]))
-        copies[-1].start()
-
-    for side, out in enumerate(outs):
-        is_last = even if side == 0 else jnp.logical_not(even)
-        start = pl.multiple_of(jnp.where(is_last, rows - halo, 0), 8)
-        for i in range(6):
+        fetches.append(pltpu.make_async_copy(source, target, in_sems.at[len(fetches)]))
+        fetches[-1].start()
+
+    def store(side, start, count):
+        span = pl.ds(start, count)
+        copy = pltpu.make_async_copy(buf_ref.at[side, span, :], outs[side].at[span, :], out_sems.at[len(stores)])
+        stores.append(copy)
+        copy.start()
+
+    is_last = [even, jnp.logical_not(even)]
+    for i in (5, 0, 1, 2, 3, 4):
+        for side in range(2):
+            start = pl.multiple_of(jnp.where(is_last[side], rows - halo, 0), 8)
             source = (grids[0].at[i] if i < 4 else grids[i - 3]).at[pl.ds(start, halo), :]
-            fetch(source, out.at[pl.ds(i * halo, halo), :] if i < 5 else wet_ref.at[side])
-        start = pl.multiple_of(jnp.where(is_last, inner - 8, 0), 8)
-        for j in range(4):
-            target = out.at[pl.ds(6 * halo, 8), pl.ds(j * LANES, LANES)] if j else cell_ref.at[side]
+            fetch(source, buf_ref.at[side, pl.ds(i * halo, halo), :] if i < 5 else wet_ref.at[side])
+    for j in range(4):
+        for side in range(2):
+            start = pl.multiple_of(jnp.where(is_last[side], inner - 8, 0), 8)
+            target = buf_ref.at[side, pl.ds(6 * halo, 8), pl.ds(j * LANES, LANES)] if j else cell_ref.at[side]
             fetch(obs[j].at[pl.ds(start, 8), :], target)
-    for copy in copies:
+    for at, copy in enumerate(fetches):
         copy.wait()
-    for side, out in enumerate(outs):
-        out[5 * halo : 6 * halo, :] = wet_ref[side].astype(jnp.float32)
-        out[6 * halo : 6 * halo + 8, 0:LANES] = (cell_ref[side] % CELLS_PER_OBS).astype(jnp.float32)
+        side = at % 2
+        if at < 2:
+            buf_ref[side, 5 * halo : 6 * halo, :] = wet_ref[side].astype(jnp.float32)
+            store(side, 5 * halo, halo)
+        elif at < 12:
+            store(side, (at // 2 - 1) * halo, halo)
+        elif at < 14:
+            buf_ref[side, 6 * halo : 6 * halo + 8, 0:LANES] = (cell_ref[side] % CELLS_PER_OBS).astype(jnp.float32)
+        elif at >= 18:
+            store(side, 6 * halo, 8)
+    for copy in stores:
+        copy.wait()
 
 
 def side_by_side(x, pairs):
@@ -85,7 +101,7 @@
 ):
     members, own_rows, halo, obs_halo = sizes
     out_ref, rest_refs, scratch = refs[0], refs[1 : members + 1], refs[members + 1 :]
-    s_ref, u_ref, v_ref, e_ref, h_ref, w_ref, flux_ref, part_ref, cell_win, gain_win = scratch
+    s_ref, u_ref, v_ref, e_ref, h_ref, w_ref, flux_ref, part_ref, cell_win, gain_win, pack_ref, equiv_buf, sems = scratch
     even = lax.axis_index("tile") % 2 == 0
     rows, width = depth_ref.shape
     pieces = width // LANES
@@ -148,6 +164,24 @@
                 e = e_ref[q, here, :]
                 e_ref[q, here, :] = w * (e - UPWIND * (e - e_ref[q, above, :]) - DAMPING * e)
 
+    me = lax.axis_index("member")
+    copies = []
+    for j in range(members):
+        source = first + j * own_rows
+        for i in range(PACKED):
+            for q in range(pieces):
+                target = (i * pieces + q) * own_rows
+                pack_ref[j, target : target + own_rows, :] = fields[i][q, source : source + own_rows, :]
+        target = out_ref.at[j, pl.ds(0, PACKED * pieces * own_rows), :]
+        copies.append(pltpu.make_async_copy(pack_ref.at[j], target, sems.at[j]))
+        copies[-1].start()
+    for j in range(members):
+        source = pl.multiple_of(first + (me ^ j) * own_rows, min(own_rows, 8))
+        for i in range(PACKED, 4):
+            for q in range(pieces):
+                target = ((i - PACKED) * pieces + q) * own_rows
+                rest_refs[j][target : target + own_rows, :] = fields[i][q, pl.ds(source, own_rows), :]
+
     window = cell_win.shape[0]
     base = 6 * halo
     offsets = (cell_ref[...] % CELLS_PER_OBS).astype(jnp.float32)
@@ -178,20 +212,14 @@
         )
     equiv = equiv * gain_win[...]
 
-    me = lax.axis_index("member")
+    equiv_buf[...] = equiv
+    body_rows = PACKED * pieces * own_rows
     for j in range(members):
-        source = first + j * own_rows
-        for i in range(PACKED):
-            for q in range(pieces):
-                target = (i * pieces + q) * own_rows
-                out_ref[j, target : target + own_rows, :] = fields[i][q, source : source + own_rows, :]
-        body_rows = PACKED * pieces * own_rows
-        out_ref[j, body_rows : body_rows + window, :] = equiv
-        source = pl.multiple_of(first + (me ^ j) * own_rows, min(own_rows, 8))
-        for i in range(PACKED, 4):
-            for q in range(pieces):
-                target = ((i - PACKED) * pieces + q) * own_rows
-                rest_refs[j][target : target + own_rows, :] = fields[i][q, pl.ds(source, own_rows), :]
+        target = out_ref.at[j, pl.ds(body_rows, window), :]
+        copies.append(pltpu.make_async_copy(equiv_buf, target, sems.at[members + j]))
+        copies[-1].start()
+    for copy in copies:
+        copy.wait()
 
 
 def group_columns(left, starts, members):
@@ -344,6 +372,17 @@
     for d in reversed(range(1, members)):
         held[d] = lax.ppermute(blocks[d], "member", [(i, i ^ d) for i in range(members)])
     return held
+
+
+def place_kernel(recv_ref, out_ref, sems):
+    members, _, own_rows, _ = recv_ref.shape
+    copies = []
+    for j in range(members):
+        target = out_ref.at[:, pl.ds(j * own_rows, own_rows), :]
+        copies.append(pltpu.make_async_copy(recv_ref.at[j], target, sems.at[j]))
+        copies[-1].start()
+    for copy in copies:
+        copy.wait()
 
 
 def swaps(near, far):
@@ -388,11 +427,13 @@
         functools.partial(edge_kernel, halo),
         out_shape=[jax.ShapeDtypeStruct((6 * halo + 8, width), jnp.float32)] * 2,
         in_specs=[pl.BlockSpec(memory_space=pl.ANY)] * 7,
-        out_specs=vmem_specs(2),
+        out_specs=[pl.BlockSpec(memory_space=pl.ANY)] * 2,
         scratch_shapes=[
+            pltpu.VMEM((2, 6 * halo + 8, width), jnp.float32),
             pltpu.VMEM((2, halo, width), jnp.int32),
             pltpu.VMEM((2, 8, LANES), jnp.int32),
             pltpu.SemaphoreType.DMA((20,)),
+            pltpu.SemaphoreType.DMA((14,)),
         ],
         name="edges",
     )(
@@ -416,8 +457,14 @@
         ]
         + [jax.ShapeDtypeStruct(((4 - PACKED) * pieces * own_rows, LANES), jnp.float32)] * members,
         in_specs=vmem_specs(7),
-        out_specs=vmem_specs(1 + members),
-        scratch_shapes=[pltpu.VMEM(grid, jnp.float32)] * 8 + [pltpu.VMEM((window, LANES), jnp.float32)] * 2,
+        out_specs=[pl.BlockSpec(memory_space=pl.ANY)] + vmem_specs(members),
+        scratch_shapes=[pltpu.VMEM(grid, jnp.float32)] * 8
+        + [pltpu.VMEM((window, LANES), jnp.float32)] * 2
+        + [
+            pltpu.VMEM((members, packet - window, LANES), jnp.float32),
+            pltpu.VMEM((window, LANES), jnp.float32),
+            pltpu.SemaphoreType.DMA((2 * members,)),
+        ],
         compiler_params=pltpu.CompilerParams(vmem_limit_bytes=24 * 2**20),
         name="forecast",
     )(
@@ -468,7 +515,16 @@
         name="mix",
     )(received, mix, *rest)
     result = lax.all_to_all(analysed, "member", split_axis=0, concat_axis=0, tiled=True)
-    return jnp.transpose(result, (1, 0, 2, 3)).reshape(1, 4, rows, width)
+    if own_rows % 8:
+        return jnp.transpose(result, (1, 0, 2, 3)).reshape(1, 4, rows, width)
+    return pl.pallas_call(
+        place_kernel,
+        out_shape=jax.ShapeDtypeStruct((4, rows, width), jnp.float32),
+        in_specs=vmem_specs(1),
+        out_specs=pl.BlockSpec(memory_space=pl.ANY),
+        scratch_shapes=[pltpu.SemaphoreType.DMA((members,))],
+        name="place",
+    )(result)[None]
 
 
 def solution(mesh):

time: 51.4 us -> 53.1 us (1.033)
  Pallas kernels: 8.4 us -> 10.3 us
  local copies, waits for them, and re-layouts: 1.54 us -> 0.71 us
    pallas_call x0 -> x1, Pallas kernels: none -> 1.89 us  [body(): pl.pallas_call(place_kernel, out_shape=jax.ShapeDtypeStruct((4, rows, wid...]
    reshape x1 -> x0, local copies, waits for them, and re-layouts: 0.83 us -> none  [body(): return jnp.transpose(result, (1, 0, 2, 3)).reshape(1, 4, rows, width)]
where the time goes in v3:
time: 53.1 us; the launch traced here: 52.7 us
  starting transfers between devices  20.3 us (38%)
  blocking collectives  16 us (30%)
  Pallas kernels  10.3 us (19%)
  waiting for transfers between devices  4.9 us (9%)
  local copies, waits for them, and re-layouts  0.71 us (1%)
    all_to_all x1, blocking collectives, body(): lax.all_to_all(analysed, 'member', split_axis=0, concat_axis=0, tiled=True)  16 us
    ppermute x7, starting transfers between devices, trade(): lax.ppermute(blocks[d], 'member', [(i, i ^ d) for i in range(members)])  9.56 us
    all_to_all x1, starting transfers between devices, body(): lax.all_to_all(sends, 'member', split_axis=0, concat_axis=0, tiled=True)  6.18 us
    ppermute x1, starting transfers between devices, swaps(): far = lax.ppermute(far, 'tile', pairs(1))  4.48 us
    pallas_call x1, Pallas kernels, body(): pl.pallas_call(functools.partial(weight_kernel, (members, halo)), out_sha...  2.97 us
    ppermute x1, waiting for transfers between devices, swaps(): far = lax.ppermute(far, 'tile', pairs(1))  2.85 us
    pallas_call x1, Pallas kernels, body(): pl.pallas_call(functools.partial(forecast_kernel, (members, own_rows, hal...  2.82 us
    pallas_call x1, Pallas kernels, body(): pl.pallas_call(functools.partial(edge_kernel, halo), out_shape=[jax.Shape...  1.95 us
  transfers between devices with their start and end apart: 10, of which 3 were waited for; matrix products, arithmetic and copies ran while one was open for 1% of the time, Pallas kernels for 6%

profile of v3, /device:TPU:1, one launch (start us, length us, event | category | flops | bytes accessed | tf_op | source)
XLA Modules:
  0.0 52.7 jit_solution(9851002631933507853)
XLA Ops:
  0.0 2.0 %edges.1 = (f32[104,512]{1,0:T(8,128)}, f32[104,512]{1,0:T(8,128)}) custom-call(f32[4,64,512]{2,1,0:T(8,128)} %bitcast.17, f32[64,512]{1,0:T(8,128)} %depth_ref.1, s32[64,512]{1,0:T(8,128)} %mask_ref.1, s32[32,128]{1,0:T(8,128)} %bitcast.19, f32[32,128]{1,0:T(8,128)} %bitcast.21, f32[32,128]{1,0:T(8,128)} %bitcast.23, f32[32,128]{1,0:T(8,128)} %bitcast.25), custom_call_target="tpu_custom_call" | custom-call | tf_op jit(solution)/shard_map/edges/pallas_call | solution.py:426
  2.0 0.1 collective-permute-start
  2.1 4.5 %collective-permute-start.1 = (f32[104,512]{1,0:T(8,128)}, f32[104,512]{1,0:T(8,128)S(1)}, u32[]{:S(2)}, u32[]{:S(2)}) collective-permute-start(f32[104,512]{1,0:T(8,128)} %get-tuple-element.17), channel_id=1, source_target_pairs={{1,2},{2,1},{5,6},{6,5},{9,10},{10,9},{13,14},{14,13},{17,18},{18,... | collective-permute-start | bytes 638984 | tf_op jit(solution)/shard_map/ppermute | solution.py:395
  6.6 0.1 multiply_add_fusion
  6.7 0.7 %copy-done.8 = s32[1,16]{1,0:T(1,128)S(1)} copy-done((s32[1,16]{1,0:T(1,128)S(1)}, s32[1,16]{1,0:T(1,128)}, u32[]{:S(2)}) %copy-start.8) | copy-done | bytes 88
  7.4 0.1 fusion.1
  7.5 2.9 %collective-permute-done.1.far_ref = f32[104,512]{1,0:T(8,128)S(1)} collective-permute-done((f32[104,512]{1,0:T(8,128)}, f32[104,512]{1,0:T(8,128)S(1)}, u32[]{:S(2)}, u32[]{:S(2)}) %collective-permute-start.1) | collective-permute-done | bytes 213024 | tf_op jit(solution)/shard_map/ppermute | solution.py:395
  10.3 2.8 %forecast.1 = (f32[8,104,128]{2,1,0:T(8,128)}, f32[64,128]{1,0:T(8,128)S(1)}, f32[64,128]{1,0:T(8,128)S(1)}, f32[64,128]{1,0:T(8,128)S(1)}, f32[64,128]{1,0:T(8,...) custom-call(f32[4,64,512]{2,1,0:T(8,128)S(1)} %bitcast.18, ...), custom_call_target="tpu_custom_call" | custom-call | tf_op jit(solution)/shard_map/forecast/pallas_call | solution.py:453
  13.2 6.2 %all-to-all-start = ((f32[8,104,128]{2,1,0:T(8,128)}), f32[8,104,128]{2,1,0:T(8,128)S(1)}, u32[]{:S(2)}, u32[]{:S(2)}) async-start(f32[8,104,128]{2,1,0:T(8,128)} %get-tuple-element.18), calls=%async_computation | async-start | bytes 851968 | tf_op jit(solution)/shard_map/all_to_all | solution.py:479
  19.4 1.5 %collective-permute-start.2 = (f32[64,128]{1,0:T(8,128)S(1)}, f32[64,128]{1,0:T(8,128)S(1)}, u32[]{:S(2)}, u32[]{:S(2)}) collective-permute-start(f32[64,128]{1,0:T(8,128)S(1)} %get-tuple-element.20), channel_id=1, source_target_pairs={{0,4},{4,0},{8,12},{12,8},{16,20},{20,16},{24,28},{28,24},{1,5},{5... | collective-permute-start | bytes 98312 | tf_op jit(solution)/shard_map/ppermute | solution.py:373
  20.9 1.2 %collective-permute-start.3 = (f32[64,128]{1,0:T(8,128)S(1)}, f32[64,128]{1,0:T(8,128)S(1)}, u32[]{:S(2)}, u32[]{:S(2)}) collective-permute-start(f32[64,128]{1,0:T(8,128)S(1)} %get-tuple-element.21), channel_id=1, source_target_pairs={{0,8},{4,12},{8,0},{12,4},{16,24},{20,28},{24,16},{28,20},{1,9},{5... | collective-permute-start | bytes 98312 | tf_op jit(solution)/shard_map/ppermute | solution.py:373
  22.1 0.1 pad_maximum_fusion
  22.1 0.1 collective-permute-start.4
  22.2 2.3 %collective-permute-start.5 = (f32[64,128]{1,0:T(8,128)S(1)}, f32[64,128]{1,0:T(8,128)S(1)}, u32[]{:S(2)}, u32[]{:S(2)}) collective-permute-start(f32[64,128]{1,0:T(8,128)S(1)} %get-tuple-element.23), channel_id=1, source_target_pairs={{0,16},{4,20},{8,24},{12,28},{16,0},{20,4},{24,8},{28,12},{1,17},{... | collective-permute-start | bytes 98312 | tf_op jit(solution)/shard_map/ppermute | solution.py:373
  24.5 1.2 %collective-permute-start.6 = (f32[64,128]{1,0:T(8,128)S(1)}, f32[64,128]{1,0:T(8,128)S(1)}, u32[]{:S(2)}, u32[]{:S(2)}) collective-permute-start(f32[64,128]{1,0:T(8,128)S(1)} %get-tuple-element.24), channel_id=1, source_target_pairs={{0,20},{4,16},{8,28},{12,24},{16,4},{20,0},{24,12},{28,8},{1,21},{... | collective-permute-start | bytes 98312 | tf_op jit(solution)/shard_map/ppermute | solution.py:373
  25.7 3.0 %collective-permute-start.7 = (f32[64,128]{1,0:T(8,128)S(1)}, f32[64,128]{1,0:T(8,128)S(1)}, u32[]{:S(2)}, u32[]{:S(2)}) collective-permute-start(f32[64,128]{1,0:T(8,128)S(1)} %get-tuple-element.25), channel_id=1, source_target_pairs={{0,24},{4,28},{8,16},{12,20},{16,8},{20,12},{24,0},{28,4},{1,25},{... | collective-permute-start | bytes 98312 | tf_op jit(solution)/shard_map/ppermute | solution.py:373
  28.7 0.3 collective-permute-start.8
  29.0 0.1 pad_add_fusion.spot_ref
  29.1 0.6 %all-to-all-done = f32[8,104,128]{2,1,0:T(8,128)S(1)} async-done(((f32[8,104,128]{2,1,0:T(8,128)}), f32[8,104,128]{2,1,0:T(8,128)S(1)}, u32[]{:S(2)}, u32[]{:S(2)}) %all-to-all-start) | async-done | bytes 426016 | tf_op jit(solution)/shard_map/all_to_all | solution.py:479
  29.7 3.0 %weights.1.mix_ref = f32[8,128]{1,0:T(8,128)S(1)} custom-call(f32[832,128]{1,0:T(8,128)S(1)} %bitcast.15, s32[8,128]{1,0:T(8,128)S(1)} %pad_add_fusion.spot_ref, f32[8,128]{1,0:T(8,128)S(1)} %get-tuple-element.33.damp_ref, f32[8,128]{1,0:T(8,128)S(1)} %get-tuple-element.34.live_ref, f32[32,128]{1,0:T(8,128)S(1)} %bitcast.24, f32[32,128]{1,0:T(8,128)S(1)} %bitcast.26, ...), custom_call_target="tpu_custom_call" | custom-call | tf_op jit(solution)/shard_map/weights/pallas_call | solution.py:490
  32.7 1.4 %collective-permute-done.8.refs_7_ = f32[64,128]{1,0:T(8,128)S(1)} collective-permute-done((f32[64,128]{1,0:T(8,128)S(1)}, f32[64,128]{1,0:T(8,128)S(1)}, u32[]{:S(2)}, u32[]{:S(2)}) %collective-permute-start.8) | collective-permute-done | bytes 32800 | tf_op jit(solution)/shard_map/ppermute | solution.py:373
  34.2 0.7 %mix.1 = f32[8,4,8,512]{3,2,1,0:T(8,128)S(1)} custom-call(f32[832,128]{1,0:T(8,128)S(1)} %bitcast.16, f32[8,128]{1,0:T(8,128)S(1)} %weights.1.mix_ref, f32[64,128]{1,0:T(8,128)S(1)} %get-tuple-element.19.refs_0_, f32[64,128]{1,0:T(8,128)S(1)} %collective-permute-done.2.refs_1_, f32[64,128]{1,0:T(8,128)S(1)} %collective-permute-done.3.refs_2_, ...), custom_call_target="tpu_custom_call" | custom-call | tf_op jit(solution)/shard_map/mix/pallas_call | solution.py:508
  34.8 16.0 %all_to_all.10.recv_ref = f32[8,4,8,512]{3,2,1,0:T(8,128)} all-to-all(f32[8,4,8,512]{3,2,1,0:T(8,128)S(1)} %mix.1), channel_id=1, replica_groups=mesh['member'=8,'tile'=4] {'member'}, dimensions={0} | all-to-all | bytes 1048576 | tf_op jit(solution)/shard_map/all_to_all | solution.py:517
  50.8 1.9 %place.1 = f32[4,64,512]{2,1,0:T(8,128)} custom-call(f32[8,4,8,512]{3,2,1,0:T(8,128)} %all_to_all.10.recv_ref), custom_call_target="tpu_custom_call" | custom-call | tf_op jit(solution)/shard_map/place/pallas_call | solution.py:520
  (29 shorter events, 0.1 us)
Async XLA Ops:
  0.0 10.3 %copy-start = (f32[1,4,64,512]{3,2,1,0:T(8,128)S(1)}, f32[1,4,64,512]{3,2,1,0:T(8,128)}, u32[]{:S(2)}) copy-start(f32[1,4,64,512]{3,2,1,0:T(8,128)} %param.9) | copy-start | bytes 1572868
  0.0 10.3 %copy-start.1 = (f32[64,512]{1,0:T(8,128)S(1)}, f32[64,512]{1,0:T(8,128)}, u32[]{:S(2)}) copy-start(f32[64,512]{1,0:T(8,128)} %depth_ref.1) | copy-start | bytes 393220
  0.0 10.3 %copy-start.2 = (s32[64,512]{1,0:T(8,128)S(1)}, s32[64,512]{1,0:T(8,128)}, u32[]{:S(2)}) copy-start(s32[64,512]{1,0:T(8,128)} %mask_ref.1) | copy-start | bytes 393220
  2.0 4.6 %copy-start.7 = (s32[1,16,64]{2,1,0:T(8,128)S(1)}, s32[1,16,64]{2,1,0:T(8,128)}, u32[]{:S(2)}) copy-start(s32[1,16,64]{2,1,0:T(8,128)} %param.16) | copy-start | bytes 12292
  2.0 5.5 %collective-permute-start = (f32[104,512]{1,0:T(8,128)}, f32[104,512]{1,0:T(8,128)S(1)}, u32[]{:S(2)}, u32[]{:S(2)}) collective-permute-start(f32[104,512]{1,0:T(8,128)} %get-tuple-element.16), channel_id=1, source_target_pairs={{0,1},{2,3},{1,0},{3,2},{4,5},{6,7},{5,4},{7,6},{8,9},{10,11},{9,8... | collective-permute-start | bytes 638984 | tf_op jit(solution)/shard_map/ppermute | solution.py:396
  2.1 8.2 %collective-permute-start.1 = (f32[104,512]{1,0:T(8,128)}, f32[104,512]{1,0:T(8,128)S(1)}, u32[]{:S(2)}, u32[]{:S(2)}) collective-permute-start(f32[104,512]{1,0:T(8,128)} %get-tuple-element.17), channel_id=1, source_target_pairs={{1,2},{2,1},{5,6},{6,5},{9,10},{10,9},{13,14},{14,13},{17,18},{18,... | collective-permute-start | bytes 638984 | tf_op jit(solution)/shard_map/ppermute | solution.py:395
  6.6 3.7 %copy-start.4 = (f32[4096]{0:T(1024)S(1)}, f32[4096]{0:T(1024)}, u32[]{:S(2)}) copy-start(f32[4096]{0:T(1024)} %param.15) | copy-start | bytes 49156
  6.7 3.6 %copy-start.3 = (s32[4096]{0:T(1024)S(1)}, s32[4096]{0:T(1024)}, u32[]{:S(2)}) copy-start(s32[4096]{0:T(1024)} %param.12) | copy-start | bytes 49156
  6.7 0.7 %copy-start.8 = (s32[1,16]{1,0:T(1,128)S(1)}, s32[1,16]{1,0:T(1,128)}, u32[]{:S(2)}) copy-start(s32[1,16]{1,0:T(1,128)} %param.17) | copy-start | bytes 196
  13.2 16.5 %all-to-all-start = ((f32[8,104,128]{2,1,0:T(8,128)}), f32[8,104,128]{2,1,0:T(8,128)S(1)}, u32[]{:S(2)}, u32[]{:S(2)}) async-start(f32[8,104,128]{2,1,0:T(8,128)} %get-tuple-element.18), calls=%async_computation | async-start | bytes 851968 | tf_op jit(solution)/shard_map/all_to_all | solution.py:479
  19.4 6.3 %collective-permute-start.2 = (f32[64,128]{1,0:T(8,128)S(1)}, f32[64,128]{1,0:T(8,128)S(1)}, u32[]{:S(2)}, u32[]{:S(2)}) collective-permute-start(f32[64,128]{1,0:T(8,128)S(1)} %get-tuple-element.20), channel_id=1, source_target_pairs={{0,4},{4,0},{8,12},{12,8},{16,20},{20,16},{24,28},{28,24},{1,5},{5... | collective-permute-start | bytes 98312 | tf_op jit(solution)/shard_map/ppermute | solution.py:373
  20.9 7.8 %collective-permute-start.3 = (f32[64,128]{1,0:T(8,128)S(1)}, f32[64,128]{1,0:T(8,128)S(1)}, u32[]{:S(2)}, u32[]{:S(2)}) collective-permute-start(f32[64,128]{1,0:T(8,128)S(1)} %get-tuple-element.21), channel_id=1, source_target_pairs={{0,8},{4,12},{8,0},{12,4},{16,24},{20,28},{24,16},{28,20},{1,9},{5... | collective-permute-start | bytes 98312 | tf_op jit(solution)/shard_map/ppermute | solution.py:373
  22.1 7.6 %copy-start.6 = (f32[4096]{0:T(1024)S(1)}, f32[4096]{0:T(1024)}, u32[]{:S(2)}) copy-start(f32[4096]{0:T(1024)} %param.14) | copy-start | bytes 49156
  22.1 7.6 %copy-start.5 = (f32[4096]{0:T(1024)S(1)}, f32[4096]{0:T(1024)}, u32[]{:S(2)}) copy-start(f32[4096]{0:T(1024)} %param.13) | copy-start | bytes 49156
  22.1 10.5 %collective-permute-start.4 = (f32[64,128]{1,0:T(8,128)S(1)}, f32[64,128]{1,0:T(8,128)S(1)}, u32[]{:S(2)}, u32[]{:S(2)}) collective-permute-start(f32[64,128]{1,0:T(8,128)S(1)} %get-tuple-element.22), channel_id=1, source_target_pairs={{0,12},{4,8},{8,4},{12,0},{16,28},{20,24},{24,20},{28,16},{1,13},{... | collective-permute-start | bytes 98312 | tf_op jit(solution)/shard_map/ppermute | solution.py:373
  22.2 10.5 %collective-permute-start.5 = (f32[64,128]{1,0:T(8,128)S(1)}, f32[64,128]{1,0:T(8,128)S(1)}, u32[]{:S(2)}, u32[]{:S(2)}) collective-permute-start(f32[64,128]{1,0:T(8,128)S(1)} %get-tuple-element.23), channel_id=1, source_target_pairs={{0,16},{4,20},{8,24},{12,28},{16,0},{20,4},{24,8},{28,12},{1,17},{... | collective-permute-start | bytes 98312 | tf_op jit(solution)/shard_map/ppermute | solution.py:373
  24.5 8.2 %collective-permute-start.6 = (f32[64,128]{1,0:T(8,128)S(1)}, f32[64,128]{1,0:T(8,128)S(1)}, u32[]{:S(2)}, u32[]{:S(2)}) collective-permute-start(f32[64,128]{1,0:T(8,128)S(1)} %get-tuple-element.24), channel_id=1, source_target_pairs={{0,20},{4,16},{8,28},{12,24},{16,4},{20,0},{24,12},{28,8},{1,21},{... | collective-permute-start | bytes 98312 | tf_op jit(solution)/shard_map/ppermute | solution.py:373
  25.7 7.0 %collective-permute-start.7 = (f32[64,128]{1,0:T(8,128)S(1)}, f32[64,128]{1,0:T(8,128)S(1)}, u32[]{:S(2)}, u32[]{:S(2)}) collective-permute-start(f32[64,128]{1,0:T(8,128)S(1)} %get-tuple-element.25), channel_id=1, source_target_pairs={{0,24},{4,28},{8,16},{12,20},{16,8},{20,12},{24,0},{28,4},{1,25},{... | collective-permute-start | bytes 98312 | tf_op jit(solution)/shard_map/ppermute | solution.py:373
  28.7 5.5 %collective-permute-start.8 = (f32[64,128]{1,0:T(8,128)S(1)}, f32[64,128]{1,0:T(8,128)S(1)}, u32[]{:S(2)}, u32[]{:S(2)}) collective-permute-start(f32[64,128]{1,0:T(8,128)S(1)} %get-tuple-element.26), channel_id=1, source_target_pairs={{0,28},{4,24},{8,20},{12,16},{16,12},{20,8},{24,4},{28,0},{1,29},{... | collective-permute-start | bytes 98312 | tf_op jit(solution)/shard_map/ppermute | solution.py:373

commit v4 on v2

--- a/solution.py
+++ b/solution.py
@@ -386,7 +386,7 @@
     pairs = per_dev * slots // LANES
     edges = pl.pallas_call(
         functools.partial(edge_kernel, halo),
-        out_shape=[jax.ShapeDtypeStruct((6 * halo + 8, width), jnp.float32)] * 2,
+        out_shape=[pltpu.VMEM((6 * halo + 8, width), jnp.float32)] * 2,
         in_specs=[pl.BlockSpec(memory_space=pl.ANY)] * 7,
         out_specs=vmem_specs(2),
         scratch_shapes=[
@@ -412,7 +412,7 @@
     sends, *rest = pl.pallas_call(
         functools.partial(forecast_kernel, (members, own_rows, halo, radius)),
         out_shape=[
-            jax.ShapeDtypeStruct((members, packet, LANES), jnp.float32),
+            pltpu.VMEM((members, packet, LANES), jnp.float32),
         ]
         + [jax.ShapeDtypeStruct(((4 - PACKED) * pieces * own_rows, LANES), jnp.float32)] * members,
         in_specs=vmem_specs(7),

time: 51.4 us -> 50.6 us (0.984)
  Pallas kernels: 8.4 us -> 7.66 us
    all_to_all x1, waiting for transfers between devices: 0.59 us -> 2.29 us  [body(): lax.all_to_all(sends, 'member', split_axis=0, concat_axis=0, tiled=True)]
    ppermute x7, waiting for transfers between devices: 1.46 us -> 0.02 us  [trade(): lax.ppermute(blocks[d], 'member', [(i, i ^ d) for i in range(members)])]
    pallas_call x1, Pallas kernels: 1.98 us -> 1.23 us  [body(): pl.pallas_call(functools.partial(edge_kernel, halo), out_shape=[pltpu.VME...]
  transfers between devices with their start and end apart: 10 -> 10, of which waited for: 3 -> 2; matrix products, arithmetic and copies ran while one was open for 1% -> 1% of each run, Pallas kernels for 6% -> 6%
where the time goes in v4:
time: 50.6 us; the launch traced here: 50.3 us
  starting transfers between devices  20.1 us (40%)
  blocking collectives  15.6 us (31%)
  Pallas kernels  7.66 us (15%)
  waiting for transfers between devices  4.95 us (10%)
  local copies, waits for them, and re-layouts  1.54 us (3%)
    all_to_all x1, blocking collectives, body(): lax.all_to_all(analysed, 'member', split_axis=0, concat_axis=0, tiled=True)  15.6 us
    ppermute x7, starting transfers between devices, trade(): lax.ppermute(blocks[d], 'member', [(i, i ^ d) for i in range(members)])  9.31 us
    all_to_all x1, starting transfers between devices, body(): lax.all_to_all(sends, 'member', split_axis=0, concat_axis=0, tiled=True)  6.17 us
    ppermute x1, starting transfers between devices, swaps(): far = lax.ppermute(far, 'tile', pairs(1))  4.48 us
    pallas_call x1, Pallas kernels, body(): pl.pallas_call(functools.partial(weight_kernel, (members, halo)), out_sha...  2.97 us
    pallas_call x1, Pallas kernels, body(): pl.pallas_call(functools.partial(forecast_kernel, (members, own_rows, hal...  2.81 us
    ppermute x1, waiting for transfers between devices, swaps(): far = lax.ppermute(far, 'tile', pairs(1))  2.64 us
    all_to_all x1, waiting for transfers between devices, body(): lax.all_to_all(sends, 'member', split_axis=0, concat_axis=0, tiled=True)  2.29 us
  transfers between devices with their start and end apart: 10, of which 2 were waited for; matrix products, arithmetic and copies ran while one was open for 1% of the time, Pallas kernels for 6%

profile of v4, /device:TPU:1, one launch (start us, length us, event | category | flops | bytes accessed | tf_op | source)
XLA Modules:
  0.0 50.3 jit_solution(2977883229004176338)
XLA Ops:
  0.0 1.2 %edges.1 = (f32[104,512]{1,0:T(8,128)S(1)}, f32[104,512]{1,0:T(8,128)S(1)}) custom-call(f32[4,64,512]{2,1,0:T(8,128)} %bitcast.21, f32[64,512]{1,0:T(8,128)} %depth_ref.1, s32[64,512]{1,0:T(8,128)} %mask_ref.1, s32[32,128]{1,0:T(8,128)} %bitcast.23, f32[32,128]{1,0:T(8,128)} %bitcast.25, f32[32,128]{1,0:T(8,128)} %bitcast.27, f32[32,128]{1,0:T(8,128)} %bitcast.29), custom_call_target="tpu_custom_call" | custom-call | tf_op jit(solution)/shard_map/edges/pallas_call | solution.py:387
  1.3 0.1 collective-permute-start
  1.4 4.5 %collective-permute-start.1 = (f32[104,512]{1,0:T(8,128)S(1)}, f32[104,512]{1,0:T(8,128)S(1)}, u32[]{:S(2)}, u32[]{:S(2)}) collective-permute-start(f32[104,512]{1,0:T(8,128)S(1)} %get-tuple-element.17), channel_id=1, source_target_pairs={{1,2},{2,1},{5,6},{6,5},{9,10},{10,9},{13,14},{14,13},{17,18},{18,... | collective-permute-start | bytes 638984 | tf_op jit(solution)/shard_map/ppermute | solution.py:356
  5.9 0.0 copy-start.4
  5.9 0.1 multiply_add_fusion
  6.0 0.7 %copy-done.8 = s32[1,16]{1,0:T(1,128)S(1)} copy-done((s32[1,16]{1,0:T(1,128)S(1)}, s32[1,16]{1,0:T(1,128)}, u32[]{:S(2)}) %copy-start.8) | copy-done | bytes 88
  6.7 0.1 fusion.1
  6.7 2.6 %collective-permute-done.1.far_ref = f32[104,512]{1,0:T(8,128)S(1)} collective-permute-done((f32[104,512]{1,0:T(8,128)S(1)}, f32[104,512]{1,0:T(8,128)S(1)}, u32[]{:S(2)}, u32[]{:S(2)}) %collective-permute-start.1) | collective-permute-done | bytes 213024 | tf_op jit(solution)/shard_map/ppermute | solution.py:356
  9.4 2.8 %forecast.1 = (f32[8,104,128]{2,1,0:T(8,128)}, f32[64,128]{1,0:T(8,128)S(1)}, f32[64,128]{1,0:T(8,128)S(1)}, f32[64,128]{1,0:T(8,128)S(1)}, f32[64,128]{1,0:T(8,...) custom-call(f32[4,64,512]{2,1,0:T(8,128)S(1)} %bitcast.22, ...), custom_call_target="tpu_custom_call" | custom-call | tf_op jit(solution)/shard_map/forecast/pallas_call | solution.py:412
  12.2 6.2 %all-to-all-start = ((f32[8,104,128]{2,1,0:T(8,128)}), f32[8,104,128]{2,1,0:T(8,128)S(1)}, u32[]{:S(2)}, u32[]{:S(2)}) async-start(f32[8,104,128]{2,1,0:T(8,128)} %get-tuple-element.18), calls=%async_computation | async-start | bytes 851968 | tf_op jit(solution)/shard_map/all_to_all | solution.py:432
  18.4 1.5 %collective-permute-start.2 = (f32[64,128]{1,0:T(8,128)S(1)}, f32[64,128]{1,0:T(8,128)S(1)}, u32[]{:S(2)}, u32[]{:S(2)}) collective-permute-start(f32[64,128]{1,0:T(8,128)S(1)} %get-tuple-element.20), channel_id=1, source_target_pairs={{0,4},{4,0},{8,12},{12,8},{16,20},{20,16},{24,28},{28,24},{1,5},{5... | collective-permute-start | bytes 98312 | tf_op jit(solution)/shard_map/ppermute | solution.py:345
  19.9 1.2 %collective-permute-start.3 = (f32[64,128]{1,0:T(8,128)S(1)}, f32[64,128]{1,0:T(8,128)S(1)}, u32[]{:S(2)}, u32[]{:S(2)}) collective-permute-start(f32[64,128]{1,0:T(8,128)S(1)} %get-tuple-element.21), channel_id=1, source_target_pairs={{0,8},{4,12},{8,0},{12,4},{16,24},{20,28},{24,16},{28,20},{1,9},{5... | collective-permute-start | bytes 98312 | tf_op jit(solution)/shard_map/ppermute | solution.py:345
  21.1 0.1 pad_maximum_fusion
  21.2 0.1 collective-permute-start.4
  21.3 2.3 %collective-permute-start.5 = (f32[64,128]{1,0:T(8,128)S(1)}, f32[64,128]{1,0:T(8,128)S(1)}, u32[]{:S(2)}, u32[]{:S(2)}) collective-permute-start(f32[64,128]{1,0:T(8,128)S(1)} %get-tuple-element.23), channel_id=1, source_target_pairs={{0,16},{4,20},{8,24},{12,28},{16,0},{20,4},{24,8},{28,12},{1,17},{... | collective-permute-start | bytes 98312 | tf_op jit(solution)/shard_map/ppermute | solution.py:345
  23.6 1.2 %collective-permute-start.6 = (f32[64,128]{1,0:T(8,128)S(1)}, f32[64,128]{1,0:T(8,128)S(1)}, u32[]{:S(2)}, u32[]{:S(2)}) collective-permute-start(f32[64,128]{1,0:T(8,128)S(1)} %get-tuple-element.24), channel_id=1, source_target_pairs={{0,20},{4,16},{8,28},{12,24},{16,4},{20,0},{24,12},{28,8},{1,21},{... | collective-permute-start | bytes 98312 | tf_op jit(solution)/shard_map/ppermute | solution.py:345
  24.7 3.0 %collective-permute-start.7 = (f32[64,128]{1,0:T(8,128)S(1)}, f32[64,128]{1,0:T(8,128)S(1)}, u32[]{:S(2)}, u32[]{:S(2)}) collective-permute-start(f32[64,128]{1,0:T(8,128)S(1)} %get-tuple-element.25), channel_id=1, source_target_pairs={{0,24},{4,28},{8,16},{12,20},{16,8},{20,12},{24,0},{28,4},{1,25},{... | collective-permute-start | bytes 98312 | tf_op jit(solution)/shard_map/ppermute | solution.py:345
  27.7 0.1 collective-permute-start.8
  27.8 0.1 pad_add_fusion.spot_ref
  27.9 2.3 %all-to-all-done = f32[8,104,128]{2,1,0:T(8,128)S(1)} async-done(((f32[8,104,128]{2,1,0:T(8,128)}), f32[8,104,128]{2,1,0:T(8,128)S(1)}, u32[]{:S(2)}, u32[]{:S(2)}) %all-to-all-start) | async-done | bytes 426016 | tf_op jit(solution)/shard_map/all_to_all | solution.py:432
  30.2 3.0 %weights.1.mix_ref = f32[8,128]{1,0:T(8,128)S(1)} custom-call(f32[832,128]{1,0:T(8,128)S(1)} %bitcast.19, s32[8,128]{1,0:T(8,128)S(1)} %pad_add_fusion.spot_ref, f32[8,128]{1,0:T(8,128)S(1)} %get-tuple-element.33.damp_ref, f32[8,128]{1,0:T(8,128)S(1)} %get-tuple-element.34.live_ref, f32[32,128]{1,0:T(8,128)S(1)} %bitcast.28, f32[32,128]{1,0:T(8,128)S(1)} %bitcast.30, ...), custom_call_target="tpu_custom_call" | custom-call | tf_op jit(solution)/shard_map/weights/pallas_call | solution.py:443
  33.2 0.7 %mix.1 = f32[8,4,8,512]{3,2,1,0:T(8,128)S(1)} custom-call(f32[832,128]{1,0:T(8,128)S(1)} %bitcast.20, f32[8,128]{1,0:T(8,128)S(1)} %weights.1.mix_ref, f32[64,128]{1,0:T(8,128)S(1)} %get-tuple-element.19.refs_0_, f32[64,128]{1,0:T(8,128)S(1)} %collective-permute-done.2.refs_1_, f32[64,128]{1,0:T(8,128)S(1)} %collective-permute-done.3.refs_2_, ...), custom_call_target="tpu_custom_call" | custom-call | tf_op jit(solution)/shard_map/mix/pallas_call | solution.py:461
  33.9 15.6 %all_to_all.10 = f32[8,4,8,512]{3,2,1,0:T(8,128)S(1)} all-to-all(f32[8,4,8,512]{3,2,1,0:T(8,128)S(1)} %mix.1), channel_id=1, replica_groups=mesh['member'=8,'tile'=4] {'member'}, dimensions={0} | all-to-all | bytes 1048576 | tf_op jit(solution)/shard_map/all_to_all | solution.py:470
  49.4 0.8 %copy_bitcast_fusion = f32[1,4,64,512]{3,2,1,0:T(8,128)} fusion(f32[8,4,8,512]{3,2,1,0:T(8,128)S(1)} %all_to_all.10), kind=kLoop, calls=%fused_computation | loop fusion | bytes 1048576 | tf_op jit(solution)/shard_map/reshape | solution.py:471
  (29 shorter events, 0.1 us)
Async XLA Ops:
  0.0 9.4 %copy-start = (f32[1,4,64,512]{3,2,1,0:T(8,128)S(1)}, f32[1,4,64,512]{3,2,1,0:T(8,128)}, u32[]{:S(2)}) copy-start(f32[1,4,64,512]{3,2,1,0:T(8,128)} %param.9) | copy-start | bytes 1572868
  0.0 9.4 %copy-start.1 = (f32[64,512]{1,0:T(8,128)S(1)}, f32[64,512]{1,0:T(8,128)}, u32[]{:S(2)}) copy-start(f32[64,512]{1,0:T(8,128)} %depth_ref.1) | copy-start | bytes 393220
  0.0 9.4 %copy-start.2 = (s32[64,512]{1,0:T(8,128)S(1)}, s32[64,512]{1,0:T(8,128)}, u32[]{:S(2)}) copy-start(s32[64,512]{1,0:T(8,128)} %mask_ref.1) | copy-start | bytes 393220
  1.2 4.6 %copy-start.7 = (s32[1,16,64]{2,1,0:T(8,128)S(1)}, s32[1,16,64]{2,1,0:T(8,128)}, u32[]{:S(2)}) copy-start(s32[1,16,64]{2,1,0:T(8,128)} %param.16) | copy-start | bytes 12292
  1.3 5.5 %collective-permute-start = (f32[104,512]{1,0:T(8,128)S(1)}, f32[104,512]{1,0:T(8,128)S(1)}, u32[]{:S(2)}, u32[]{:S(2)}) collective-permute-start(f32[104,512]{1,0:T(8,128)S(1)} %get-tuple-element.16), channel_id=1, source_target_pairs={{0,1},{2,3},{1,0},{3,2},{4,5},{6,7},{5,4},{7,6},{8,9},{10,11},{9,8... | collective-permute-start | bytes 638984 | tf_op jit(solution)/shard_map/ppermute | solution.py:357
  1.4 8.0 %collective-permute-start.1 = (f32[104,512]{1,0:T(8,128)S(1)}, f32[104,512]{1,0:T(8,128)S(1)}, u32[]{:S(2)}, u32[]{:S(2)}) collective-permute-start(f32[104,512]{1,0:T(8,128)S(1)} %get-tuple-element.17), channel_id=1, source_target_pairs={{1,2},{2,1},{5,6},{6,5},{9,10},{10,9},{13,14},{14,13},{17,18},{18,... | collective-permute-start | bytes 638984 | tf_op jit(solution)/shard_map/ppermute | solution.py:356
  5.9 3.5 %copy-start.4 = (f32[4096]{0:T(1024)S(1)}, f32[4096]{0:T(1024)}, u32[]{:S(2)}) copy-start(f32[4096]{0:T(1024)} %param.15) | copy-start | bytes 49156
  6.0 3.4 %copy-start.3 = (s32[4096]{0:T(1024)S(1)}, s32[4096]{0:T(1024)}, u32[]{:S(2)}) copy-start(s32[4096]{0:T(1024)} %param.12) | copy-start | bytes 49156
  6.0 0.7 %copy-start.8 = (s32[1,16]{1,0:T(1,128)S(1)}, s32[1,16]{1,0:T(1,128)}, u32[]{:S(2)}) copy-start(s32[1,16]{1,0:T(1,128)} %param.17) | copy-start | bytes 196
  12.2 18.0 %all-to-all-start = ((f32[8,104,128]{2,1,0:T(8,128)}), f32[8,104,128]{2,1,0:T(8,128)S(1)}, u32[]{:S(2)}, u32[]{:S(2)}) async-start(f32[8,104,128]{2,1,0:T(8,128)} %get-tuple-element.18), calls=%async_computation | async-start | bytes 851968 | tf_op jit(solution)/shard_map/all_to_all | solution.py:432
  18.4 6.3 %collective-permute-start.2 = (f32[64,128]{1,0:T(8,128)S(1)}, f32[64,128]{1,0:T(8,128)S(1)}, u32[]{:S(2)}, u32[]{:S(2)}) collective-permute-start(f32[64,128]{1,0:T(8,128)S(1)} %get-tuple-element.20), channel_id=1, source_target_pairs={{0,4},{4,0},{8,12},{12,8},{16,20},{20,16},{24,28},{28,24},{1,5},{5... | collective-permute-start | bytes 98312 | tf_op jit(solution)/shard_map/ppermute | solution.py:345
  19.9 7.8 %collective-permute-start.3 = (f32[64,128]{1,0:T(8,128)S(1)}, f32[64,128]{1,0:T(8,128)S(1)}, u32[]{:S(2)}, u32[]{:S(2)}) collective-permute-start(f32[64,128]{1,0:T(8,128)S(1)} %get-tuple-element.21), channel_id=1, source_target_pairs={{0,8},{4,12},{8,0},{12,4},{16,24},{20,28},{24,16},{28,20},{1,9},{5... | collective-permute-start | bytes 98312 | tf_op jit(solution)/shard_map/ppermute | solution.py:345
  21.1 9.1 %copy-start.6 = (f32[4096]{0:T(1024)S(1)}, f32[4096]{0:T(1024)}, u32[]{:S(2)}) copy-start(f32[4096]{0:T(1024)} %param.14) | copy-start | bytes 49156
  21.2 9.0 %copy-start.5 = (f32[4096]{0:T(1024)S(1)}, f32[4096]{0:T(1024)}, u32[]{:S(2)}) copy-start(f32[4096]{0:T(1024)} %param.13) | copy-start | bytes 49156
  21.2 12.0 %collective-permute-start.4 = (f32[64,128]{1,0:T(8,128)S(1)}, f32[64,128]{1,0:T(8,128)S(1)}, u32[]{:S(2)}, u32[]{:S(2)}) collective-permute-start(f32[64,128]{1,0:T(8,128)S(1)} %get-tuple-element.22), channel_id=1, source_target_pairs={{0,12},{4,8},{8,4},{12,0},{16,28},{20,24},{24,20},{28,16},{1,13},{... | collective-permute-start | bytes 98312 | tf_op jit(solution)/shard_map/ppermute | solution.py:345
  21.3 11.9 %collective-permute-start.5 = (f32[64,128]{1,0:T(8,128)S(1)}, f32[64,128]{1,0:T(8,128)S(1)}, u32[]{:S(2)}, u32[]{:S(2)}) collective-permute-start(f32[64,128]{1,0:T(8,128)S(1)} %get-tuple-element.23), channel_id=1, source_target_pairs={{0,16},{4,20},{8,24},{12,28},{16,0},{20,4},{24,8},{28,12},{1,17},{... | collective-permute-start | bytes 98312 | tf_op jit(solution)/shard_map/ppermute | solution.py:345
  23.6 9.6 %collective-permute-start.6 = (f32[64,128]{1,0:T(8,128)S(1)}, f32[64,128]{1,0:T(8,128)S(1)}, u32[]{:S(2)}, u32[]{:S(2)}) collective-permute-start(f32[64,128]{1,0:T(8,128)S(1)} %get-tuple-element.24), channel_id=1, source_target_pairs={{0,20},{4,16},{8,28},{12,24},{16,4},{20,0},{24,12},{28,8},{1,21},{... | collective-permute-start | bytes 98312 | tf_op jit(solution)/shard_map/ppermute | solution.py:345
  24.7 8.4 %collective-permute-start.7 = (f32[64,128]{1,0:T(8,128)S(1)}, f32[64,128]{1,0:T(8,128)S(1)}, u32[]{:S(2)}, u32[]{:S(2)}) collective-permute-start(f32[64,128]{1,0:T(8,128)S(1)} %get-tuple-element.25), channel_id=1, source_target_pairs={{0,24},{4,28},{8,16},{12,20},{16,8},{20,12},{24,0},{28,4},{1,25},{... | collective-permute-start | bytes 98312 | tf_op jit(solution)/shard_map/ppermute | solution.py:345
  27.7 5.5 %collective-permute-start.8 = (f32[64,128]{1,0:T(8,128)S(1)}, f32[64,128]{1,0:T(8,128)S(1)}, u32[]{:S(2)}, u32[]{:S(2)}) collective-permute-start(f32[64,128]{1,0:T(8,128)S(1)} %get-tuple-element.26), channel_id=1, source_target_pairs={{0,28},{4,24},{8,20},{12,16},{16,12},{20,8},{24,4},{28,0},{1,29},{... | collective-permute-start | bytes 98312 | tf_op jit(solution)/shard_map/ppermute | solution.py:345

commit v5 on v4

--- a/solution.py
+++ b/solution.py
@@ -84,7 +84,9 @@
     *refs,
 ):
     members, own_rows, halo, obs_halo = sizes
-    out_ref, rest_refs, scratch = refs[0], refs[1 : members + 1], refs[members + 1 :]
+    half = members // 2
+    out_ref, equiv_ref, across_ref = refs[:3]
+    along_refs, scratch = refs[3 : half + 3], refs[half + 3 :]
     s_ref, u_ref, v_ref, e_ref, h_ref, w_ref, flux_ref, part_ref, cell_win, gain_win = scratch
     even = lax.axis_index("tile") % 2 == 0
     rows, width = depth_ref.shape
@@ -177,6 +179,8 @@
             part, spread, (((1,), (1,)), ((), ())), preferred_element_type=jnp.float32
         )
     equiv = equiv * gain_win[...]
+    equiv_ref[...] = equiv
+    across_ref[across_ref.shape[0] - window :, :] = equiv
 
     me = lax.axis_index("member")
     for j in range(members):
@@ -185,13 +189,16 @@
             for q in range(pieces):
                 target = (i * pieces + q) * own_rows
                 out_ref[j, target : target + own_rows, :] = fields[i][q, source : source + own_rows, :]
-        body_rows = PACKED * pieces * own_rows
-        out_ref[j, body_rows : body_rows + window, :] = equiv
         source = pl.multiple_of(first + (me ^ j) * own_rows, min(own_rows, 8))
         for i in range(PACKED, 4):
             for q in range(pieces):
                 target = ((i - PACKED) * pieces + q) * own_rows
-                rest_refs[j][target : target + own_rows, :] = fields[i][q, pl.ds(source, own_rows), :]
+                block = fields[i][q, pl.ds(source, own_rows), :]
+                if j % 2:
+                    target += j // 2 * (4 - PACKED) * pieces * own_rows
+                    across_ref[target : target + own_rows, :] = block
+                else:
+                    along_refs[j // 2][target : target + own_rows, :] = block
 
 
 def group_columns(left, starts, members):
@@ -205,23 +212,18 @@
     return terms[0]
 
 
-def weight_kernel(
-    sizes,
-    recv_ref,
-    spot_ref,
-    damp_ref,
-    live_ref,
-    value_ref,
-    error_ref,
-    near_ref,
-    far_ref,
-    mix_ref,
-    value_win,
-    error_win,
-):
+def weight_kernel(sizes, four_ref, *refs):
     members, halo = sizes
+    half = members // 2
+    near_refs, refs = refs[: half // 2 - 1], refs[half // 2 - 1 :]
+    spot_ref, damp_ref, live_ref, value_ref, error_ref, near_ref, far_ref = refs[:7]
+    mix_ref, value_win, error_win, equiv_win = refs[7:]
     window = value_win.shape[0]
-    stride = recv_ref.shape[0] // members
+    for i, ref in enumerate((four_ref, *near_refs)):
+        start = ref.shape[0] - 4 * window
+        for place in (2 * i, 2 * i + half, 2 * i + 1, 2 * i + half + 1):
+            equiv_win[place * window : (place + 1) * window, :] = ref[start : start + window, :]
+            start += window
     even = lax.axis_index("tile") % 2 == 0
     window_parts(value_win, value_ref[...], near_ref, far_ref, 6 * halo, 2, even)
     window_parts(error_win, error_ref[...], near_ref, far_ref, 6 * halo, 3, even)
@@ -235,7 +237,7 @@
     value = jnp.zeros((pairs, LANES), jnp.float32)
     error = jnp.zeros((pairs, LANES), jnp.float32)
     for r in range(window):
-        source = recv_ref[pl.ds(stride - window + r, members, stride=stride), :]
+        source = equiv_win[pl.ds(r, members, stride=window), :]
         for i in range(pairs):
             got = jnp.take_along_axis(source, lanes_of[i], axis=1, mode="promise_in_bounds")
             picked[i] = jnp.where(rows_of[i] == r, got, picked[i])
@@ -303,13 +305,12 @@
 
 def mix_kernel(sizes, recv_ref, mix_ref, *refs):
     members, own_rows, pieces = sizes
-    rest_refs, (out_ref, table_ref) = refs[:members], refs[members:]
+    half = members // 2
+    rest_refs, (out_ref, table_ref) = refs[: half + 1], refs[half + 1 :]
+    rest_rows = (4 - PACKED) * pieces * own_rows
     stride = recv_ref.shape[0] // members
     me = lax.axis_index("member")
-    order = (iota((members, members), 0) == iota((members, members), 1) ^ me).astype(jnp.float32)
-    table_ref[...] = lax.dot_general(
-        mix_ref[...], order, (((0,), (0,)), ((), ())), preferred_element_type=jnp.float32, precision=HIGH
-    )
+    table_ref[...] = mix_ref[...].T
     bases = [pl.multiple_of((me ^ d) * stride, 8) for d in range(members)]
 
     def analyse(m, carry):
@@ -325,10 +326,12 @@
                             block = recv_ref[pl.ds(bases[d] + start, own_rows), :]
                         else:
                             start = ((i - PACKED) * pieces + q) * own_rows
-                            block = rest_refs[d][start : start + own_rows, :]
+                            if d >= 2:
+                                start += d % 2 * rest_rows
+                            block = rest_refs[d if d < 2 else d // 2 + 1][start : start + own_rows, :]
                         term = columns[d] * block
                         total = term if total is None else total + term
-                    out_ref[m, i, :, q * LANES : (q + 1) * LANES] = total
+                    out_ref[me ^ m, i, :, q * LANES : (q + 1) * LANES] = total
         return carry
 
     if members <= 8:
@@ -338,12 +341,22 @@
         lax.fori_loop(0, members, analyse, 0)
 
 
-def trade(blocks):
-    members = len(blocks)
-    held = list(blocks)
-    for d in reversed(range(1, members)):
-        held[d] = lax.ppermute(blocks[d], "member", [(i, i ^ d) for i in range(members)])
-    return held
+def trade(block, distance):
+    members = lax.axis_size("member")
+    return lax.ppermute(block, "member", [(i, i ^ distance) for i in range(members)])
+
+
+def trade_blocks(equiv, across, along):
+    half = len(along)
+    size = along[0].shape[0]
+    passed = trade(across, 1)
+    far = [trade(equiv, half + i) for i in range(2)]
+    four = jnp.concatenate([equiv, far[0], passed[half * size :], far[1]], axis=0)
+    pairs = []
+    for i in range(1, half):
+        parts = [along[i], passed[i * size : (i + 1) * size]] + ([four] if 2 * i < half else [])
+        pairs.append(trade(jnp.concatenate(parts, axis=0), 2 * i))
+    return four, pairs[: half // 2 - 1], [along[0], passed, *pairs]
 
 
 def swaps(near, far):
@@ -407,16 +420,20 @@
     near, far = swaps(*edges)
 
     window = (obs_tile + 2 * radius) // LANES
-    packet = PACKED * pieces * own_rows + window
+    packet = PACKED * pieces * own_rows
     grid = (pieces, rows + 2 * halo + 2 * PAD, LANES)
-    sends, *rest = pl.pallas_call(
+    half = members // 2
+    rest_rows = (4 - PACKED) * pieces * own_rows
+    sends, equiv, across, *along = pl.pallas_call(
         functools.partial(forecast_kernel, (members, own_rows, halo, radius)),
         out_shape=[
             pltpu.VMEM((members, packet, LANES), jnp.float32),
+            jax.ShapeDtypeStruct((window, LANES), jnp.float32),
+            jax.ShapeDtypeStruct((half * rest_rows + window, LANES), jnp.float32),
         ]
-        + [jax.ShapeDtypeStruct(((4 - PACKED) * pieces * own_rows, LANES), jnp.float32)] * members,
+        + [jax.ShapeDtypeStruct((rest_rows, LANES), jnp.float32)] * half,
         in_specs=vmem_specs(7),
-        out_specs=vmem_specs(1 + members),
+        out_specs=vmem_specs(3 + half),
         scratch_shapes=[pltpu.VMEM(grid, jnp.float32)] * 8 + [pltpu.VMEM((window, LANES), jnp.float32)] * 2,
         compiler_params=pltpu.CompilerParams(vmem_limit_bytes=24 * 2**20),
         name="forecast",
@@ -430,7 +447,7 @@
         far,
     )
     received = lax.all_to_all(sends, "member", split_axis=0, concat_axis=0, tiled=True)
-    rest = trade(rest)
+    four, near_pairs, rest = trade_blocks(equiv, across, along)
     received = received.reshape(members * packet, LANES)
 
     patch_index = lax.axis_index("member") * per_dev + jnp.arange(per_dev, dtype=jnp.int32)
@@ -443,13 +460,15 @@
     mix = pl.pallas_call(
         functools.partial(weight_kernel, (members, halo)),
         out_shape=jax.ShapeDtypeStruct((members, LANES), jnp.float32),
-        in_specs=vmem_specs(8),
+        in_specs=vmem_specs(8 + len(near_pairs)),
         out_specs=vmem_specs(1)[0],
-        scratch_shapes=[pltpu.VMEM((window, LANES), jnp.float32)] * 2,
+        scratch_shapes=[pltpu.VMEM((window, LANES), jnp.float32)] * 2
+        + [pltpu.VMEM((members * window, LANES), jnp.float32)],
         compiler_params=pltpu.CompilerParams(vmem_limit_bytes=24 * 2**20),
         name="weights",
     )(
-        received,
+        four,
+        *near_pairs,
         spot,
         side_by_side(damp, pairs),
         side_by_side(live.astype(jnp.float32), pairs),
@@ -461,7 +480,7 @@
     analysed = pl.pallas_call(
         functools.partial(mix_kernel, (members, own_rows, pieces)),
         out_shape=jax.ShapeDtypeStruct((members, 4, own_rows, width), jnp.float32),
-        in_specs=vmem_specs(2 + members),
+        in_specs=vmem_specs(3 + half),
         out_specs=vmem_specs(1)[0],
         scratch_shapes=[pltpu.VMEM((LANES, members), jnp.float32)],
         compiler_params=pltpu.CompilerParams(vmem_limit_bytes=24 * 2**20),

time: 50.6 us -> 50.2 us (level)
  waiting for transfers between devices: 4.95 us -> 7.93 us
  starting transfers between devices: 20.1 us -> 18 us
  local copies, waits for them, and re-layouts: 1.54 us -> 0.91 us
    ppermute x7 -> x6, waiting for transfers between devices: 0.02 us -> 4.41 us  [trade(): lax.ppermute(block, 'member', [(i, i ^ distance) for i in range(members)])]
    all_to_all x1, waiting for transfers between devices: 2.29 us -> 0.01 us  [body(): lax.all_to_all(sends, 'member', split_axis=0, concat_axis=0, tiled=True)]
    ppermute x7 -> x6, starting transfers between devices: 9.31 us -> 7.85 us  [trade(): lax.ppermute(block, 'member', [(i, i ^ distance) for i in range(members)])]
    ppermute x1, waiting for transfers between devices: 2.64 us -> 3.52 us  [swaps(): far = lax.ppermute(far, 'tile', pairs(1))]
    unnamed x18 -> x22, local copies, waits for them, and re-layouts: 0.7 us -> 0.05 us
    all_to_all x1, starting transfers between devices: 6.17 us -> 5.55 us  [body(): lax.all_to_all(sends, 'member', split_axis=0, concat_axis=0, tiled=True)]
  transfers between devices with their start and end apart: 10 -> 9, of which waited for: 2 -> 3; matrix products, arithmetic and copies ran while one was open for 1% -> 1% of each run, Pallas kernels for 6% -> 6%
where the time goes in v5:
time: 50.2 us; the launch traced here: 49.9 us
  starting transfers between devices  18 us (36%)
  blocking collectives  15.2 us (30%)
  waiting for transfers between devices  7.93 us (16%)
  Pallas kernels  7.25 us (14%)
  local copies, waits for them, and re-layouts  0.91 us (2%)
    all_to_all x1, blocking collectives, body(): lax.all_to_all(analysed, 'member', split_axis=0, concat_axis=0, tiled=True)  15.2 us
    ppermute x6, starting transfers between devices, trade(): lax.ppermute(block, 'member', [(i, i ^ distance) for i in range(members)])  7.85 us
    all_to_all x1, starting transfers between devices, body(): lax.all_to_all(sends, 'member', split_axis=0, concat_axis=0, tiled=True)  5.55 us
    ppermute x1, starting transfers between devices, swaps(): far = lax.ppermute(far, 'tile', pairs(1))  4.48 us
    ppermute x6, waiting for transfers between devices, trade(): lax.ppermute(block, 'member', [(i, i ^ distance) for i in range(members)])  4.41 us
    ppermute x1, waiting for transfers between devices, swaps(): far = lax.ppermute(far, 'tile', pairs(1))  3.52 us
    pallas_call x1, Pallas kernels, body(): pl.pallas_call(functools.partial(weight_kernel, (members, halo)), out_sha...  2.97 us
    pallas_call x1, Pallas kernels, body(): pl.pallas_call(functools.partial(forecast_kernel, (members, own_rows, hal...  2.6 us
  transfers between devices with their start and end apart: 9, of which 3 were waited for; matrix products, arithmetic and copies ran while one was open for 1% of the time, Pallas kernels for 6%

profile of v5, /device:TPU:1, one launch (start us, length us, event | category | flops | bytes accessed | tf_op | source)
XLA Modules:
  0.0 49.9 jit_solution(11882509768228946476)
XLA Ops:
  0.0 1.2 %edges.1 = (f32[104,512]{1,0:T(8,128)S(1)}, f32[104,512]{1,0:T(8,128)S(1)}) custom-call(f32[4,64,512]{2,1,0:T(8,128)} %bitcast.19, f32[64,512]{1,0:T(8,128)} %depth_ref.1, s32[64,512]{1,0:T(8,128)} %mask_ref.1, s32[32,128]{1,0:T(8,128)} %bitcast.22, f32[32,128]{1,0:T(8,128)} %bitcast.24, f32[32,128]{1,0:T(8,128)} %bitcast.26, f32[32,128]{1,0:T(8,128)} %bitcast.28), custom_call_target="tpu_custom_call" | custom-call | tf_op jit(solution)/shard_map/edges/pallas_call | solution.py:400
  1.3 0.0 copy-start.1
  1.3 0.1 collective-permute-start
  1.4 4.5 %collective-permute-start.1 = (f32[104,512]{1,0:T(8,128)S(1)}, f32[104,512]{1,0:T(8,128)S(1)}, u32[]{:S(2)}, u32[]{:S(2)}) collective-permute-start(f32[104,512]{1,0:T(8,128)S(1)} %get-tuple-element.15), channel_id=1, source_target_pairs={{1,2},{2,1},{5,6},{6,5},{9,10},{10,9},{13,14},{14,13},{17,18},{18,... | collective-permute-start | bytes 638984 | tf_op jit(solution)/shard_map/ppermute | solution.py:369
  5.9 0.1 multiply_add_fusion
  6.0 0.1 fusion.1
  6.1 0.1 pad_maximum_fusion.3
  6.2 0.0 collective-permute-done.near_ref.refs_6_
  6.2 3.5 %collective-permute-done.1.far_ref.refs_7_ = f32[104,512]{1,0:T(8,128)S(1)} collective-permute-done((f32[104,512]{1,0:T(8,128)S(1)}, f32[104,512]{1,0:T(8,128)S(1)}, u32[]{:S(2)}, u32[]{:S(2)}) %collective-permute-start.1) | collective-permute-done | bytes 213024 | tf_op jit(solution)/shard_map/ppermute | solution.py:369
  9.7 2.6 %forecast.1 = (f32[8,64,128]{2,1,0:T(8,128)}, f32[40,128]{1,0:T(8,128)S(1)}, f32[296,128]{1,0:T(8,128)S(1)}, f32[64,128]{1,0:T(8,128)S(1)}, f32[64,128]{1,0:T(8,...) custom-call(f32[4,64,512]{2,1,0:T(8,128)S(1)} %bitcast.20, f32[64,512]{1,0:T(8,128)S(1)} %copy-done.1, ...), custom_call_target="tpu_custom_call" | custom-call | tf_op jit(solution)/shard_map/forecast/pallas_call | solution.py:427
  12.3 1.9 %collective-permute-start.3 = (f32[296,128]{1,0:T(8,128)S(1)}, f32[296,128]{1,0:T(8,128)S(1)}, u32[]{:S(2)}, u32[]{:S(2)}) collective-permute-start(f32[296,128]{1,0:T(8,128)S(1)} %get-tuple-element.18), channel_id=1, source_target_pairs={{0,4},{4,0},{8,12},{12,8},{16,20},{20,16},{24,28},{28,24},{1,5},{5... | collective-permute-start | bytes 454664 | tf_op jit(solution)/shard_map/ppermute | solution.py:346
  14.2 0.1 pad_add_fusion.refs_1_
  14.2 2.3 %collective-permute-start.2 = (f32[40,128]{1,0:T(8,128)S(1)}, f32[40,128]{1,0:T(8,128)S(1)}, u32[]{:S(2)}, u32[]{:S(2)}) collective-permute-start(f32[40,128]{1,0:T(8,128)S(1)} %get-tuple-element.17), channel_id=1, source_target_pairs={{0,16},{4,20},{8,24},{12,28},{16,0},{20,4},{24,8},{28,12},{1,17},{... | collective-permute-start | bytes 61448 | tf_op jit(solution)/shard_map/ppermute | solution.py:346
  16.5 0.0 collective-permute-start.4
  16.5 5.5 %all-to-all-start = ((f32[8,64,128]{2,1,0:T(8,128)}), f32[8,64,128]{2,1,0:T(8,128)S(1)}, u32[]{:S(2)}, u32[]{:S(2)}) async-start(f32[8,64,128]{2,1,0:T(8,128)} %get-tuple-element.16), calls=%async_computation | async-start | bytes 524288 | tf_op jit(solution)/shard_map/all_to_all | solution.py:449
  22.2 1.5 %collective-permute-start.5 = (f32[288,128]{1,0:T(8,128)S(1)}, f32[288,128]{1,0:T(8,128)S(1)}, u32[]{:S(2)}, u32[]{:S(2)}) collective-permute-start(f32[288,128]{1,0:T(8,128)S(1)} %constant_dynamic-update-slice_fusion), channel_id=1, source_target_pairs={{0,8},{4,12},{8,0},{12,4},{16,24},{20,28},{24,16},{28,20},{1,9},{5... | collective-permute-start | bytes 442376 | tf_op jit(solution)/shard_map/ppermute | solution.py:346
  23.7 2.1 %collective-permute-start.7 = (f32[128,128]{1,0:T(8,128)S(1)}, f32[128,128]{1,0:T(8,128)S(1)}, u32[]{:S(2)}, u32[]{:S(2)}) collective-permute-start(f32[128,128]{1,0:T(8,128)S(1)} %pad_maximum_fusion.2), channel_id=1, source_target_pairs={{0,24},{4,28},{8,16},{12,20},{16,8},{20,12},{24,0},{28,4},{1,25},{... | collective-permute-start | bytes 196616 | tf_op jit(solution)/shard_map/ppermute | solution.py:346
  25.8 0.1 collective-permute-start.6
  25.9 3.3 %collective-permute-done.5.refs_0_.refs_2_ = f32[288,128]{1,0:T(8,128)S(1)} collective-permute-done((f32[288,128]{1,0:T(8,128)S(1)}, f32[288,128]{1,0:T(8,128)S(1)}, u32[]{:S(2)}, u32[]{:S(2)}) %collective-permute-start.5) | collective-permute-done | bytes 147488 | tf_op jit(solution)/shard_map/ppermute | solution.py:346
  29.2 3.0 %weights.1.mix_ref = f32[8,128]{1,0:T(8,128)S(1)} custom-call(f32[160,128]{1,0:T(8,128)S(1)} %pad_maximum_fusion.four_ref, f32[288,128]{1,0:T(8,128)S(1)} %collective-permute-done.5.refs_0_.refs_2_, s32[8,128]{1,0:T(8,128)S(1)} %pad_add_fusion.refs_1_, f32[8,128]{1,0:T(8,128)S(1)} %get-tuple-element.34.refs_2_, f32[8,128]{1,0:T(8,128)S(1)} %get-tuple-element.35.refs_3_, ...), custom_call_target="tpu_custom_call" | custom-call | tf_op jit(solution)/shard_map/weights/pallas_call | solution.py:460
  32.2 1.1 %collective-permute-done.6.refs_3_ = f32[128,128]{1,0:T(8,128)S(1)} collective-permute-done((f32[128,128]{1,0:T(8,128)S(1)}, f32[128,128]{1,0:T(8,128)S(1)}, u32[]{:S(2)}, u32[]{:S(2)}) %collective-permute-start.6) | collective-permute-done | bytes 65568 | tf_op jit(solution)/shard_map/ppermute | solution.py:346
  33.3 0.5 mix.1
  33.8 15.2 %all_to_all.10 = f32[8,4,8,512]{3,2,1,0:T(8,128)S(1)} all-to-all(f32[8,4,8,512]{3,2,1,0:T(8,128)S(1)} %mix.1), channel_id=1, replica_groups=mesh['member'=8,'tile'=4] {'member'}, dimensions={0} | all-to-all | bytes 1048576 | tf_op jit(solution)/shard_map/all_to_all | solution.py:489
  49.0 0.8 %copy_bitcast_fusion = f32[1,4,64,512]{3,2,1,0:T(8,128)} fusion(f32[8,4,8,512]{3,2,1,0:T(8,128)S(1)} %all_to_all.10), kind=kLoop, calls=%fused_computation | loop fusion | bytes 1048576 | tf_op jit(solution)/shard_map/reshape | solution.py:490
  (36 shorter events, 0.1 us)
Async XLA Ops:
  0.0 9.7 %copy-start = (f32[1,4,64,512]{3,2,1,0:T(8,128)S(1)}, f32[1,4,64,512]{3,2,1,0:T(8,128)}, u32[]{:S(2)}) copy-start(f32[1,4,64,512]{3,2,1,0:T(8,128)} %param.9) | copy-start | bytes 1572868
  0.0 5.9 %copy-start.7 = (s32[1,16,64]{2,1,0:T(8,128)S(1)}, s32[1,16,64]{2,1,0:T(8,128)}, u32[]{:S(2)}) copy-start(s32[1,16,64]{2,1,0:T(8,128)} %param.16) | copy-start | bytes 12292
  0.0 6.0 %copy-start.8 = (s32[1,16]{1,0:T(1,128)S(1)}, s32[1,16]{1,0:T(1,128)}, u32[]{:S(2)}) copy-start(s32[1,16]{1,0:T(1,128)} %param.17) | copy-start | bytes 196
  0.0 9.7 %copy-start.2 = (s32[64,512]{1,0:T(8,128)S(1)}, s32[64,512]{1,0:T(8,128)}, u32[]{:S(2)}) copy-start(s32[64,512]{1,0:T(8,128)} %mask_ref.1) | copy-start | bytes 393220
  0.0 9.7 %copy-start.3 = (s32[4096]{0:T(1024)S(1)}, s32[4096]{0:T(1024)}, u32[]{:S(2)}) copy-start(s32[4096]{0:T(1024)} %param.12) | copy-start | bytes 49156
  0.0 9.7 %copy-start.4 = (f32[4096]{0:T(1024)S(1)}, f32[4096]{0:T(1024)}, u32[]{:S(2)}) copy-start(f32[4096]{0:T(1024)} %param.15) | copy-start | bytes 49156
  1.3 8.4 %copy-start.1 = (f32[64,512]{1,0:T(8,128)S(1)}, f32[64,512]{1,0:T(8,128)}, u32[]{:S(2)}) copy-start(f32[64,512]{1,0:T(8,128)} %depth_ref.1) | copy-start | bytes 393220
  1.3 4.9 %collective-permute-start = (f32[104,512]{1,0:T(8,128)S(1)}, f32[104,512]{1,0:T(8,128)S(1)}, u32[]{:S(2)}, u32[]{:S(2)}) collective-permute-start(f32[104,512]{1,0:T(8,128)S(1)} %get-tuple-element.14), channel_id=1, source_target_pairs={{0,1},{2,3},{1,0},{3,2},{4,5},{6,7},{5,4},{7,6},{8,9},{10,11},{9,8... | collective-permute-start | bytes 638984 | tf_op jit(solution)/shard_map/ppermute | solution.py:370
  1.4 8.3 %collective-permute-start.1 = (f32[104,512]{1,0:T(8,128)S(1)}, f32[104,512]{1,0:T(8,128)S(1)}, u32[]{:S(2)}, u32[]{:S(2)}) collective-permute-start(f32[104,512]{1,0:T(8,128)S(1)} %get-tuple-element.15), channel_id=1, source_target_pairs={{1,2},{2,1},{5,6},{6,5},{9,10},{10,9},{13,14},{14,13},{17,18},{18,... | collective-permute-start | bytes 638984 | tf_op jit(solution)/shard_map/ppermute | solution.py:369
  12.3 9.8 %collective-permute-start.3 = (f32[296,128]{1,0:T(8,128)S(1)}, f32[296,128]{1,0:T(8,128)S(1)}, u32[]{:S(2)}, u32[]{:S(2)}) collective-permute-start(f32[296,128]{1,0:T(8,128)S(1)} %get-tuple-element.18), channel_id=1, source_target_pairs={{0,4},{4,0},{8,12},{12,8},{16,20},{20,16},{24,28},{28,24},{1,5},{5... | collective-permute-start | bytes 454664 | tf_op jit(solution)/shard_map/ppermute | solution.py:346
  14.2 7.9 %collective-permute-start.2 = (f32[40,128]{1,0:T(8,128)S(1)}, f32[40,128]{1,0:T(8,128)S(1)}, u32[]{:S(2)}, u32[]{:S(2)}) collective-permute-start(f32[40,128]{1,0:T(8,128)S(1)} %get-tuple-element.17), channel_id=1, source_target_pairs={{0,16},{4,20},{8,24},{12,28},{16,0},{20,4},{24,8},{28,12},{1,17},{... | collective-permute-start | bytes 61448 | tf_op jit(solution)/shard_map/ppermute | solution.py:346
  16.5 5.6 %collective-permute-start.4 = (f32[40,128]{1,0:T(8,128)S(1)}, f32[40,128]{1,0:T(8,128)S(1)}, u32[]{:S(2)}, u32[]{:S(2)}) collective-permute-start(f32[40,128]{1,0:T(8,128)S(1)} %get-tuple-element.17), channel_id=1, source_target_pairs={{0,20},{4,16},{8,28},{12,24},{16,4},{20,0},{24,12},{28,8},{1,21},{... | collective-permute-start | bytes 61448 | tf_op jit(solution)/shard_map/ppermute | solution.py:346
  16.5 16.8 %all-to-all-start = ((f32[8,64,128]{2,1,0:T(8,128)}), f32[8,64,128]{2,1,0:T(8,128)S(1)}, u32[]{:S(2)}, u32[]{:S(2)}) async-start(f32[8,64,128]{2,1,0:T(8,128)} %get-tuple-element.16), calls=%async_computation | async-start | bytes 524288 | tf_op jit(solution)/shard_map/all_to_all | solution.py:449
  22.2 7.0 %collective-permute-start.5 = (f32[288,128]{1,0:T(8,128)S(1)}, f32[288,128]{1,0:T(8,128)S(1)}, u32[]{:S(2)}, u32[]{:S(2)}) collective-permute-start(f32[288,128]{1,0:T(8,128)S(1)} %constant_dynamic-update-slice_fusion), channel_id=1, source_target_pairs={{0,8},{4,12},{8,0},{12,4},{16,24},{20,28},{24,16},{28,20},{1,9},{5... | collective-permute-start | bytes 442376 | tf_op jit(solution)/shard_map/ppermute | solution.py:346
  23.7 8.4 %collective-permute-start.7 = (f32[128,128]{1,0:T(8,128)S(1)}, f32[128,128]{1,0:T(8,128)S(1)}, u32[]{:S(2)}, u32[]{:S(2)}) collective-permute-start(f32[128,128]{1,0:T(8,128)S(1)} %pad_maximum_fusion.2), channel_id=1, source_target_pairs={{0,24},{4,28},{8,16},{12,20},{16,8},{20,12},{24,0},{28,4},{1,25},{... | collective-permute-start | bytes 196616 | tf_op jit(solution)/shard_map/ppermute | solution.py:346
  25.8 7.5 %collective-permute-start.6 = (f32[128,128]{1,0:T(8,128)S(1)}, f32[128,128]{1,0:T(8,128)S(1)}, u32[]{:S(2)}, u32[]{:S(2)}) collective-permute-start(f32[128,128]{1,0:T(8,128)S(1)} %pad_maximum_fusion.1), channel_id=1, source_target_pairs={{0,16},{4,20},{8,24},{12,28},{16,0},{20,4},{24,8},{28,12},{1,17},{... | collective-permute-start | bytes 196616 | tf_op jit(solution)/shard_map/ppermute | solution.py:346
  25.9 3.3 %copy-start.5 = (f32[4096]{0:T(1024)S(1)}, f32[4096]{0:T(1024)}, u32[]{:S(2)}) copy-start(f32[4096]{0:T(1024)} %param.13) | copy-start | bytes 49156
  25.9 3.3 %copy-start.6 = (f32[4096]{0:T(1024)S(1)}, f32[4096]{0:T(1024)}, u32[]{:S(2)}) copy-start(f32[4096]{0:T(1024)} %param.14) | copy-start | bytes 49156

commit v6 on v5

--- a/solution.py
+++ b/solution.py
@@ -22,7 +22,7 @@
 HIGH = lax.Precision.HIGHEST
 
 PAD = 8
-PACKED = 2
+PACKED = 3
 
 
 def iota(shape, dim):
@@ -178,9 +178,7 @@
         equiv = equiv + lax.dot_general(
             part, spread, (((1,), (1,)), ((), ())), preferred_element_type=jnp.float32
         )
-    equiv = equiv * gain_win[...]
-    equiv_ref[...] = equiv
-    across_ref[across_ref.shape[0] - window :, :] = equiv
+    equiv_ref[...] = equiv * gain_win[...]
 
     me = lax.axis_index("member")
     for j in range(members):
@@ -349,9 +347,10 @@
 def trade_blocks(equiv, across, along):
     half = len(along)
     size = along[0].shape[0]
+    far_equiv = trade(equiv, half)
     passed = trade(across, 1)
-    far = [trade(equiv, half + i) for i in range(2)]
-    four = jnp.concatenate([equiv, far[0], passed[half * size :], far[1]], axis=0)
+    two = jnp.concatenate([equiv, far_equiv], axis=0)
+    four = jnp.concatenate([two, trade(two, 1)], axis=0)
     pairs = []
     for i in range(1, half):
         parts = [along[i], passed[i * size : (i + 1) * size]] + ([four] if 2 * i < half else [])
@@ -429,7 +428,7 @@
         out_shape=[
             pltpu.VMEM((members, packet, LANES), jnp.float32),
             jax.ShapeDtypeStruct((window, LANES), jnp.float32),
-            jax.ShapeDtypeStruct((half * rest_rows + window, LANES), jnp.float32),
+            jax.ShapeDtypeStruct((half * rest_rows, LANES), jnp.float32),
         ]
         + [jax.ShapeDtypeStruct((rest_rows, LANES), jnp.float32)] * half,
         in_specs=vmem_specs(7),

time: 50.2 us -> 51.7 us (1.030)
  blocking collectives: 15.2 us -> 18 us
  starting transfers between devices: 18 us -> 16.9 us
    all_to_all x1, blocking collectives: 15.2 us -> 18 us  [body(): lax.all_to_all(analysed, 'member', split_axis=0, concat_axis=0, tiled=True)]
    all_to_all x1, starting transfers between devices: 5.55 us -> 3.45 us  [body(): lax.all_to_all(sends, 'member', split_axis=0, concat_axis=0, tiled=True)]
    ppermute x6, starting transfers between devices: 7.85 us -> 8.9 us  [trade(): lax.ppermute(block, 'member', [(i, i ^ distance) for i in range(members)])]
where the time goes in v6:
time: 51.7 us; the launch traced here: 51.1 us
  blocking collectives  18 us (35%)
  starting transfers between devices  16.9 us (33%)
  waiting for transfers between devices  7.51 us (15%)
  Pallas kernels  7.29 us (14%)
  local copies, waits for them, and re-layouts  0.9 us (2%)
    all_to_all x1, blocking collectives, body(): lax.all_to_all(analysed, 'member', split_axis=0, concat_axis=0, tiled=True)  18 us
    ppermute x6, starting transfers between devices, trade(): lax.ppermute(block, 'member', [(i, i ^ distance) for i in range(members)])  8.9 us
    ppermute x1, starting transfers between devices, swaps(): far = lax.ppermute(far, 'tile', pairs(1))  4.48 us
    ppermute x6, waiting for transfers between devices, trade(): lax.ppermute(block, 'member', [(i, i ^ distance) for i in range(members)])  4.36 us
    all_to_all x1, starting transfers between devices, body(): lax.all_to_all(sends, 'member', split_axis=0, concat_axis=0, tiled=True)  3.45 us
    ppermute x1, waiting for transfers between devices, swaps(): far = lax.ppermute(far, 'tile', pairs(1))  3.14 us
    pallas_call x1, Pallas kernels, body(): pl.pallas_call(functools.partial(weight_kernel, (members, halo)), out_sha...  2.97 us
    pallas_call x1, Pallas kernels, body(): pl.pallas_call(functools.partial(forecast_kernel, (members, own_rows, hal...  2.64 us
  transfers between devices with their start and end apart: 9, of which 3 were waited for; matrix products, arithmetic and copies ran while one was open for 1% of the time, Pallas kernels for 6%

profile of v6, /device:TPU:1, one launch (start us, length us, event | category | flops | bytes accessed | tf_op | source)
XLA Modules:
  0.0 51.1 jit_solution(3675651345387976546)
XLA Ops:
  0.0 1.2 %edges.1 = (f32[104,512]{1,0:T(8,128)S(1)}, f32[104,512]{1,0:T(8,128)S(1)}) custom-call(f32[4,64,512]{2,1,0:T(8,128)} %bitcast.19, f32[64,512]{1,0:T(8,128)} %depth_ref.1, s32[64,512]{1,0:T(8,128)} %mask_ref.1, s32[32,128]{1,0:T(8,128)} %bitcast.22, f32[32,128]{1,0:T(8,128)} %bitcast.24, f32[32,128]{1,0:T(8,128)} %bitcast.26, f32[32,128]{1,0:T(8,128)} %bitcast.28), custom_call_target="tpu_custom_call" | custom-call | tf_op jit(solution)/shard_map/edges/pallas_call | solution.py:399
  1.2 0.0 copy-start.1
  1.3 0.1 collective-permute-start
  1.4 4.5 %collective-permute-start.1 = (f32[104,512]{1,0:T(8,128)S(1)}, f32[104,512]{1,0:T(8,128)S(1)}, u32[]{:S(2)}, u32[]{:S(2)}) collective-permute-start(f32[104,512]{1,0:T(8,128)S(1)} %get-tuple-element.15), channel_id=1, source_target_pairs={{1,2},{2,1},{5,6},{6,5},{9,10},{10,9},{13,14},{14,13},{17,18},{18,... | collective-permute-start | bytes 638984 | tf_op jit(solution)/shard_map/ppermute | solution.py:368
  5.9 0.1 multiply_add_fusion
  6.0 0.1 fusion.1
  6.1 0.1 pad_add_fusion.refs_1_
  6.1 0.1 pad_maximum_fusion.4
  6.2 0.0 collective-permute-done.near_ref.refs_6_
  6.2 3.1 %collective-permute-done.1.far_ref.refs_7_ = f32[104,512]{1,0:T(8,128)S(1)} collective-permute-done((f32[104,512]{1,0:T(8,128)S(1)}, f32[104,512]{1,0:T(8,128)S(1)}, u32[]{:S(2)}, u32[]{:S(2)}) %collective-permute-start.1) | collective-permute-done | bytes 213024 | tf_op jit(solution)/shard_map/ppermute | solution.py:368
  9.4 2.6 %forecast.1 = (f32[8,96,128]{2,1,0:T(8,128)}, f32[40,128]{1,0:T(8,128)S(1)}, f32[128,128]{1,0:T(8,128)S(1)}, f32[32,128]{1,0:T(8,128)S(1)}, f32[32,128]{1,0:T(8,...) custom-call(f32[4,64,512]{2,1,0:T(8,128)S(1)} %bitcast.20, f32[64,512]{1,0:T(8,128)S(1)} %copy-done.1, ...), custom_call_target="tpu_custom_call" | custom-call | tf_op jit(solution)/shard_map/forecast/pallas_call | solution.py:426
  12.0 1.9 %collective-permute-start.4 = (f32[128,128]{1,0:T(8,128)S(1)}, f32[128,128]{1,0:T(8,128)S(1)}, u32[]{:S(2)}, u32[]{:S(2)}) collective-permute-start(f32[128,128]{1,0:T(8,128)S(1)} %get-tuple-element.19), channel_id=1, source_target_pairs={{0,4},{4,0},{8,12},{12,8},{16,20},{20,16},{24,28},{28,24},{1,5},{5... | collective-permute-start | bytes 196616 | tf_op jit(solution)/shard_map/ppermute | solution.py:344
  13.9 2.3 %collective-permute-start.2 = (f32[40,128]{1,0:T(8,128)S(1)}, f32[40,128]{1,0:T(8,128)S(1)}, u32[]{:S(2)}, u32[]{:S(2)}) collective-permute-start(f32[40,128]{1,0:T(8,128)S(1)} %get-tuple-element.17), channel_id=1, source_target_pairs={{0,16},{4,20},{8,24},{12,28},{16,0},{20,4},{24,8},{28,12},{1,17},{... | collective-permute-start | bytes 61448 | tf_op jit(solution)/shard_map/ppermute | solution.py:344
  16.2 3.5 %all-to-all-start = ((f32[8,96,128]{2,1,0:T(8,128)}), f32[8,96,128]{2,1,0:T(8,128)S(1)}, u32[]{:S(2)}, u32[]{:S(2)}) async-start(f32[8,96,128]{2,1,0:T(8,128)} %get-tuple-element.16), calls=%async_computation | async-start | bytes 786432 | tf_op jit(solution)/shard_map/all_to_all | solution.py:448
  19.7 1.4 %collective-permute-start.3 = (f32[80,128]{1,0:T(8,128)S(1)}, f32[80,128]{1,0:T(8,128)S(1)}, u32[]{:S(2)}, u32[]{:S(2)}) collective-permute-start(f32[80,128]{1,0:T(8,128)S(1)} %pad_maximum_fusion.1), channel_id=1, source_target_pairs={{0,4},{4,0},{8,12},{12,8},{16,20},{20,16},{24,28},{28,24},{1,5},{5... | collective-permute-start | bytes 122888 | tf_op jit(solution)/shard_map/ppermute | solution.py:344
  21.1 2.8 %collective-permute-done.3 = f32[80,128]{1,0:T(8,128)S(1)} collective-permute-done((f32[80,128]{1,0:T(8,128)S(1)}, f32[80,128]{1,0:T(8,128)S(1)}, u32[]{:S(2)}, u32[]{:S(2)}) %collective-permute-start.3) | collective-permute-done | bytes 40992 | tf_op jit(solution)/shard_map/ppermute | solution.py:344
  24.0 0.7 %collective-permute-start.5 = (f32[224,128]{1,0:T(8,128)S(1)}, f32[224,128]{1,0:T(8,128)S(1)}, u32[]{:S(2)}, u32[]{:S(2)}) collective-permute-start(f32[224,128]{1,0:T(8,128)S(1)} %constant_dynamic-update-slice_fusion), channel_id=1, source_target_pairs={{0,8},{4,12},{8,0},{12,4},{16,24},{20,28},{24,16},{28,20},{1,9},{5... | collective-permute-start | bytes 344072 | tf_op jit(solution)/shard_map/ppermute | solution.py:344
  24.6 2.6 %collective-permute-start.7 = (f32[64,128]{1,0:T(8,128)S(1)}, f32[64,128]{1,0:T(8,128)S(1)}, u32[]{:S(2)}, u32[]{:S(2)}) collective-permute-start(f32[64,128]{1,0:T(8,128)S(1)} %pad_maximum_fusion.3), channel_id=1, source_target_pairs={{0,24},{4,28},{8,16},{12,20},{16,8},{20,12},{24,0},{28,4},{1,25},{... | collective-permute-start | bytes 98312 | tf_op jit(solution)/shard_map/ppermute | solution.py:344
  27.2 0.1 collective-permute-start.6
  27.3 1.5 %collective-permute-done.5.refs_0_.refs_2_ = f32[224,128]{1,0:T(8,128)S(1)} collective-permute-done((f32[224,128]{1,0:T(8,128)S(1)}, f32[224,128]{1,0:T(8,128)S(1)}, u32[]{:S(2)}, u32[]{:S(2)}) %collective-permute-start.5) | collective-permute-done | bytes 114720 | tf_op jit(solution)/shard_map/ppermute | solution.py:344
  28.9 3.0 %weights.1.mix_ref = f32[8,128]{1,0:T(8,128)S(1)} custom-call(f32[160,128]{1,0:T(8,128)S(1)} %pad_maximum_fusion.four_ref, f32[224,128]{1,0:T(8,128)S(1)} %collective-permute-done.5.refs_0_.refs_2_, s32[8,128]{1,0:T(8,128)S(1)} %pad_add_fusion.refs_1_, f32[8,128]{1,0:T(8,128)S(1)} %get-tuple-element.32.refs_2_, f32[8,128]{1,0:T(8,128)S(1)} %get-tuple-element.33.refs_3_, ...), custom_call_target="tpu_custom_call" | custom-call | tf_op jit(solution)/shard_map/weights/pallas_call | solution.py:459
  31.9 0.5 mix.1
  32.3 18.0 %all_to_all.10 = f32[8,4,8,512]{3,2,1,0:T(8,128)S(1)} all-to-all(f32[8,4,8,512]{3,2,1,0:T(8,128)S(1)} %mix.1), channel_id=1, replica_groups=mesh['member'=8,'tile'=4] {'member'}, dimensions={0} | all-to-all | bytes 1048576 | tf_op jit(solution)/shard_map/all_to_all | solution.py:488
  50.3 0.8 %copy_bitcast_fusion = f32[1,4,64,512]{3,2,1,0:T(8,128)} fusion(f32[8,4,8,512]{3,2,1,0:T(8,128)S(1)} %all_to_all.10), kind=kLoop, calls=%fused_computation | loop fusion | bytes 1048576 | tf_op jit(solution)/shard_map/reshape | solution.py:489
  (36 shorter events, 0.1 us)
Async XLA Ops:
  0.0 9.4 %copy-start = (f32[1,4,64,512]{3,2,1,0:T(8,128)S(1)}, f32[1,4,64,512]{3,2,1,0:T(8,128)}, u32[]{:S(2)}) copy-start(f32[1,4,64,512]{3,2,1,0:T(8,128)} %param.9) | copy-start | bytes 1572868
  0.0 5.9 %copy-start.7 = (s32[1,16,64]{2,1,0:T(8,128)S(1)}, s32[1,16,64]{2,1,0:T(8,128)}, u32[]{:S(2)}) copy-start(s32[1,16,64]{2,1,0:T(8,128)} %param.16) | copy-start | bytes 12292
  0.0 6.0 %copy-start.8 = (s32[1,16]{1,0:T(1,128)S(1)}, s32[1,16]{1,0:T(1,128)}, u32[]{:S(2)}) copy-start(s32[1,16]{1,0:T(1,128)} %param.17) | copy-start | bytes 196
  0.0 9.4 %copy-start.2 = (s32[64,512]{1,0:T(8,128)S(1)}, s32[64,512]{1,0:T(8,128)}, u32[]{:S(2)}) copy-start(s32[64,512]{1,0:T(8,128)} %mask_ref.1) | copy-start | bytes 393220
  0.0 9.4 %copy-start.4 = (f32[4096]{0:T(1024)S(1)}, f32[4096]{0:T(1024)}, u32[]{:S(2)}) copy-start(f32[4096]{0:T(1024)} %param.15) | copy-start | bytes 49156
  1.2 8.1 %copy-start.1 = (f32[64,512]{1,0:T(8,128)S(1)}, f32[64,512]{1,0:T(8,128)}, u32[]{:S(2)}) copy-start(f32[64,512]{1,0:T(8,128)} %depth_ref.1) | copy-start | bytes 393220
  1.3 5.0 %collective-permute-start = (f32[104,512]{1,0:T(8,128)S(1)}, f32[104,512]{1,0:T(8,128)S(1)}, u32[]{:S(2)}, u32[]{:S(2)}) collective-permute-start(f32[104,512]{1,0:T(8,128)S(1)} %get-tuple-element.14), channel_id=1, source_target_pairs={{0,1},{2,3},{1,0},{3,2},{4,5},{6,7},{5,4},{7,6},{8,9},{10,11},{9,8... | collective-permute-start | bytes 638984 | tf_op jit(solution)/shard_map/ppermute | solution.py:369
  1.4 8.0 %collective-permute-start.1 = (f32[104,512]{1,0:T(8,128)S(1)}, f32[104,512]{1,0:T(8,128)S(1)}, u32[]{:S(2)}, u32[]{:S(2)}) collective-permute-start(f32[104,512]{1,0:T(8,128)S(1)} %get-tuple-element.15), channel_id=1, source_target_pairs={{1,2},{2,1},{5,6},{6,5},{9,10},{10,9},{13,14},{14,13},{17,18},{18,... | collective-permute-start | bytes 638984 | tf_op jit(solution)/shard_map/ppermute | solution.py:368
  6.1 3.2 %copy-start.3 = (s32[4096]{0:T(1024)S(1)}, s32[4096]{0:T(1024)}, u32[]{:S(2)}) copy-start(s32[4096]{0:T(1024)} %param.12) | copy-start | bytes 49156
  12.0 9.1 %collective-permute-start.4 = (f32[128,128]{1,0:T(8,128)S(1)}, f32[128,128]{1,0:T(8,128)S(1)}, u32[]{:S(2)}, u32[]{:S(2)}) collective-permute-start(f32[128,128]{1,0:T(8,128)S(1)} %get-tuple-element.19), channel_id=1, source_target_pairs={{0,4},{4,0},{8,12},{12,8},{16,20},{20,16},{24,28},{28,24},{1,5},{5... | collective-permute-start | bytes 196616 | tf_op jit(solution)/shard_map/ppermute | solution.py:344
  13.9 5.8 %collective-permute-start.2 = (f32[40,128]{1,0:T(8,128)S(1)}, f32[40,128]{1,0:T(8,128)S(1)}, u32[]{:S(2)}, u32[]{:S(2)}) collective-permute-start(f32[40,128]{1,0:T(8,128)S(1)} %get-tuple-element.17), channel_id=1, source_target_pairs={{0,16},{4,20},{8,24},{12,28},{16,0},{20,4},{24,8},{28,12},{1,17},{... | collective-permute-start | bytes 61448 | tf_op jit(solution)/shard_map/ppermute | solution.py:344
  16.2 15.6 %all-to-all-start = ((f32[8,96,128]{2,1,0:T(8,128)}), f32[8,96,128]{2,1,0:T(8,128)S(1)}, u32[]{:S(2)}, u32[]{:S(2)}) async-start(f32[8,96,128]{2,1,0:T(8,128)} %get-tuple-element.16), calls=%async_computation | async-start | bytes 786432 | tf_op jit(solution)/shard_map/all_to_all | solution.py:448
  19.7 4.3 %collective-permute-start.3 = (f32[80,128]{1,0:T(8,128)S(1)}, f32[80,128]{1,0:T(8,128)S(1)}, u32[]{:S(2)}, u32[]{:S(2)}) collective-permute-start(f32[80,128]{1,0:T(8,128)S(1)} %pad_maximum_fusion.1), channel_id=1, source_target_pairs={{0,4},{4,0},{8,12},{12,8},{16,20},{20,16},{24,28},{28,24},{1,5},{5... | collective-permute-start | bytes 122888 | tf_op jit(solution)/shard_map/ppermute | solution.py:344
  24.0 4.9 %collective-permute-start.5 = (f32[224,128]{1,0:T(8,128)S(1)}, f32[224,128]{1,0:T(8,128)S(1)}, u32[]{:S(2)}, u32[]{:S(2)}) collective-permute-start(f32[224,128]{1,0:T(8,128)S(1)} %constant_dynamic-update-slice_fusion), channel_id=1, source_target_pairs={{0,8},{4,12},{8,0},{12,4},{16,24},{20,28},{24,16},{28,20},{1,9},{5... | collective-permute-start | bytes 344072 | tf_op jit(solution)/shard_map/ppermute | solution.py:344
  24.6 7.2 %collective-permute-start.7 = (f32[64,128]{1,0:T(8,128)S(1)}, f32[64,128]{1,0:T(8,128)S(1)}, u32[]{:S(2)}, u32[]{:S(2)}) collective-permute-start(f32[64,128]{1,0:T(8,128)S(1)} %pad_maximum_fusion.3), channel_id=1, source_target_pairs={{0,24},{4,28},{8,16},{12,20},{16,8},{20,12},{24,0},{28,4},{1,25},{... | collective-permute-start | bytes 98312 | tf_op jit(solution)/shard_map/ppermute | solution.py:344
  27.2 1.6 %copy-start.5 = (f32[4096]{0:T(1024)S(1)}, f32[4096]{0:T(1024)}, u32[]{:S(2)}) copy-start(f32[4096]{0:T(1024)} %param.13) | copy-start | bytes 49156
  27.2 1.6 %copy-start.6 = (f32[4096]{0:T(1024)S(1)}, f32[4096]{0:T(1024)}, u32[]{:S(2)}) copy-start(f32[4096]{0:T(1024)} %param.14) | copy-start | bytes 49156
  27.2 4.6 %collective-permute-start.6 = (f32[64,128]{1,0:T(8,128)S(1)}, f32[64,128]{1,0:T(8,128)S(1)}, u32[]{:S(2)}, u32[]{:S(2)}) collective-permute-start(f32[64,128]{1,0:T(8,128)S(1)} %pad_maximum_fusion.2), channel_id=1, source_target_pairs={{0,16},{4,20},{8,24},{12,28},{16,0},{20,4},{24,8},{28,12},{1,17},{... | collective-permute-start | bytes 98312 | tf_op jit(solution)/shard_map/ppermute | solution.py:344

commit v7 on v5

--- a/solution.py
+++ b/solution.py
@@ -106,6 +106,8 @@
             if i < 4:
                 field[q, own, :] = state_ref[i, :, lanes]
         h_ref[q, own, :] = depth_ref[:, lanes]
+        s_ref[q, PAD : PAD + total, :] *= PRESSURE
+        h_ref[q, PAD : PAD + total, :] *= PRESSURE * DIVERGE
         w_ref[q, own, :] = mask_ref[:, lanes].astype(jnp.float32)
         for field in (s_ref, e_ref, flux_ref):
             field[q, 0:PAD, :] = edge
@@ -122,33 +124,39 @@
             for q in range(pieces)
         ]
 
+    outer = (halo - obs_halo * CELLS_PER_OBS // width) // 8
     for step in range(STEPS):
+        skip, skip_energy = (outer, halo // 8) if step == STEPS - 1 else (0, 0)
         for block in range(total // 8):
             r = PAD + 8 * block
             here, below, above = pl.ds(r, 8), pl.ds(r + 1, 8), pl.ds(r - 1, 8)
+            inside = skip <= block < total // 8 - skip
             s = [s_ref[q, here, :] for q in range(pieces)]
-            slope = across(s)
+            slope = across(s) if inside else None
             flux = []
             for q in range(pieces):
                 w, h = w_ref[q, here, :], h_ref[q, here, :]
-                u = w * (FRICTION * u_ref[q, here, :] - PRESSURE * (s_ref[q, below, :] - s_ref[q, above, :]))
+                u = w * (FRICTION * u_ref[q, here, :] - (s_ref[q, below, :] - s_ref[q, above, :]))
                 u_ref[q, here, :] = u
                 flux_ref[q, here, :] = h * u
-                v = w * (FRICTION * v_ref[q, here, :] - PRESSURE * slope[q])
-                v_ref[q, here, :] = v
-                flux.append(h * v)
-            rise = across(flux)
-            for q in range(pieces):
-                part_ref[q, here, :] = s[q] - DIVERGE * rise[q] + FORCING * e_ref[q, here, :]
-        for block in reversed(range(total // 8)):
+                if inside:
+                    v = w * (FRICTION * v_ref[q, here, :] - slope[q])
+                    v_ref[q, here, :] = v
+                    flux.append(h * v)
+            if inside:
+                rise = across(flux)
+                for q in range(pieces):
+                    part_ref[q, here, :] = s[q] - rise[q] + (PRESSURE * FORCING) * e_ref[q, here, :]
+        for block in reversed(range(skip, total // 8 - skip)):
             r = PAD + 8 * block
             here, below, above = pl.ds(r, 8), pl.ds(r + 1, 8), pl.ds(r - 1, 8)
             for q in range(pieces):
                 w = w_ref[q, here, :]
                 rise = flux_ref[q, below, :] - flux_ref[q, above, :]
-                s_ref[q, here, :] = w * (part_ref[q, here, :] - DIVERGE * rise)
-                e = e_ref[q, here, :]
-                e_ref[q, here, :] = w * (e - UPWIND * (e - e_ref[q, above, :]) - DAMPING * e)
+                s_ref[q, here, :] = w * (part_ref[q, here, :] - rise)
+                if skip_energy <= block < total // 8 - skip_energy:
+                    e = e_ref[q, here, :]
+                    e_ref[q, here, :] = w * ((1.0 - UPWIND - DAMPING) * e + UPWIND * e_ref[q, above, :])
 
     window = cell_win.shape[0]
     base = 6 * halo
@@ -178,7 +186,7 @@
         equiv = equiv + lax.dot_general(
             part, spread, (((1,), (1,)), ((), ())), preferred_element_type=jnp.float32
         )
-    equiv = equiv * gain_win[...]
+    equiv = equiv * ((1.0 / PRESSURE) * gain_win[...])
     equiv_ref[...] = equiv
     across_ref[across_ref.shape[0] - window :, :] = equiv
 
@@ -188,7 +196,8 @@
         for i in range(PACKED):
             for q in range(pieces):
                 target = (i * pieces + q) * own_rows
-                out_ref[j, target : target + own_rows, :] = fields[i][q, source : source + own_rows, :]
+                block = fields[i][q, source : source + own_rows, :]
+                out_ref[j, target : target + own_rows, :] = block if i else block * (1.0 / PRESSURE)
         source = pl.multiple_of(first + (me ^ j) * own_rows, min(own_rows, 8))
         for i in range(PACKED, 4):
             for q in range(pieces):
@@ -212,18 +221,20 @@
     return terms[0]
 
 
-def weight_kernel(sizes, four_ref, *refs):
+def weight_kernel(sizes, three_ref, last_ref, *refs):
     members, halo = sizes
     half = members // 2
     near_refs, refs = refs[: half // 2 - 1], refs[half // 2 - 1 :]
     spot_ref, damp_ref, live_ref, value_ref, error_ref, near_ref, far_ref = refs[:7]
     mix_ref, value_win, error_win, equiv_win = refs[7:]
     window = value_win.shape[0]
-    for i, ref in enumerate((four_ref, *near_refs)):
-        start = ref.shape[0] - 4 * window
-        for place in (2 * i, 2 * i + half, 2 * i + 1, 2 * i + half + 1):
+    for i, ref in enumerate((three_ref, *near_refs)):
+        start = ref.shape[0] - 3 * window
+        for place in (2 * i, 2 * i + 1, 2 * i + half):
             equiv_win[place * window : (place + 1) * window, :] = ref[start : start + window, :]
             start += window
+        place = 2 * i + half + 1
+        equiv_win[place * window : (place + 1) * window, :] = last_ref[i * window : (i + 1) * window, :]
     even = lax.axis_index("tile") % 2 == 0
     window_parts(value_win, value_ref[...], near_ref, far_ref, 6 * halo, 2, even)
     window_parts(error_win, error_ref[...], near_ref, far_ref, 6 * halo, 3, even)
@@ -349,14 +360,17 @@
 def trade_blocks(equiv, across, along):
     half = len(along)
     size = along[0].shape[0]
+    window = equiv.shape[0]
     passed = trade(across, 1)
-    far = [trade(equiv, half + i) for i in range(2)]
-    four = jnp.concatenate([equiv, far[0], passed[half * size :], far[1]], axis=0)
+    far = trade(equiv, half)
+    three = jnp.concatenate([equiv, passed[half * size :], far], axis=0)
     pairs = []
     for i in range(1, half):
-        parts = [along[i], passed[i * size : (i + 1) * size]] + ([four] if 2 * i < half else [])
+        parts = [along[i], passed[i * size : (i + 1) * size]] + ([three] if 2 * i < half else [])
         pairs.append(trade(jnp.concatenate(parts, axis=0), 2 * i))
-    return four, pairs[: half // 2 - 1], [along[0], passed, *pairs]
+    near = pairs[: half // 2 - 1]
+    last = trade(jnp.concatenate([far] + [x[x.shape[0] - window :] for x in near], axis=0), 1)
+    return three, last, near, [along[0], passed, *pairs]
 
 
 def swaps(near, far):
@@ -447,7 +461,7 @@
         far,
     )
     received = lax.all_to_all(sends, "member", split_axis=0, concat_axis=0, tiled=True)
-    four, near_pairs, rest = trade_blocks(equiv, across, along)
+    three, last, near_pairs, rest = trade_blocks(equiv, across, along)
     received = received.reshape(members * packet, LANES)
 
     patch_index = lax.axis_index("member") * per_dev + jnp.arange(per_dev, dtype=jnp.int32)
@@ -460,14 +474,15 @@
     mix = pl.pallas_call(
         functools.partial(weight_kernel, (members, halo)),
         out_shape=jax.ShapeDtypeStruct((members, LANES), jnp.float32),
-        in_specs=vmem_specs(8 + len(near_pairs)),
+        in_specs=vmem_specs(9 + len(near_pairs)),
         out_specs=vmem_specs(1)[0],
         scratch_shapes=[pltpu.VMEM((window, LANES), jnp.float32)] * 2
         + [pltpu.VMEM((members * window, LANES), jnp.float32)],
         compiler_params=pltpu.CompilerParams(vmem_limit_bytes=24 * 2**20),
         name="weights",
     )(
-        four,
+        three,
+        last,
         *near_pairs,
         spot,
         side_by_side(damp, pairs),

time: 50.2 us -> 50 us (level)
    all_to_all x1, starting transfers between devices: 5.55 us -> 3.41 us  [body(): lax.all_to_all(sends, 'member', split_axis=0, concat_axis=0, tiled=True)]
    ppermute x6, starting transfers between devices: 7.85 us -> 9.46 us  [trade(): lax.ppermute(block, 'member', [(i, i ^ distance) for i in range(members)])]
where the time goes in v7:
time: 50 us; the launch traced here: 49.7 us
  starting transfers between devices  17.5 us (35%)
  blocking collectives  15.7 us (31%)
  waiting for transfers between devices  7.99 us (16%)
  Pallas kernels  7.05 us (14%)
  local copies, waits for them, and re-layouts  0.91 us (2%)
    all_to_all x1, blocking collectives, body(): lax.all_to_all(analysed, 'member', split_axis=0, concat_axis=0, tiled=True)  15.7 us
    ppermute x6, starting transfers between devices, trade(): lax.ppermute(block, 'member', [(i, i ^ distance) for i in range(members)])  9.46 us
    ppermute x1, starting transfers between devices, swaps(): far = lax.ppermute(far, 'tile', pairs(1))  4.48 us
    ppermute x6, waiting for transfers between devices, trade(): lax.ppermute(block, 'member', [(i, i ^ distance) for i in range(members)])  4.46 us
    ppermute x1, waiting for transfers between devices, swaps(): far = lax.ppermute(far, 'tile', pairs(1))  3.52 us
    all_to_all x1, starting transfers between devices, body(): lax.all_to_all(sends, 'member', split_axis=0, concat_axis=0, tiled=True)  3.41 us
    pallas_call x1, Pallas kernels, body(): pl.pallas_call(functools.partial(weight_kernel, (members, halo)), out_sha...  2.96 us
    pallas_call x1, Pallas kernels, body(): pl.pallas_call(functools.partial(forecast_kernel, (members, own_rows, hal...  2.41 us
  transfers between devices with their start and end apart: 9, of which 3 were waited for; matrix products, arithmetic and copies ran while one was open for 1% of the time, Pallas kernels for 6%

profile of v7, /device:TPU:1, one launch (start us, length us, event | category | flops | bytes accessed | tf_op | source)
XLA Modules:
  0.0 49.7 jit_solution(3992163513288380938)
XLA Ops:
  0.0 1.2 %edges.1 = (f32[104,512]{1,0:T(8,128)S(1)}, f32[104,512]{1,0:T(8,128)S(1)}) custom-call(f32[4,64,512]{2,1,0:T(8,128)} %bitcast.19, f32[64,512]{1,0:T(8,128)} %depth_ref.1, s32[64,512]{1,0:T(8,128)} %mask_ref.1, s32[32,128]{1,0:T(8,128)} %bitcast.22, f32[32,128]{1,0:T(8,128)} %bitcast.24, f32[32,128]{1,0:T(8,128)} %bitcast.26, f32[32,128]{1,0:T(8,128)} %bitcast.28), custom_call_target="tpu_custom_call" | custom-call | tf_op jit(solution)/shard_map/edges/pallas_call | solution.py:414
  1.3 0.0 copy-start.1
  1.3 0.1 collective-permute-start
  1.4 4.5 %collective-permute-start.1 = (f32[104,512]{1,0:T(8,128)S(1)}, f32[104,512]{1,0:T(8,128)S(1)}, u32[]{:S(2)}, u32[]{:S(2)}) collective-permute-start(f32[104,512]{1,0:T(8,128)S(1)} %get-tuple-element.15), channel_id=1, source_target_pairs={{1,2},{2,1},{5,6},{6,5},{9,10},{10,9},{13,14},{14,13},{17,18},{18,... | collective-permute-start | bytes 638984 | tf_op jit(solution)/shard_map/ppermute | solution.py:383
  5.9 0.1 multiply_add_fusion
  6.0 0.1 fusion.1
  6.1 0.1 pad_maximum_fusion.4
  6.2 3.5 %collective-permute-done.1.far_ref.refs_7_ = f32[104,512]{1,0:T(8,128)S(1)} collective-permute-done((f32[104,512]{1,0:T(8,128)S(1)}, f32[104,512]{1,0:T(8,128)S(1)}, u32[]{:S(2)}, u32[]{:S(2)}) %collective-permute-start.1) | collective-permute-done | bytes 213024 | tf_op jit(solution)/shard_map/ppermute | solution.py:383
  9.7 2.4 %forecast.1 = (f32[8,64,128]{2,1,0:T(8,128)}, f32[40,128]{1,0:T(8,128)S(1)}, f32[296,128]{1,0:T(8,128)S(1)}, f32[64,128]{1,0:T(8,128)S(1)}, f32[64,128]{1,0:T(8,...) custom-call(f32[4,64,512]{2,1,0:T(8,128)S(1)} %bitcast.20, f32[64,512]{1,0:T(8,128)S(1)} %copy-done.1, ...), custom_call_target="tpu_custom_call" | custom-call | tf_op jit(solution)/shard_map/forecast/pallas_call | solution.py:441
  12.1 1.9 %collective-permute-start.2 = (f32[296,128]{1,0:T(8,128)S(1)}, f32[296,128]{1,0:T(8,128)S(1)}, u32[]{:S(2)}, u32[]{:S(2)}) collective-permute-start(f32[296,128]{1,0:T(8,128)S(1)} %get-tuple-element.18), channel_id=1, source_target_pairs={{0,4},{4,0},{8,12},{12,8},{16,20},{20,16},{24,28},{28,24},{1,5},{5... | collective-permute-start | bytes 454664 | tf_op jit(solution)/shard_map/ppermute | solution.py:357
  14.0 0.1 pad_add_fusion.refs_1_
  14.0 2.3 %collective-permute-start.3 = (f32[40,128]{1,0:T(8,128)S(1)}, f32[40,128]{1,0:T(8,128)S(1)}, u32[]{:S(2)}, u32[]{:S(2)}) collective-permute-start(f32[40,128]{1,0:T(8,128)S(1)} %get-tuple-element.17), channel_id=1, source_target_pairs={{0,16},{4,20},{8,24},{12,28},{16,0},{20,4},{24,8},{28,12},{1,17},{... | collective-permute-start | bytes 61448 | tf_op jit(solution)/shard_map/ppermute | solution.py:357
  16.3 3.4 %all-to-all-start = ((f32[8,64,128]{2,1,0:T(8,128)}), f32[8,64,128]{2,1,0:T(8,128)S(1)}, u32[]{:S(2)}, u32[]{:S(2)}) async-start(f32[8,64,128]{2,1,0:T(8,128)} %get-tuple-element.16), calls=%async_computation | async-start | bytes 524288 | tf_op jit(solution)/shard_map/all_to_all | solution.py:463
  19.8 0.0 collective-permute-done.2.refs_1_
  19.9 1.4 %collective-permute-start.4 = (f32[248,128]{1,0:T(8,128)S(1)}, f32[248,128]{1,0:T(8,128)S(1)}, u32[]{:S(2)}, u32[]{:S(2)}) collective-permute-start(f32[248,128]{1,0:T(8,128)S(1)} %constant_dynamic-update-slice_fusion), channel_id=1, source_target_pairs={{0,8},{4,12},{8,0},{12,4},{16,24},{20,28},{24,16},{28,20},{1,9},{5... | collective-permute-start | bytes 380936 | tf_op jit(solution)/shard_map/ppermute | solution.py:357
  21.3 2.1 %collective-permute-start.7 = (f32[128,128]{1,0:T(8,128)S(1)}, f32[128,128]{1,0:T(8,128)S(1)}, u32[]{:S(2)}, u32[]{:S(2)}) collective-permute-start(f32[128,128]{1,0:T(8,128)S(1)} %pad_maximum_fusion.1), channel_id=1, source_target_pairs={{0,24},{4,28},{8,16},{12,20},{16,8},{20,12},{24,0},{28,4},{1,25},{... | collective-permute-start | bytes 196616 | tf_op jit(solution)/shard_map/ppermute | solution.py:357
  23.4 0.1 collective-permute-start.6
  23.5 3.1 %collective-permute-done.4.refs_0_.refs_2_ = f32[248,128]{1,0:T(8,128)S(1)} collective-permute-done((f32[248,128]{1,0:T(8,128)S(1)}, f32[248,128]{1,0:T(8,128)S(1)}, u32[]{:S(2)}, u32[]{:S(2)}) %collective-permute-start.4) | collective-permute-done | bytes 127008 | tf_op jit(solution)/shard_map/ppermute | solution.py:357
  26.6 1.7 %collective-permute-start.5 = (f32[80,128]{1,0:T(8,128)S(1)}, f32[80,128]{1,0:T(8,128)S(1)}, u32[]{:S(2)}, u32[]{:S(2)}) collective-permute-start(f32[80,128]{1,0:T(8,128)S(1)} %pad_maximum_fusion.3), channel_id=1, source_target_pairs={{0,4},{4,0},{8,12},{12,8},{16,20},{20,16},{24,28},{28,24},{1,5},{5... | collective-permute-start | bytes 122888 | tf_op jit(solution)/shard_map/ppermute | solution.py:357
  28.3 1.4 %collective-permute-done.5.last_ref = f32[80,128]{1,0:T(8,128)S(1)} collective-permute-done((f32[80,128]{1,0:T(8,128)S(1)}, f32[80,128]{1,0:T(8,128)S(1)}, u32[]{:S(2)}, u32[]{:S(2)}) %collective-permute-start.5) | collective-permute-done | bytes 40992 | tf_op jit(solution)/shard_map/ppermute | solution.py:357
  29.7 3.0 %weights.1.mix_ref = f32[8,128]{1,0:T(8,128)S(1)} custom-call(f32[120,128]{1,0:T(8,128)S(1)} %pad_maximum_fusion.2.three_ref, f32[80,128]{1,0:T(8,128)S(1)} %collective-permute-done.5.last_ref, f32[248,128]{1,0:T(8,128)S(1)} %collective-permute-done.4.refs_0_.refs_2_, s32[8,128]{1,0:T(8,128)S(1)} %pad_add_fusion.refs_1_, ...), custom_call_target="tpu_custom_call" | custom-call | tf_op jit(solution)/shard_map/weights/pallas_call | solution.py:474
  32.6 0.5 mix.1
  33.1 15.7 %all_to_all.10 = f32[8,4,8,512]{3,2,1,0:T(8,128)S(1)} all-to-all(f32[8,4,8,512]{3,2,1,0:T(8,128)S(1)} %mix.1), channel_id=1, replica_groups=mesh['member'=8,'tile'=4] {'member'}, dimensions={0} | all-to-all | bytes 1048576 | tf_op jit(solution)/shard_map/all_to_all | solution.py:504
  48.9 0.8 %copy_bitcast_fusion = f32[1,4,64,512]{3,2,1,0:T(8,128)} fusion(f32[8,4,8,512]{3,2,1,0:T(8,128)S(1)} %all_to_all.10), kind=kLoop, calls=%fused_computation | loop fusion | bytes 1048576 | tf_op jit(solution)/shard_map/reshape | solution.py:505
  (37 shorter events, 0.1 us)
Async XLA Ops:
  0.0 9.7 %copy-start = (f32[1,4,64,512]{3,2,1,0:T(8,128)S(1)}, f32[1,4,64,512]{3,2,1,0:T(8,128)}, u32[]{:S(2)}) copy-start(f32[1,4,64,512]{3,2,1,0:T(8,128)} %param.9) | copy-start | bytes 1572868
  0.0 5.9 %copy-start.7 = (s32[1,16,64]{2,1,0:T(8,128)S(1)}, s32[1,16,64]{2,1,0:T(8,128)}, u32[]{:S(2)}) copy-start(s32[1,16,64]{2,1,0:T(8,128)} %param.16) | copy-start | bytes 12292
  0.0 6.0 %copy-start.8 = (s32[1,16]{1,0:T(1,128)S(1)}, s32[1,16]{1,0:T(1,128)}, u32[]{:S(2)}) copy-start(s32[1,16]{1,0:T(1,128)} %param.17) | copy-start | bytes 196
  0.0 9.7 %copy-start.2 = (s32[64,512]{1,0:T(8,128)S(1)}, s32[64,512]{1,0:T(8,128)}, u32[]{:S(2)}) copy-start(s32[64,512]{1,0:T(8,128)} %mask_ref.1) | copy-start | bytes 393220
  0.0 9.7 %copy-start.3 = (s32[4096]{0:T(1024)S(1)}, s32[4096]{0:T(1024)}, u32[]{:S(2)}) copy-start(s32[4096]{0:T(1024)} %param.12) | copy-start | bytes 49156
  0.0 9.7 %copy-start.4 = (f32[4096]{0:T(1024)S(1)}, f32[4096]{0:T(1024)}, u32[]{:S(2)}) copy-start(f32[4096]{0:T(1024)} %param.15) | copy-start | bytes 49156
  1.3 8.4 %copy-start.1 = (f32[64,512]{1,0:T(8,128)S(1)}, f32[64,512]{1,0:T(8,128)}, u32[]{:S(2)}) copy-start(f32[64,512]{1,0:T(8,128)} %depth_ref.1) | copy-start | bytes 393220
  1.3 4.9 %collective-permute-start = (f32[104,512]{1,0:T(8,128)S(1)}, f32[104,512]{1,0:T(8,128)S(1)}, u32[]{:S(2)}, u32[]{:S(2)}) collective-permute-start(f32[104,512]{1,0:T(8,128)S(1)} %get-tuple-element.14), channel_id=1, source_target_pairs={{0,1},{2,3},{1,0},{3,2},{4,5},{6,7},{5,4},{7,6},{8,9},{10,11},{9,8... | collective-permute-start | bytes 638984 | tf_op jit(solution)/shard_map/ppermute | solution.py:384
  1.4 8.3 %collective-permute-start.1 = (f32[104,512]{1,0:T(8,128)S(1)}, f32[104,512]{1,0:T(8,128)S(1)}, u32[]{:S(2)}, u32[]{:S(2)}) collective-permute-start(f32[104,512]{1,0:T(8,128)S(1)} %get-tuple-element.15), channel_id=1, source_target_pairs={{1,2},{2,1},{5,6},{6,5},{9,10},{10,9},{13,14},{14,13},{17,18},{18,... | collective-permute-start | bytes 638984 | tf_op jit(solution)/shard_map/ppermute | solution.py:383
  12.1 7.7 %collective-permute-start.2 = (f32[296,128]{1,0:T(8,128)S(1)}, f32[296,128]{1,0:T(8,128)S(1)}, u32[]{:S(2)}, u32[]{:S(2)}) collective-permute-start(f32[296,128]{1,0:T(8,128)S(1)} %get-tuple-element.18), channel_id=1, source_target_pairs={{0,4},{4,0},{8,12},{12,8},{16,20},{20,16},{24,28},{28,24},{1,5},{5... | collective-permute-start | bytes 454664 | tf_op jit(solution)/shard_map/ppermute | solution.py:357
  14.0 5.8 %collective-permute-start.3 = (f32[40,128]{1,0:T(8,128)S(1)}, f32[40,128]{1,0:T(8,128)S(1)}, u32[]{:S(2)}, u32[]{:S(2)}) collective-permute-start(f32[40,128]{1,0:T(8,128)S(1)} %get-tuple-element.17), channel_id=1, source_target_pairs={{0,16},{4,20},{8,24},{12,28},{16,0},{20,4},{24,8},{28,12},{1,17},{... | collective-permute-start | bytes 61448 | tf_op jit(solution)/shard_map/ppermute | solution.py:357
  16.3 16.3 %all-to-all-start = ((f32[8,64,128]{2,1,0:T(8,128)}), f32[8,64,128]{2,1,0:T(8,128)S(1)}, u32[]{:S(2)}, u32[]{:S(2)}) async-start(f32[8,64,128]{2,1,0:T(8,128)} %get-tuple-element.16), calls=%async_computation | async-start | bytes 524288 | tf_op jit(solution)/shard_map/all_to_all | solution.py:463
  19.9 6.7 %collective-permute-start.4 = (f32[248,128]{1,0:T(8,128)S(1)}, f32[248,128]{1,0:T(8,128)S(1)}, u32[]{:S(2)}, u32[]{:S(2)}) collective-permute-start(f32[248,128]{1,0:T(8,128)S(1)} %constant_dynamic-update-slice_fusion), channel_id=1, source_target_pairs={{0,8},{4,12},{8,0},{12,4},{16,24},{20,28},{24,16},{28,20},{1,9},{5... | collective-permute-start | bytes 380936 | tf_op jit(solution)/shard_map/ppermute | solution.py:357
  21.3 11.3 %collective-permute-start.7 = (f32[128,128]{1,0:T(8,128)S(1)}, f32[128,128]{1,0:T(8,128)S(1)}, u32[]{:S(2)}, u32[]{:S(2)}) collective-permute-start(f32[128,128]{1,0:T(8,128)S(1)} %pad_maximum_fusion.1), channel_id=1, source_target_pairs={{0,24},{4,28},{8,16},{12,20},{16,8},{20,12},{24,0},{28,4},{1,25},{... | collective-permute-start | bytes 196616 | tf_op jit(solution)/shard_map/ppermute | solution.py:357
  23.4 9.2 %collective-permute-start.6 = (f32[128,128]{1,0:T(8,128)S(1)}, f32[128,128]{1,0:T(8,128)S(1)}, u32[]{:S(2)}, u32[]{:S(2)}) collective-permute-start(f32[128,128]{1,0:T(8,128)S(1)} %pad_maximum_fusion), channel_id=1, source_target_pairs={{0,16},{4,20},{8,24},{12,28},{16,0},{20,4},{24,8},{28,12},{1,17},{... | collective-permute-start | bytes 196616 | tf_op jit(solution)/shard_map/ppermute | solution.py:357
  26.6 3.1 %collective-permute-start.5 = (f32[80,128]{1,0:T(8,128)S(1)}, f32[80,128]{1,0:T(8,128)S(1)}, u32[]{:S(2)}, u32[]{:S(2)}) collective-permute-start(f32[80,128]{1,0:T(8,128)S(1)} %pad_maximum_fusion.3), channel_id=1, source_target_pairs={{0,4},{4,0},{8,12},{12,8},{16,20},{20,16},{24,28},{28,24},{1,5},{5... | collective-permute-start | bytes 122888 | tf_op jit(solution)/shard_map/ppermute | solution.py:357
  28.3 1.4 %copy-start.5 = (f32[4096]{0:T(1024)S(1)}, f32[4096]{0:T(1024)}, u32[]{:S(2)}) copy-start(f32[4096]{0:T(1024)} %param.13) | copy-start | bytes 49156
  28.3 1.4 %copy-start.6 = (f32[4096]{0:T(1024)S(1)}, f32[4096]{0:T(1024)}, u32[]{:S(2)}) copy-start(f32[4096]{0:T(1024)} %param.14) | copy-start | bytes 49156

commit v8 on v7

--- a/solution.py
+++ b/solution.py
@@ -221,23 +221,37 @@
     return terms[0]
 
 
-def weight_kernel(sizes, three_ref, last_ref, *refs):
-    members, halo = sizes
-    half = members // 2
-    near_refs, refs = refs[: half // 2 - 1], refs[half // 2 - 1 :]
-    spot_ref, damp_ref, live_ref, value_ref, error_ref, near_ref, far_ref = refs[:7]
-    mix_ref, value_win, error_win, equiv_win = refs[7:]
+def precision_kernel(
+    halo, spot_ref, damp_ref, live_ref, value_ref, error_ref, near_ref, far_ref, out_ref, value_win, error_win
+):
     window = value_win.shape[0]
-    for i, ref in enumerate((three_ref, *near_refs)):
-        start = ref.shape[0] - 3 * window
-        for place in (2 * i, 2 * i + 1, 2 * i + half):
-            equiv_win[place * window : (place + 1) * window, :] = ref[start : start + window, :]
-            start += window
-        place = 2 * i + half + 1
-        equiv_win[place * window : (place + 1) * window, :] = last_ref[i * window : (i + 1) * window, :]
     even = lax.axis_index("tile") % 2 == 0
     window_parts(value_win, value_ref[...], near_ref, far_ref, 6 * halo, 2, even)
     window_parts(error_win, error_ref[...], near_ref, far_ref, 6 * halo, 3, even)
+    spot = spot_ref[...]
+    row, lane = spot // LANES, spot % LANES
+    value = jnp.zeros(spot.shape, jnp.float32)
+    error = jnp.zeros(spot.shape, jnp.float32)
+    for r in range(window):
+        hit = row == r
+        line = jnp.broadcast_to(value_win[r : r + 1, :], spot.shape)
+        value = jnp.where(hit, jnp.take_along_axis(line, lane, axis=1, mode="promise_in_bounds"), value)
+        line = jnp.broadcast_to(error_win[r : r + 1, :], spot.shape)
+        error = jnp.where(hit, jnp.take_along_axis(line, lane, axis=1, mode="promise_in_bounds"), error)
+    out_ref[0] = value
+    out_ref[1] = jnp.where(live_ref[...] > 0.0, 1.0 / (damp_ref[...] * error), 0.0)
+
+
+def weight_kernel(members, three_ref, last_ref, *refs):
+    half = members // 2
+    near_refs, (spot_ref, known_ref, mix_ref, equiv_win) = refs[: half // 2 - 1], refs[half // 2 - 1 :]
+    window = equiv_win.shape[0] // members
+    for i, ref in enumerate((three_ref, *near_refs)):
+        for j, place in enumerate((2 * i, 2 * i + 1, 2 * i + half)):
+            equiv_win[place * window : (place + 1) * window, :] = ref[j * window : (j + 1) * window, :]
+        place = 2 * i + half + 1
+        equiv_win[place * window : (place + 1) * window, :] = last_ref[i * window : (i + 1) * window, :]
+    value, precision = known_ref[0], known_ref[1]
 
     spot = spot_ref[...]
     pairs = spot.shape[0]
@@ -245,19 +259,11 @@
     rows_of = [jnp.broadcast_to(row[i : i + 1, :], (members, LANES)) for i in range(pairs)]
     lanes_of = [jnp.broadcast_to(lane[i : i + 1, :], (members, LANES)) for i in range(pairs)]
     picked = [jnp.zeros((members, LANES), jnp.float32) for i in range(pairs)]
-    value = jnp.zeros((pairs, LANES), jnp.float32)
-    error = jnp.zeros((pairs, LANES), jnp.float32)
     for r in range(window):
         source = equiv_win[pl.ds(r, members, stride=window), :]
         for i in range(pairs):
             got = jnp.take_along_axis(source, lanes_of[i], axis=1, mode="promise_in_bounds")
             picked[i] = jnp.where(rows_of[i] == r, got, picked[i])
-        hit = row == r
-        line = jnp.broadcast_to(value_win[r : r + 1, :], spot.shape)
-        value = jnp.where(hit, jnp.take_along_axis(line, lane, axis=1, mode="promise_in_bounds"), value)
-        line = jnp.broadcast_to(error_win[r : r + 1, :], spot.shape)
-        error = jnp.where(hit, jnp.take_along_axis(line, lane, axis=1, mode="promise_in_bounds"), error)
-    precision = jnp.where(live_ref[...] > 0.0, 1.0 / (damp_ref[...] * error), 0.0)
 
     left_half = iota((members, LANES), 1) < LANES // 2
     weighted, spreads, innovations = [], [], []
@@ -364,12 +370,12 @@
     passed = trade(across, 1)
     far = trade(equiv, half)
     three = jnp.concatenate([equiv, passed[half * size :], far], axis=0)
-    pairs = []
-    for i in range(1, half):
-        parts = [along[i], passed[i * size : (i + 1) * size]] + ([three] if 2 * i < half else [])
-        pairs.append(trade(jnp.concatenate(parts, axis=0), 2 * i))
-    near = pairs[: half // 2 - 1]
-    last = trade(jnp.concatenate([far] + [x[x.shape[0] - window :] for x in near], axis=0), 1)
+    near = [trade(three, 2 * i) for i in range(1, half // 2)]
+    last = trade(jnp.concatenate([far] + [x[2 * window :] for x in near], axis=0), 1)
+    pairs = [
+        trade(jnp.concatenate([along[i], passed[i * size : (i + 1) * size]], axis=0), 2 * i)
+        for i in range(1, half)
+    ]
     return three, last, near, [along[0], passed, *pairs]
 
 
@@ -461,7 +467,7 @@
         far,
     )
     received = lax.all_to_all(sends, "member", split_axis=0, concat_axis=0, tiled=True)
-    three, last, near_pairs, rest = trade_blocks(equiv, across, along)
+    three, last, near_equivs, rest = trade_blocks(equiv, across, along)
     received = received.reshape(members * packet, LANES)
 
     patch_index = lax.axis_index("member") * per_dev + jnp.arange(per_dev, dtype=jnp.int32)
@@ -471,19 +477,14 @@
     damp = 1.0 + 4.0 * dist * dist
     live = jnp.arange(slots, dtype=jnp.int32)[None, :] < obs_count[0][:, None]
     spot = side_by_side(obs_list[0] - (obs_tile - radius), pairs)
-    mix = pl.pallas_call(
-        functools.partial(weight_kernel, (members, halo)),
-        out_shape=jax.ShapeDtypeStruct((members, LANES), jnp.float32),
-        in_specs=vmem_specs(9 + len(near_pairs)),
+    known = pl.pallas_call(
+        functools.partial(precision_kernel, halo),
+        out_shape=pltpu.VMEM((2, pairs, LANES), jnp.float32),
+        in_specs=vmem_specs(7),
         out_specs=vmem_specs(1)[0],
-        scratch_shapes=[pltpu.VMEM((window, LANES), jnp.float32)] * 2
-        + [pltpu.VMEM((members * window, LANES), jnp.float32)],
-        compiler_params=pltpu.CompilerParams(vmem_limit_bytes=24 * 2**20),
-        name="weights",
+        scratch_shapes=[pltpu.VMEM((window, LANES), jnp.float32)] * 2,
+        name="precision",
     )(
-        three,
-        last,
-        *near_pairs,
         spot,
         side_by_side(damp, pairs),
         side_by_side(live.astype(jnp.float32), pairs),
@@ -492,6 +493,15 @@
         near,
         far,
     )
+    mix = pl.pallas_call(
+        functools.partial(weight_kernel, members),
+        out_shape=jax.ShapeDtypeStruct((members, LANES), jnp.float32),
+        in_specs=vmem_specs(4 + len(near_equivs)),
+        out_specs=vmem_specs(1)[0],
+        scratch_shapes=[pltpu.VMEM((members * window, LANES), jnp.float32)],
+        compiler_params=pltpu.CompilerParams(vmem_limit_bytes=24 * 2**20),
+        name="weights",
+    )(three, last, *near_equivs, spot, known)
     analysed = pl.pallas_call(
         functools.partial(mix_kernel, (members, own_rows, pieces)),
         out_shape=jax.ShapeDtypeStruct((members, 4, own_rows, width), jnp.float32),

time: 50 us -> 50.5 us (1.010)
  waiting for transfers between devices: 7.99 us -> 2.97 us
  blocking collectives: 15.7 us -> 17.3 us
  other arithmetic: 0.34 us -> 1.53 us
  Pallas kernels: 7.05 us -> 8.19 us
  starting transfers between devices: 17.5 us -> 18.5 us
  local copies, waits for them, and re-layouts: 0.91 us -> 1.53 us
    ppermute x6 -> x7, waiting for transfers between devices: 4.46 us -> 0.02 us  [trade(): lax.ppermute(block, 'member', [(i, i ^ distance) for i in range(members)])]
    all_to_all x1, blocking collectives: 15.7 us -> 17.3 us  [body(): lax.all_to_all(analysed, 'member', split_axis=0, concat_axis=0, tiled=True)]
    concatenate x2, other arithmetic: 0.15 us -> 1.33 us  [side_by_side(): return jnp.concatenate([x[:pairs], x[pairs:]], axis=1)]
    pallas_call x1 -> x2, Pallas kernels: 2.96 us -> 4.04 us  [the longest x1 2.8 us: body(): pl.pallas_call(functools.partial(weight_kernel, members), out_shape=jax.S...]
    ppermute x6 -> x7, starting transfers between devices: 9.46 us -> 10.4 us  [trade(): lax.ppermute(block, 'member', [(i, i ^ distance) for i in range(members)])]
    unnamed x21 -> x20, local copies, waits for them, and re-layouts: 0.05 us -> 0.68 us
    ppermute x1, waiting for transfers between devices: 3.52 us -> 2.94 us  [swaps(): far = lax.ppermute(far, 'tile', pairs(1))]
  transfers between devices with their start and end apart: 9 -> 10, of which waited for: 3 -> 1; matrix products, arithmetic and copies ran while one was open for 1% -> 3% of each run, Pallas kernels for 6% -> 8%
where the time goes in v8:
time: 50.5 us; the launch traced here: 50.2 us
  starting transfers between devices  18.5 us (37%)
  blocking collectives  17.3 us (34%)
  Pallas kernels  8.19 us (16%)
  waiting for transfers between devices  2.97 us (6%)
  local copies, waits for them, and re-layouts  1.53 us (3%)
  other arithmetic  1.53 us (3%)
    all_to_all x1, blocking collectives, body(): lax.all_to_all(analysed, 'member', split_axis=0, concat_axis=0, tiled=True)  17.3 us
    ppermute x7, starting transfers between devices, trade(): lax.ppermute(block, 'member', [(i, i ^ distance) for i in range(members)])  10.4 us
    ppermute x1, starting transfers between devices, swaps(): far = lax.ppermute(far, 'tile', pairs(1))  4.48 us
    all_to_all x1, starting transfers between devices, body(): lax.all_to_all(sends, 'member', split_axis=0, concat_axis=0, tiled=True)  3.41 us
    ppermute x1, waiting for transfers between devices, swaps(): far = lax.ppermute(far, 'tile', pairs(1))  2.94 us
    pallas_call x1, Pallas kernels, body(): pl.pallas_call(functools.partial(weight_kernel, members), out_shape=jax.S...  2.8 us
    pallas_call x1, Pallas kernels, body(): pl.pallas_call(functools.partial(forecast_kernel, (members, own_rows, hal...  2.41 us
    concatenate x2, other arithmetic, side_by_side(): return jnp.concatenate([x[:pairs], x[pairs:]], axis=1)  1.33 us
  transfers between devices with their start and end apart: 10, of which 1 were waited for; matrix products, arithmetic and copies ran while one was open for 3% of the time, Pallas kernels for 8%

profile of v8, /device:TPU:1, one launch (start us, length us, event | category | flops | bytes accessed | tf_op | source)
XLA Modules:
  0.0 50.2 jit_solution(10295130899145749638)
XLA Ops:
  0.0 1.2 %edges.1 = (f32[104,512]{1,0:T(8,128)S(1)}, f32[104,512]{1,0:T(8,128)S(1)}) custom-call(f32[4,64,512]{2,1,0:T(8,128)} %bitcast.19, f32[64,512]{1,0:T(8,128)} %depth_ref.1, s32[64,512]{1,0:T(8,128)} %mask_ref.1, s32[32,128]{1,0:T(8,128)} %bitcast.22, f32[32,128]{1,0:T(8,128)} %bitcast.24, f32[32,128]{1,0:T(8,128)} %bitcast.26, f32[32,128]{1,0:T(8,128)} %bitcast.28), custom_call_target="tpu_custom_call" | custom-call | tf_op jit(solution)/shard_map/edges/pallas_call | solution.py:420
  1.3 0.1 collective-permute-start
  1.4 4.5 %collective-permute-start.1 = (f32[104,512]{1,0:T(8,128)S(1)}, f32[104,512]{1,0:T(8,128)S(1)}, u32[]{:S(2)}, u32[]{:S(2)}) collective-permute-start(f32[104,512]{1,0:T(8,128)S(1)} %get-tuple-element.15), channel_id=1, source_target_pairs={{1,2},{2,1},{5,6},{6,5},{9,10},{10,9},{13,14},{14,13},{17,18},{18,... | collective-permute-start | bytes 638984 | tf_op jit(solution)/shard_map/ppermute | solution.py:389
  5.9 0.1 multiply_add_fusion
  6.0 0.0 copy-start.5
  6.0 0.6 %copy-done.9 = s32[1,16]{1,0:T(1,128)S(1)} copy-done((s32[1,16]{1,0:T(1,128)S(1)}, s32[1,16]{1,0:T(1,128)}, u32[]{:S(2)}) %copy-start.9) | copy-done | bytes 88
  6.6 0.1 fusion.1
  6.7 2.9 %collective-permute-done.1.far_ref = f32[104,512]{1,0:T(8,128)S(1)} collective-permute-done((f32[104,512]{1,0:T(8,128)S(1)}, f32[104,512]{1,0:T(8,128)S(1)}, u32[]{:S(2)}, u32[]{:S(2)}) %collective-permute-start.1) | collective-permute-done | bytes 213024 | tf_op jit(solution)/shard_map/ppermute | solution.py:389
  9.7 2.4 %forecast.1 = (f32[8,64,128]{2,1,0:T(8,128)}, f32[40,128]{1,0:T(8,128)S(1)}, f32[296,128]{1,0:T(8,128)S(1)}, f32[64,128]{1,0:T(8,128)S(1)}, f32[64,128]{1,0:T(8,...) custom-call(f32[4,64,512]{2,1,0:T(8,128)S(1)} %bitcast.20, f32[64,512]{1,0:T(8,128)S(1)} %copy-done.3, ...), custom_call_target="tpu_custom_call" | custom-call | tf_op jit(solution)/shard_map/forecast/pallas_call | solution.py:447
  12.1 1.9 %collective-permute-start.2 = (f32[296,128]{1,0:T(8,128)S(1)}, f32[296,128]{1,0:T(8,128)S(1)}, u32[]{:S(2)}, u32[]{:S(2)}) collective-permute-start(f32[296,128]{1,0:T(8,128)S(1)} %get-tuple-element.18), channel_id=1, source_target_pairs={{0,4},{4,0},{8,12},{12,8},{16,20},{20,16},{24,28},{28,24},{1,5},{5... | collective-permute-start | bytes 454664 | tf_op jit(solution)/shard_map/ppermute | solution.py:363
  14.0 2.3 %collective-permute-start.3 = (f32[40,128]{1,0:T(8,128)S(1)}, f32[40,128]{1,0:T(8,128)S(1)}, u32[]{:S(2)}, u32[]{:S(2)}) collective-permute-start(f32[40,128]{1,0:T(8,128)S(1)} %get-tuple-element.17), channel_id=1, source_target_pairs={{0,16},{4,20},{8,24},{12,28},{16,0},{20,4},{24,8},{28,12},{1,17},{... | collective-permute-start | bytes 61448 | tf_op jit(solution)/shard_map/ppermute | solution.py:363
  16.3 0.7 %pad_maximum_fusion.5 = (f32[8,128]{1,0:T(8,128)}, f32[8,128]{1,0:T(8,128)}) fusion(f32[8,64]{1,0:T(8,128)S(1)} %get-tuple-element.29, f32[8,64]{1,0:T(8,128)S(1)} %get-tuple-element.28, f32[8,64]{1,0:T(8,128)S(1)} %get-tuple-element.27, f32[8,64]{1,0:T(8,128)S(1)} %get-tuple-element.26), kind=kLoop, calls=%fused_computation.13 | loop fusion | flops 2048 | bytes 16384 | tf_op jit(solution)/shard_map/concatenate | solution.py:62
  16.9 3.4 %all-to-all-start = ((f32[8,64,128]{2,1,0:T(8,128)}), f32[8,64,128]{2,1,0:T(8,128)S(1)}, u32[]{:S(2)}, u32[]{:S(2)}) async-start(f32[8,64,128]{2,1,0:T(8,128)} %get-tuple-element.16), calls=%async_computation | async-start | bytes 524288 | tf_op jit(solution)/shard_map/all_to_all | solution.py:469
  20.4 1.4 %collective-permute-start.4 = (f32[120,128]{1,0:T(8,128)S(1)}, f32[120,128]{1,0:T(8,128)S(1)}, u32[]{:S(2)}, u32[]{:S(2)}) collective-permute-start(f32[120,128]{1,0:T(8,128)S(1)} %pad_maximum_fusion.3.three_ref), channel_id=1, source_target_pairs={{0,8},{4,12},{8,0},{12,4},{16,24},{20,28},{24,16},{28,20},{1,9},{5... | collective-permute-start | bytes 184328 | tf_op jit(solution)/shard_map/ppermute | solution.py:363
  21.9 0.2 collective-permute-start.6
  22.0 2.3 %collective-permute-start.7 = (f32[128,128]{1,0:T(8,128)S(1)}, f32[128,128]{1,0:T(8,128)S(1)}, u32[]{:S(2)}, u32[]{:S(2)}) collective-permute-start(f32[128,128]{1,0:T(8,128)S(1)} %pad_maximum_fusion.1), channel_id=1, source_target_pairs={{0,16},{4,20},{8,24},{12,28},{16,0},{20,4},{24,8},{28,12},{1,17},{... | collective-permute-start | bytes 196616 | tf_op jit(solution)/shard_map/ppermute | solution.py:363
  24.3 1.2 %collective-permute-start.8 = (f32[128,128]{1,0:T(8,128)S(1)}, f32[128,128]{1,0:T(8,128)S(1)}, u32[]{:S(2)}, u32[]{:S(2)}) collective-permute-start(f32[128,128]{1,0:T(8,128)S(1)} %pad_maximum_fusion.2), channel_id=1, source_target_pairs={{0,24},{4,28},{8,16},{12,20},{16,8},{20,12},{24,0},{28,4},{1,25},{... | collective-permute-start | bytes 196616 | tf_op jit(solution)/shard_map/ppermute | solution.py:363
  25.5 1.3 %collective-permute-start.5 = (f32[80,128]{1,0:T(8,128)S(1)}, f32[80,128]{1,0:T(8,128)S(1)}, u32[]{:S(2)}, u32[]{:S(2)}) collective-permute-start(f32[80,128]{1,0:T(8,128)S(1)} %pad_maximum_fusion.4), channel_id=1, source_target_pairs={{0,4},{4,0},{8,12},{12,8},{16,20},{20,16},{24,28},{28,24},{1,5},{5... | collective-permute-start | bytes 122888 | tf_op jit(solution)/shard_map/ppermute | solution.py:363
  26.7 0.7 %pad_add_fusion.spot_ref.refs_1_ = s32[8,128]{1,0:T(8,128)} fusion(s32[8,64]{1,0:T(8,128)S(1)} %get-tuple-element.31, s32[8,64]{1,0:T(8,128)S(1)} %get-tuple-element.30), kind=kLoop, calls=%fused_computation.12 | loop fusion | flops 1024 | bytes 8192 | tf_op jit(solution)/shard_map/concatenate | solution.py:62
  27.4 1.2 %precision.1.refs_2_ = f32[2,8,128]{2,1,0:T(8,128)S(1)} custom-call(s32[8,128]{1,0:T(8,128)} %pad_add_fusion.spot_ref.refs_1_, f32[8,128]{1,0:T(8,128)} %get-tuple-element.32.damp_ref, f32[8,128]{1,0:T(8,128)} %get-tuple-element.33.live_ref, f32[32,128]{1,0:T(8,128)} %bitcast.27, f32[32,128]{1,0:T(8,128)} %bitcast.29, f32[104,512]{1,0:T(8,128)} %copy-done.1, ...), custom_call_target="tpu_custom_call" | custom-call | tf_op jit(solution)/shard_map/precision/pallas_call | solution.py:480
  28.7 2.8 %weights.1.mix_ref = f32[8,128]{1,0:T(8,128)S(1)} custom-call(f32[120,128]{1,0:T(8,128)S(1)} %pad_maximum_fusion.3.three_ref, f32[80,128]{1,0:T(8,128)S(1)} %collective-permute-done.5.last_ref, f32[120,128]{1,0:T(8,128)S(1)} %collective-permute-done.4.refs_0_, s32[8,128]{1,0:T(8,128)S(1)} %copy-done.7, f32[2,8,128]{2,1,0:T(8,128)S(1)} %precision.1.refs_2_), custom_call_target="tpu_custom_call" | custom-call | tf_op jit(solution)/shard_map/weights/pallas_call | solution.py:496
  31.5 0.5 %mix.1 = f32[8,4,8,512]{3,2,1,0:T(8,128)S(1)} custom-call(f32[512,128]{1,0:T(8,128)S(1)} %bitcast.21, f32[8,128]{1,0:T(8,128)S(1)} %weights.1.mix_ref, f32[64,128]{1,0:T(8,128)S(1)} %get-tuple-element.19.refs_0_, f32[296,128]{1,0:T(8,128)S(1)} %collective-permute-done.2.refs_1_, f32[128,128]{1,0:T(8,128)S(1)} %collective-permute-done.6.refs_2_, ...), custom_call_target="tpu_custom_call" | custom-call | tf_op jit(solution)/shard_map/mix/pallas_call | solution.py:505
  32.1 17.3 %all_to_all.10 = f32[8,4,8,512]{3,2,1,0:T(8,128)S(1)} all-to-all(f32[8,4,8,512]{3,2,1,0:T(8,128)S(1)} %mix.1), channel_id=1, replica_groups=mesh['member'=8,'tile'=4] {'member'}, dimensions={0} | all-to-all | bytes 1048576 | tf_op jit(solution)/shard_map/all_to_all | solution.py:514
  49.3 0.8 %copy_bitcast_fusion = f32[1,4,64,512]{3,2,1,0:T(8,128)} fusion(f32[8,4,8,512]{3,2,1,0:T(8,128)S(1)} %all_to_all.10), kind=kLoop, calls=%fused_computation | loop fusion | bytes 1048576 | tf_op jit(solution)/shard_map/reshape | solution.py:515
  (40 shorter events, 0.1 us)
Async XLA Ops:
  0.0 9.7 %copy-start = (f32[1,4,64,512]{3,2,1,0:T(8,128)S(1)}, f32[1,4,64,512]{3,2,1,0:T(8,128)}, u32[]{:S(2)}) copy-start(f32[1,4,64,512]{3,2,1,0:T(8,128)} %param.9) | copy-start | bytes 1572868
  0.0 9.7 %copy-start.3 = (f32[64,512]{1,0:T(8,128)S(1)}, f32[64,512]{1,0:T(8,128)}, u32[]{:S(2)}) copy-start(f32[64,512]{1,0:T(8,128)} %depth_ref.1) | copy-start | bytes 393220
  0.0 9.7 %copy-start.4 = (s32[64,512]{1,0:T(8,128)S(1)}, s32[64,512]{1,0:T(8,128)}, u32[]{:S(2)}) copy-start(s32[64,512]{1,0:T(8,128)} %mask_ref.1) | copy-start | bytes 393220
  1.2 4.6 %copy-start.8 = (s32[1,16,64]{2,1,0:T(8,128)S(1)}, s32[1,16,64]{2,1,0:T(8,128)}, u32[]{:S(2)}) copy-start(s32[1,16,64]{2,1,0:T(8,128)} %param.16) | copy-start | bytes 12292
  1.3 5.5 %collective-permute-start = (f32[104,512]{1,0:T(8,128)S(1)}, f32[104,512]{1,0:T(8,128)S(1)}, u32[]{:S(2)}, u32[]{:S(2)}) collective-permute-start(f32[104,512]{1,0:T(8,128)S(1)} %get-tuple-element.14), channel_id=1, source_target_pairs={{0,1},{2,3},{1,0},{3,2},{4,5},{6,7},{5,4},{7,6},{8,9},{10,11},{9,8... | collective-permute-start | bytes 638984 | tf_op jit(solution)/shard_map/ppermute | solution.py:390
  1.4 8.3 %collective-permute-start.1 = (f32[104,512]{1,0:T(8,128)S(1)}, f32[104,512]{1,0:T(8,128)S(1)}, u32[]{:S(2)}, u32[]{:S(2)}) collective-permute-start(f32[104,512]{1,0:T(8,128)S(1)} %get-tuple-element.15), channel_id=1, source_target_pairs={{1,2},{2,1},{5,6},{6,5},{9,10},{10,9},{13,14},{14,13},{17,18},{18,... | collective-permute-start | bytes 638984 | tf_op jit(solution)/shard_map/ppermute | solution.py:389
  6.0 0.7 %copy-start.9 = (s32[1,16]{1,0:T(1,128)S(1)}, s32[1,16]{1,0:T(1,128)}, u32[]{:S(2)}) copy-start(s32[1,16]{1,0:T(1,128)} %param.17) | copy-start | bytes 196
  6.0 3.7 %copy-start.6 = (f32[4096]{0:T(1024)S(1)}, f32[4096]{0:T(1024)}, u32[]{:S(2)}) copy-start(f32[4096]{0:T(1024)} %param.15) | copy-start | bytes 49156
  6.0 3.7 %copy-start.5 = (s32[4096]{0:T(1024)S(1)}, s32[4096]{0:T(1024)}, u32[]{:S(2)}) copy-start(s32[4096]{0:T(1024)} %param.12) | copy-start | bytes 49156
  6.7 5.4 %copy-start.1 = (f32[104,512]{1,0:T(8,128)}, f32[104,512]{1,0:T(8,128)S(1)}, u32[]{:S(2)}) copy-start(f32[104,512]{1,0:T(8,128)S(1)} %collective-permute-done.near_ref) | copy-start | bytes 638980
  9.7 2.4 %copy-start.2 = (f32[104,512]{1,0:T(8,128)}, f32[104,512]{1,0:T(8,128)S(1)}, u32[]{:S(2)}) copy-start(f32[104,512]{1,0:T(8,128)S(1)} %collective-permute-done.1.far_ref) | copy-start | bytes 638980
  12.1 8.3 %collective-permute-start.2 = (f32[296,128]{1,0:T(8,128)S(1)}, f32[296,128]{1,0:T(8,128)S(1)}, u32[]{:S(2)}, u32[]{:S(2)}) collective-permute-start(f32[296,128]{1,0:T(8,128)S(1)} %get-tuple-element.18), channel_id=1, source_target_pairs={{0,4},{4,0},{8,12},{12,8},{16,20},{20,16},{24,28},{28,24},{1,5},{5... | collective-permute-start | bytes 454664 | tf_op jit(solution)/shard_map/ppermute | solution.py:363
  14.0 6.4 %collective-permute-start.3 = (f32[40,128]{1,0:T(8,128)S(1)}, f32[40,128]{1,0:T(8,128)S(1)}, u32[]{:S(2)}, u32[]{:S(2)}) collective-permute-start(f32[40,128]{1,0:T(8,128)S(1)} %get-tuple-element.17), channel_id=1, source_target_pairs={{0,16},{4,20},{8,24},{12,28},{16,0},{20,4},{24,8},{28,12},{1,17},{... | collective-permute-start | bytes 61448 | tf_op jit(solution)/shard_map/ppermute | solution.py:363
  16.9 14.6 %all-to-all-start = ((f32[8,64,128]{2,1,0:T(8,128)}), f32[8,64,128]{2,1,0:T(8,128)S(1)}, u32[]{:S(2)}, u32[]{:S(2)}) async-start(f32[8,64,128]{2,1,0:T(8,128)} %get-tuple-element.16), calls=%async_computation | async-start | bytes 524288 | tf_op jit(solution)/shard_map/all_to_all | solution.py:469
  20.4 5.1 %collective-permute-start.4 = (f32[120,128]{1,0:T(8,128)S(1)}, f32[120,128]{1,0:T(8,128)S(1)}, u32[]{:S(2)}, u32[]{:S(2)}) collective-permute-start(f32[120,128]{1,0:T(8,128)S(1)} %pad_maximum_fusion.3.three_ref), channel_id=1, source_target_pairs={{0,8},{4,12},{8,0},{12,4},{16,24},{20,28},{24,16},{28,20},{1,9},{5... | collective-permute-start | bytes 184328 | tf_op jit(solution)/shard_map/ppermute | solution.py:363
  21.9 9.6 %collective-permute-start.6 = (f32[128,128]{1,0:T(8,128)S(1)}, f32[128,128]{1,0:T(8,128)S(1)}, u32[]{:S(2)}, u32[]{:S(2)}) collective-permute-start(f32[128,128]{1,0:T(8,128)S(1)} %pad_maximum_fusion), channel_id=1, source_target_pairs={{0,8},{4,12},{8,0},{12,4},{16,24},{20,28},{24,16},{28,20},{1,9},{5... | collective-permute-start | bytes 196616 | tf_op jit(solution)/shard_map/ppermute | solution.py:363
  22.0 9.5 %collective-permute-start.7 = (f32[128,128]{1,0:T(8,128)S(1)}, f32[128,128]{1,0:T(8,128)S(1)}, u32[]{:S(2)}, u32[]{:S(2)}) collective-permute-start(f32[128,128]{1,0:T(8,128)S(1)} %pad_maximum_fusion.1), channel_id=1, source_target_pairs={{0,16},{4,20},{8,24},{12,28},{16,0},{20,4},{24,8},{28,12},{1,17},{... | collective-permute-start | bytes 196616 | tf_op jit(solution)/shard_map/ppermute | solution.py:363
  24.3 7.2 %collective-permute-start.8 = (f32[128,128]{1,0:T(8,128)S(1)}, f32[128,128]{1,0:T(8,128)S(1)}, u32[]{:S(2)}, u32[]{:S(2)}) collective-permute-start(f32[128,128]{1,0:T(8,128)S(1)} %pad_maximum_fusion.2), channel_id=1, source_target_pairs={{0,24},{4,28},{8,16},{12,20},{16,8},{20,12},{24,0},{28,4},{1,25},{... | collective-permute-start | bytes 196616 | tf_op jit(solution)/shard_map/ppermute | solution.py:363
  25.5 3.2 %collective-permute-start.5 = (f32[80,128]{1,0:T(8,128)S(1)}, f32[80,128]{1,0:T(8,128)S(1)}, u32[]{:S(2)}, u32[]{:S(2)}) collective-permute-start(f32[80,128]{1,0:T(8,128)S(1)} %pad_maximum_fusion.4), channel_id=1, source_target_pairs={{0,4},{4,0},{8,12},{12,8},{16,20},{20,16},{24,28},{28,24},{1,5},{5... | collective-permute-start | bytes 122888 | tf_op jit(solution)/shard_map/ppermute | solution.py:363
  27.4 1.3 %copy-start.7 = (s32[8,128]{1,0:T(8,128)S(1)}, s32[8,128]{1,0:T(8,128)}, u32[]{:S(2)}) copy-start(s32[8,128]{1,0:T(8,128)} %pad_add_fusion.spot_ref.refs_1_) | copy-start | bytes 12292

commit v9 on v8

--- a/solution.py
+++ b/solution.py
@@ -222,13 +222,27 @@
 
 
 def precision_kernel(
-    halo, spot_ref, damp_ref, live_ref, value_ref, error_ref, near_ref, far_ref, out_ref, value_win, error_win
+    sizes, list_ref, count_ref, value_ref, error_ref, near_ref, far_ref, out_ref, spot_ref, value_win, error_win
 ):
+    halo, rows, width, radius = sizes
     window = value_win.shape[0]
+    per_dev, slots = list_ref.shape
+    obs_tile = value_ref.shape[0] * LANES
     even = lax.axis_index("tile") % 2 == 0
     window_parts(value_win, value_ref[...], near_ref, far_ref, 6 * halo, 2, even)
     window_parts(error_win, error_ref[...], near_ref, far_ref, 6 * halo, 3, even)
-    spot = spot_ref[...]
+    named = list_ref[...]
+    patch = iota((per_dev, slots), 0)
+    row_index = (lax.axis_index("member") * per_dev + patch) * REGION_POINTS // width
+    dist = (named - (obs_tile + row_index * obs_tile // rows)).astype(jnp.float32) / radius
+    counts = jnp.zeros((per_dev, slots), jnp.int32)
+    for p in range(per_dev):
+        counts = jnp.where(patch == p, count_ref[0, p], counts)
+    live = jnp.where(iota((per_dev, slots), 1) < counts, 1.0, 0.0)
+    live = side_by_side(live, per_dev // 2)
+    damp = side_by_side(1.0 + 4.0 * dist * dist, per_dev // 2)
+    spot = side_by_side(named - (obs_tile - radius), per_dev // 2)
+    spot_ref[...] = spot
     row, lane = spot // LANES, spot % LANES
     value = jnp.zeros(spot.shape, jnp.float32)
     error = jnp.zeros(spot.shape, jnp.float32)
@@ -239,7 +253,7 @@
         line = jnp.broadcast_to(error_win[r : r + 1, :], spot.shape)
         error = jnp.where(hit, jnp.take_along_axis(line, lane, axis=1, mode="promise_in_bounds"), error)
     out_ref[0] = value
-    out_ref[1] = jnp.where(live_ref[...] > 0.0, 1.0 / (damp_ref[...] * error), 0.0)
+    out_ref[1] = jnp.where(live > 0.0, 1.0 / (damp * error), 0.0)
 
 
 def weight_kernel(members, three_ref, last_ref, *refs):
@@ -470,24 +484,16 @@
     three, last, near_equivs, rest = trade_blocks(equiv, across, along)
     received = received.reshape(members * packet, LANES)
 
-    patch_index = lax.axis_index("member") * per_dev + jnp.arange(per_dev, dtype=jnp.int32)
-    row_index = patch_index * REGION_POINTS // width
-    centre = obs_tile + row_index * obs_tile // rows
-    dist = (obs_list[0] - centre[:, None]).astype(jnp.float32) / radius
-    damp = 1.0 + 4.0 * dist * dist
-    live = jnp.arange(slots, dtype=jnp.int32)[None, :] < obs_count[0][:, None]
-    spot = side_by_side(obs_list[0] - (obs_tile - radius), pairs)
-    known = pl.pallas_call(
-        functools.partial(precision_kernel, halo),
-        out_shape=pltpu.VMEM((2, pairs, LANES), jnp.float32),
-        in_specs=vmem_specs(7),
-        out_specs=vmem_specs(1)[0],
+    known, spot = pl.pallas_call(
+        functools.partial(precision_kernel, (halo, rows, width, radius)),
+        out_shape=[pltpu.VMEM((2, pairs, LANES), jnp.float32), pltpu.VMEM((pairs, LANES), jnp.int32)],
+        in_specs=vmem_specs(1) + [pl.BlockSpec(memory_space=pltpu.SMEM)] + vmem_specs(4),
+        out_specs=vmem_specs(2),
         scratch_shapes=[pltpu.VMEM((window, LANES), jnp.float32)] * 2,
         name="precision",
     )(
-        spot,
-        side_by_side(damp, pairs),
-        side_by_side(live.astype(jnp.float32), pairs),
+        obs_list[0],
+        obs_count,
         obs_value.reshape(panel),
         obs_error.reshape(panel),
         near,

time: 50.5 us -> 49.7 us (0.984)
  other arithmetic: 1.53 us -> 0.03 us
  waiting for transfers between devices: 2.97 us -> 4.24 us
  local copies, waits for them, and re-layouts: 1.53 us -> 0.88 us
    concatenate x2 -> x0, other arithmetic: 1.33 us -> none  [side_by_side(): return jnp.concatenate([x[:pairs], x[pairs:]], axis=1)]
    ppermute x1, waiting for transfers between devices: 2.94 us -> 3.79 us  [swaps(): far = lax.ppermute(far, 'tile', pairs(1))]
    unnamed x20 -> x14, local copies, waits for them, and re-layouts: 0.68 us -> 0.03 us
  transfers between devices with their start and end apart: 10 -> 10, of which waited for: 1 -> 2; matrix products, arithmetic and copies ran while one was open for 3% -> 0% of each run, Pallas kernels for 8% -> 8%
where the time goes in v9:
time: 49.7 us; the launch traced here: 49.4 us
  starting transfers between devices  18.4 us (37%)
  blocking collectives  17.3 us (35%)
  Pallas kernels  8.26 us (17%)
  waiting for transfers between devices  4.24 us (9%)
  local copies, waits for them, and re-layouts  0.88 us (2%)
    all_to_all x1, blocking collectives, body(): lax.all_to_all(analysed, 'member', split_axis=0, concat_axis=0, tiled=True)  17.3 us
    ppermute x7, starting transfers between devices, trade(): lax.ppermute(block, 'member', [(i, i ^ distance) for i in range(members)])  10.4 us
    ppermute x1, starting transfers between devices, swaps(): far = lax.ppermute(far, 'tile', pairs(1))  4.48 us
    ppermute x1, waiting for transfers between devices, swaps(): far = lax.ppermute(far, 'tile', pairs(1))  3.79 us
    all_to_all x1, starting transfers between devices, body(): lax.all_to_all(sends, 'member', split_axis=0, concat_axis=0, tiled=True)  3.41 us
    pallas_call x1, Pallas kernels, body(): pl.pallas_call(functools.partial(weight_kernel, members), out_shape=jax.S...  2.8 us
    pallas_call x1, Pallas kernels, body(): pl.pallas_call(functools.partial(forecast_kernel, (members, own_rows, hal...  2.41 us
    pallas_call x1, Pallas kernels, body(): pl.pallas_call(functools.partial(precision_kernel, (halo, rows, width, ra...  1.32 us
  transfers between devices with their start and end apart: 10, of which 2 were waited for; matrix products, arithmetic and copies ran while one was open for 0% of the time, Pallas kernels for 8%

profile of v9, /device:TPU:1, one launch (start us, length us, event | category | flops | bytes accessed | tf_op | source)
XLA Modules:
  0.0 49.4 jit_solution(5175488736087732510)
XLA Ops:
  0.0 1.2 %edges.1 = (f32[104,512]{1,0:T(8,128)S(1)}, f32[104,512]{1,0:T(8,128)S(1)}) custom-call(f32[4,64,512]{2,1,0:T(8,128)} %bitcast.12, f32[64,512]{1,0:T(8,128)} %depth_ref.1, s32[64,512]{1,0:T(8,128)} %mask_ref.1, s32[32,128]{1,0:T(8,128)} %bitcast.15, f32[32,128]{1,0:T(8,128)} %bitcast.17, f32[32,128]{1,0:T(8,128)} %bitcast.19, f32[32,128]{1,0:T(8,128)} %bitcast.21), custom_call_target="tpu_custom_call" | custom-call | tf_op jit(solution)/shard_map/edges/pallas_call | solution.py:434
  1.2 0.1 collective-permute-start
  1.4 4.5 %collective-permute-start.1 = (f32[104,512]{1,0:T(8,128)S(1)}, f32[104,512]{1,0:T(8,128)S(1)}, u32[]{:S(2)}, u32[]{:S(2)}) collective-permute-start(f32[104,512]{1,0:T(8,128)S(1)} %get-tuple-element.17), channel_id=1, source_target_pairs={{1,2},{2,1},{5,6},{6,5},{9,10},{10,9},{13,14},{14,13},{17,18},{18,... | collective-permute-start | bytes 638984 | tf_op jit(solution)/shard_map/ppermute | solution.py:403
  5.8 0.0 collective-permute-done.near_ref
  5.9 3.8 %collective-permute-done.1.far_ref = f32[104,512]{1,0:T(8,128)S(1)} collective-permute-done((f32[104,512]{1,0:T(8,128)S(1)}, f32[104,512]{1,0:T(8,128)S(1)}, u32[]{:S(2)}, u32[]{:S(2)}) %collective-permute-start.1) | collective-permute-done | bytes 213024 | tf_op jit(solution)/shard_map/ppermute | solution.py:403
  9.7 2.4 %forecast.1 = (f32[8,64,128]{2,1,0:T(8,128)}, f32[40,128]{1,0:T(8,128)S(1)}, f32[296,128]{1,0:T(8,128)S(1)}, f32[64,128]{1,0:T(8,128)S(1)}, f32[64,128]{1,0:T(8,...) custom-call(f32[4,64,512]{2,1,0:T(8,128)S(1)} %bitcast.13, f32[64,512]{1,0:T(8,128)S(1)} %copy-done.3, ...), custom_call_target="tpu_custom_call" | custom-call | tf_op jit(solution)/shard_map/forecast/pallas_call | solution.py:461
  12.1 1.9 %collective-permute-start.2 = (f32[296,128]{1,0:T(8,128)S(1)}, f32[296,128]{1,0:T(8,128)S(1)}, u32[]{:S(2)}, u32[]{:S(2)}) collective-permute-start(f32[296,128]{1,0:T(8,128)S(1)} %get-tuple-element.20), channel_id=1, source_target_pairs={{0,4},{4,0},{8,12},{12,8},{16,20},{20,16},{24,28},{28,24},{1,5},{5... | collective-permute-start | bytes 454664 | tf_op jit(solution)/shard_map/ppermute | solution.py:377
  14.0 2.3 %collective-permute-start.3 = (f32[40,128]{1,0:T(8,128)S(1)}, f32[40,128]{1,0:T(8,128)S(1)}, u32[]{:S(2)}, u32[]{:S(2)}) collective-permute-start(f32[40,128]{1,0:T(8,128)S(1)} %get-tuple-element.19), channel_id=1, source_target_pairs={{0,16},{4,20},{8,24},{12,28},{16,0},{20,4},{24,8},{28,12},{1,17},{... | collective-permute-start | bytes 61448 | tf_op jit(solution)/shard_map/ppermute | solution.py:377
  16.3 3.4 %all-to-all-start = ((f32[8,64,128]{2,1,0:T(8,128)}), f32[8,64,128]{2,1,0:T(8,128)S(1)}, u32[]{:S(2)}, u32[]{:S(2)}) async-start(f32[8,64,128]{2,1,0:T(8,128)} %get-tuple-element.18), calls=%async_computation | async-start | bytes 524288 | tf_op jit(solution)/shard_map/all_to_all | solution.py:483
  19.7 0.0 collective-permute-done.2.refs_1_
  19.7 0.0 collective-permute-done.3
  19.7 1.4 %collective-permute-start.4 = (f32[120,128]{1,0:T(8,128)S(1)}, f32[120,128]{1,0:T(8,128)S(1)}, u32[]{:S(2)}, u32[]{:S(2)}) collective-permute-start(f32[120,128]{1,0:T(8,128)S(1)} %pad_maximum_fusion.3.three_ref), channel_id=1, source_target_pairs={{0,8},{4,12},{8,0},{12,4},{16,24},{20,28},{24,16},{28,20},{1,9},{5... | collective-permute-start | bytes 184328 | tf_op jit(solution)/shard_map/ppermute | solution.py:377
  21.2 0.2 collective-permute-start.6
  21.4 2.3 %collective-permute-start.7 = (f32[128,128]{1,0:T(8,128)S(1)}, f32[128,128]{1,0:T(8,128)S(1)}, u32[]{:S(2)}, u32[]{:S(2)}) collective-permute-start(f32[128,128]{1,0:T(8,128)S(1)} %pad_maximum_fusion.1), channel_id=1, source_target_pairs={{0,16},{4,20},{8,24},{12,28},{16,0},{20,4},{24,8},{28,12},{1,17},{... | collective-permute-start | bytes 196616 | tf_op jit(solution)/shard_map/ppermute | solution.py:377
  23.6 1.2 %collective-permute-start.8 = (f32[128,128]{1,0:T(8,128)S(1)}, f32[128,128]{1,0:T(8,128)S(1)}, u32[]{:S(2)}, u32[]{:S(2)}) collective-permute-start(f32[128,128]{1,0:T(8,128)S(1)} %pad_maximum_fusion.2), channel_id=1, source_target_pairs={{0,24},{4,28},{8,16},{12,20},{16,8},{20,12},{24,0},{28,4},{1,25},{... | collective-permute-start | bytes 196616 | tf_op jit(solution)/shard_map/ppermute | solution.py:377
  24.8 1.3 %collective-permute-start.5 = (f32[80,128]{1,0:T(8,128)S(1)}, f32[80,128]{1,0:T(8,128)S(1)}, u32[]{:S(2)}, u32[]{:S(2)}) collective-permute-start(f32[80,128]{1,0:T(8,128)S(1)} %pad_maximum_fusion.4), channel_id=1, source_target_pairs={{0,4},{4,0},{8,12},{12,8},{16,20},{20,16},{24,28},{28,24},{1,5},{5... | collective-permute-start | bytes 122888 | tf_op jit(solution)/shard_map/ppermute | solution.py:377
  26.1 1.3 %precision.1 = (f32[2,8,128]{2,1,0:T(8,128)S(1)}, s32[8,128]{1,0:T(8,128)S(1)}) custom-call(s32[16,64]{1,0:T(8,128)} %bitcast.23, s32[1,16]{1,0:T(1,128)} %count_ref.1, f32[32,128]{1,0:T(8,128)} %bitcast.20, f32[32,128]{1,0:T(8,128)} %bitcast.22, f32[104,512]{1,0:T(8,128)} %copy-done.1, f32[104,512]{1,0:T(8,128)} %copy-done.2), custom_call_target="tpu_custom_call" | custom-call | tf_op jit(solution)/shard_map/precision/pallas_call | solution.py:487
  27.4 0.4 collective-permute-done.5.last_ref
  27.8 2.8 %weights.1.mix_ref = f32[8,128]{1,0:T(8,128)S(1)} custom-call(f32[120,128]{1,0:T(8,128)S(1)} %pad_maximum_fusion.3.three_ref, f32[80,128]{1,0:T(8,128)S(1)} %collective-permute-done.5.last_ref, f32[120,128]{1,0:T(8,128)S(1)} %collective-permute-done.4.refs_0_, s32[8,128]{1,0:T(8,128)S(1)} %get-tuple-element.21.refs_1_, ...), custom_call_target="tpu_custom_call" | custom-call | tf_op jit(solution)/shard_map/weights/pallas_call | solution.py:502
  30.6 0.0 collective-permute-done.6.refs_2_
  30.6 0.0 collective-permute-done.7.refs_3_
  30.7 0.5 %mix.1 = f32[8,4,8,512]{3,2,1,0:T(8,128)S(1)} custom-call(f32[512,128]{1,0:T(8,128)S(1)} %bitcast.14, f32[8,128]{1,0:T(8,128)S(1)} %weights.1.mix_ref, f32[64,128]{1,0:T(8,128)S(1)} %get-tuple-element.23.refs_0_, f32[296,128]{1,0:T(8,128)S(1)} %collective-permute-done.2.refs_1_, f32[128,128]{1,0:T(8,128)S(1)} %collective-permute-done.6.refs_2_, ...), custom_call_target="tpu_custom_call" | custom-call | tf_op jit(solution)/shard_map/mix/pallas_call | solution.py:511
  31.2 17.3 %all_to_all.10 = f32[8,4,8,512]{3,2,1,0:T(8,128)S(1)} all-to-all(f32[8,4,8,512]{3,2,1,0:T(8,128)S(1)} %mix.1), channel_id=1, replica_groups=mesh['member'=8,'tile'=4] {'member'}, dimensions={0} | all-to-all | bytes 1048576 | tf_op jit(solution)/shard_map/all_to_all | solution.py:520
  48.5 0.8 %copy_bitcast_fusion = f32[1,4,64,512]{3,2,1,0:T(8,128)} fusion(f32[8,4,8,512]{3,2,1,0:T(8,128)S(1)} %all_to_all.10), kind=kLoop, calls=%fused_computation | loop fusion | bytes 1048576 | tf_op jit(solution)/shard_map/reshape | solution.py:521
  (25 shorter events, 0.1 us)
Async XLA Ops:
  0.0 9.7 %copy-start = (f32[1,4,64,512]{3,2,1,0:T(8,128)S(1)}, f32[1,4,64,512]{3,2,1,0:T(8,128)}, u32[]{:S(2)}) copy-start(f32[1,4,64,512]{3,2,1,0:T(8,128)} %param.9) | copy-start | bytes 1572868
  0.0 9.7 %copy-start.3 = (f32[64,512]{1,0:T(8,128)S(1)}, f32[64,512]{1,0:T(8,128)}, u32[]{:S(2)}) copy-start(f32[64,512]{1,0:T(8,128)} %depth_ref.1) | copy-start | bytes 393220
  0.0 9.7 %copy-start.4 = (s32[64,512]{1,0:T(8,128)S(1)}, s32[64,512]{1,0:T(8,128)}, u32[]{:S(2)}) copy-start(s32[64,512]{1,0:T(8,128)} %mask_ref.1) | copy-start | bytes 393220
  0.0 9.7 %copy-start.5 = (s32[4096]{0:T(1024)S(1)}, s32[4096]{0:T(1024)}, u32[]{:S(2)}) copy-start(s32[4096]{0:T(1024)} %param.12) | copy-start | bytes 49156
  0.0 9.7 %copy-start.6 = (f32[4096]{0:T(1024)S(1)}, f32[4096]{0:T(1024)}, u32[]{:S(2)}) copy-start(f32[4096]{0:T(1024)} %param.15) | copy-start | bytes 49156
  1.2 4.6 %collective-permute-start = (f32[104,512]{1,0:T(8,128)S(1)}, f32[104,512]{1,0:T(8,128)S(1)}, u32[]{:S(2)}, u32[]{:S(2)}) collective-permute-start(f32[104,512]{1,0:T(8,128)S(1)} %get-tuple-element.16), channel_id=1, source_target_pairs={{0,1},{2,3},{1,0},{3,2},{4,5},{6,7},{5,4},{7,6},{8,9},{10,11},{9,8... | collective-permute-start | bytes 638984 | tf_op jit(solution)/shard_map/ppermute | solution.py:404
  1.4 8.3 %collective-permute-start.1 = (f32[104,512]{1,0:T(8,128)S(1)}, f32[104,512]{1,0:T(8,128)S(1)}, u32[]{:S(2)}, u32[]{:S(2)}) collective-permute-start(f32[104,512]{1,0:T(8,128)S(1)} %get-tuple-element.17), channel_id=1, source_target_pairs={{1,2},{2,1},{5,6},{6,5},{9,10},{10,9},{13,14},{14,13},{17,18},{18,... | collective-permute-start | bytes 638984 | tf_op jit(solution)/shard_map/ppermute | solution.py:403
  5.9 6.2 %copy-start.1 = (f32[104,512]{1,0:T(8,128)}, f32[104,512]{1,0:T(8,128)S(1)}, u32[]{:S(2)}) copy-start(f32[104,512]{1,0:T(8,128)S(1)} %collective-permute-done.near_ref) | copy-start | bytes 638980
  9.7 2.4 %copy-start.2 = (f32[104,512]{1,0:T(8,128)}, f32[104,512]{1,0:T(8,128)S(1)}, u32[]{:S(2)}) copy-start(f32[104,512]{1,0:T(8,128)S(1)} %collective-permute-done.1.far_ref) | copy-start | bytes 638980
  12.1 7.6 %collective-permute-start.2 = (f32[296,128]{1,0:T(8,128)S(1)}, f32[296,128]{1,0:T(8,128)S(1)}, u32[]{:S(2)}, u32[]{:S(2)}) collective-permute-start(f32[296,128]{1,0:T(8,128)S(1)} %get-tuple-element.20), channel_id=1, source_target_pairs={{0,4},{4,0},{8,12},{12,8},{16,20},{20,16},{24,28},{28,24},{1,5},{5... | collective-permute-start | bytes 454664 | tf_op jit(solution)/shard_map/ppermute | solution.py:377
  14.0 5.8 %collective-permute-start.3 = (f32[40,128]{1,0:T(8,128)S(1)}, f32[40,128]{1,0:T(8,128)S(1)}, u32[]{:S(2)}, u32[]{:S(2)}) collective-permute-start(f32[40,128]{1,0:T(8,128)S(1)} %get-tuple-element.19), channel_id=1, source_target_pairs={{0,16},{4,20},{8,24},{12,28},{16,0},{20,4},{24,8},{28,12},{1,17},{... | collective-permute-start | bytes 61448 | tf_op jit(solution)/shard_map/ppermute | solution.py:377
  16.3 14.4 %all-to-all-start = ((f32[8,64,128]{2,1,0:T(8,128)}), f32[8,64,128]{2,1,0:T(8,128)S(1)}, u32[]{:S(2)}, u32[]{:S(2)}) async-start(f32[8,64,128]{2,1,0:T(8,128)} %get-tuple-element.18), calls=%async_computation | async-start | bytes 524288 | tf_op jit(solution)/shard_map/all_to_all | solution.py:483
  19.7 5.1 %collective-permute-start.4 = (f32[120,128]{1,0:T(8,128)S(1)}, f32[120,128]{1,0:T(8,128)S(1)}, u32[]{:S(2)}, u32[]{:S(2)}) collective-permute-start(f32[120,128]{1,0:T(8,128)S(1)} %pad_maximum_fusion.3.three_ref), channel_id=1, source_target_pairs={{0,8},{4,12},{8,0},{12,4},{16,24},{20,28},{24,16},{28,20},{1,9},{5... | collective-permute-start | bytes 184328 | tf_op jit(solution)/shard_map/ppermute | solution.py:377
  21.2 9.5 %collective-permute-start.6 = (f32[128,128]{1,0:T(8,128)S(1)}, f32[128,128]{1,0:T(8,128)S(1)}, u32[]{:S(2)}, u32[]{:S(2)}) collective-permute-start(f32[128,128]{1,0:T(8,128)S(1)} %pad_maximum_fusion), channel_id=1, source_target_pairs={{0,8},{4,12},{8,0},{12,4},{16,24},{20,28},{24,16},{28,20},{1,9},{5... | collective-permute-start | bytes 196616 | tf_op jit(solution)/shard_map/ppermute | solution.py:377
  21.4 9.3 %collective-permute-start.7 = (f32[128,128]{1,0:T(8,128)S(1)}, f32[128,128]{1,0:T(8,128)S(1)}, u32[]{:S(2)}, u32[]{:S(2)}) collective-permute-start(f32[128,128]{1,0:T(8,128)S(1)} %pad_maximum_fusion.1), channel_id=1, source_target_pairs={{0,16},{4,20},{8,24},{12,28},{16,0},{20,4},{24,8},{28,12},{1,17},{... | collective-permute-start | bytes 196616 | tf_op jit(solution)/shard_map/ppermute | solution.py:377
  23.6 7.0 %collective-permute-start.8 = (f32[128,128]{1,0:T(8,128)S(1)}, f32[128,128]{1,0:T(8,128)S(1)}, u32[]{:S(2)}, u32[]{:S(2)}) collective-permute-start(f32[128,128]{1,0:T(8,128)S(1)} %pad_maximum_fusion.2), channel_id=1, source_target_pairs={{0,24},{4,28},{8,16},{12,20},{16,8},{20,12},{24,0},{28,4},{1,25},{... | collective-permute-start | bytes 196616 | tf_op jit(solution)/shard_map/ppermute | solution.py:377
  24.8 3.0 %collective-permute-start.5 = (f32[80,128]{1,0:T(8,128)S(1)}, f32[80,128]{1,0:T(8,128)S(1)}, u32[]{:S(2)}, u32[]{:S(2)}) collective-permute-start(f32[80,128]{1,0:T(8,128)S(1)} %pad_maximum_fusion.4), channel_id=1, source_target_pairs={{0,4},{4,0},{8,12},{12,8},{16,20},{20,16},{24,28},{28,24},{1,5},{5... | collective-permute-start | bytes 122888 | tf_op jit(solution)/shard_map/ppermute | solution.py:377

commit v10 on v9

--- a/solution.py
+++ b/solution.py
@@ -22,7 +22,6 @@
 HIGH = lax.Precision.HIGHEST
 
 PAD = 8
-PACKED = 2
 
 
 def iota(shape, dim):
@@ -85,8 +84,8 @@
 ):
     members, own_rows, halo, obs_halo = sizes
     half = members // 2
-    out_ref, equiv_ref, across_ref = refs[:3]
-    along_refs, scratch = refs[3 : half + 3], refs[half + 3 :]
+    equiv_ref, across_ref = refs[:2]
+    along_refs, scratch = refs[2 : half + 2], refs[half + 2 :]
     s_ref, u_ref, v_ref, e_ref, h_ref, w_ref, flux_ref, part_ref, cell_win, gain_win = scratch
     even = lax.axis_index("tile") % 2 == 0
     rows, width = depth_ref.shape
@@ -192,19 +191,14 @@
 
     me = lax.axis_index("member")
     for j in range(members):
-        source = first + j * own_rows
-        for i in range(PACKED):
+        source = pl.multiple_of(first + (me ^ j) * own_rows, min(own_rows, 8))
+        for i in range(4):
             for q in range(pieces):
                 target = (i * pieces + q) * own_rows
-                block = fields[i][q, source : source + own_rows, :]
-                out_ref[j, target : target + own_rows, :] = block if i else block * (1.0 / PRESSURE)
-        source = pl.multiple_of(first + (me ^ j) * own_rows, min(own_rows, 8))
-        for i in range(PACKED, 4):
-            for q in range(pieces):
-                target = ((i - PACKED) * pieces + q) * own_rows
                 block = fields[i][q, pl.ds(source, own_rows), :]
+                block = block if i else block * (1.0 / PRESSURE)
                 if j % 2:
-                    target += j // 2 * (4 - PACKED) * pieces * own_rows
+                    target += j // 2 * 4 * pieces * own_rows
                     across_ref[target : target + own_rows, :] = block
                 else:
                     along_refs[j // 2][target : target + own_rows, :] = block
@@ -334,15 +328,13 @@
     mix_ref[...] = mix
 
 
-def mix_kernel(sizes, recv_ref, mix_ref, *refs):
+def mix_kernel(sizes, mix_ref, *refs):
     members, own_rows, pieces = sizes
     half = members // 2
-    rest_refs, (out_ref, table_ref) = refs[: half + 1], refs[half + 1 :]
-    rest_rows = (4 - PACKED) * pieces * own_rows
-    stride = recv_ref.shape[0] // members
+    block_refs, (out_ref, table_ref) = refs[: half + 1], refs[half + 1 :]
+    block_rows = 4 * pieces * own_rows
     me = lax.axis_index("member")
     table_ref[...] = mix_ref[...].T
-    bases = [pl.multiple_of((me ^ d) * stride, 8) for d in range(members)]
 
     def analyse(m, carry):
         for side in range(2):
@@ -352,14 +344,8 @@
                 for q in range(side * pieces // 2, (side + 1) * pieces // 2):
                     total = None
                     for d in range(members):
-                        if i < PACKED:
-                            start = (i * pieces + q) * own_rows
-                            block = recv_ref[pl.ds(bases[d] + start, own_rows), :]
-                        else:
-                            start = ((i - PACKED) * pieces + q) * own_rows
-                            if d >= 2:
-                                start += d % 2 * rest_rows
-                            block = rest_refs[d if d < 2 else d // 2 + 1][start : start + own_rows, :]
+                        start = (i * pieces + q) * own_rows + (d % 2 * block_rows if d >= 2 else 0)
+                        block = block_refs[d if d < 2 else d // 2 + 1][start : start + own_rows, :]
                         term = columns[d] * block
                         total = term if total is None else total + term
                     out_ref[me ^ m, i, :, q * LANES : (q + 1) * LANES] = total
@@ -454,20 +440,18 @@
     near, far = swaps(*edges)
 
     window = (obs_tile + 2 * radius) // LANES
-    packet = PACKED * pieces * own_rows
     grid = (pieces, rows + 2 * halo + 2 * PAD, LANES)
     half = members // 2
-    rest_rows = (4 - PACKED) * pieces * own_rows
-    sends, equiv, across, *along = pl.pallas_call(
+    block_rows = 4 * pieces * own_rows
+    equiv, across, *along = pl.pallas_call(
         functools.partial(forecast_kernel, (members, own_rows, halo, radius)),
         out_shape=[
-            pltpu.VMEM((members, packet, LANES), jnp.float32),
             jax.ShapeDtypeStruct((window, LANES), jnp.float32),
-            jax.ShapeDtypeStruct((half * rest_rows + window, LANES), jnp.float32),
+            jax.ShapeDtypeStruct((half * block_rows + window, LANES), jnp.float32),
         ]
-        + [jax.ShapeDtypeStruct((rest_rows, LANES), jnp.float32)] * half,
+        + [jax.ShapeDtypeStruct((block_rows, LANES), jnp.float32)] * half,
         in_specs=vmem_specs(7),
-        out_specs=vmem_specs(3 + half),
+        out_specs=vmem_specs(2 + half),
         scratch_shapes=[pltpu.VMEM(grid, jnp.float32)] * 8 + [pltpu.VMEM((window, LANES), jnp.float32)] * 2,
         compiler_params=pltpu.CompilerParams(vmem_limit_bytes=24 * 2**20),
         name="forecast",
@@ -480,9 +464,7 @@
         near,
         far,
     )
-    received = lax.all_to_all(sends, "member", split_axis=0, concat_axis=0, tiled=True)
-    three, last, near_equivs, rest = trade_blocks(equiv, across, along)
-    received = received.reshape(members * packet, LANES)
+    three, last, near_equivs, blocks = trade_blocks(equiv, across, along)
 
     known, spot = pl.pallas_call(
         functools.partial(precision_kernel, (halo, rows, width, radius)),
@@ -511,12 +493,12 @@
     analysed = pl.pallas_call(
         functools.partial(mix_kernel, (members, own_rows, pieces)),
         out_shape=jax.ShapeDtypeStruct((members, 4, own_rows, width), jnp.float32),
-        in_specs=vmem_specs(3 + half),
+        in_specs=vmem_specs(2 + half),
         out_specs=vmem_specs(1)[0],
         scratch_shapes=[pltpu.VMEM((LANES, members), jnp.float32)],
         compiler_params=pltpu.CompilerParams(vmem_limit_bytes=24 * 2**20),
         name="mix",
-    )(received, mix, *rest)
+    )(mix, *blocks)
     result = lax.all_to_all(analysed, "member", split_axis=0, concat_axis=0, tiled=True)
     return jnp.transpose(result, (1, 0, 2, 3)).reshape(1, 4, rows, width)
 

time: 49.7 us -> 52.7 us (1.060)
  the two profiles are of different devices: /device:TPU:1 before, /device:TPU:2 now
where the time goes in v10:
time: 52.7 us; the launch traced here: 52.5 us
  blocking collectives  19.2 us (36%)
  starting transfers between devices  15.3 us (29%)
  waiting for transfers between devices  9.08 us (17%)
  Pallas kernels  7.71 us (15%)
  local copies, waits for them, and re-layouts  0.88 us (2%)
    all_to_all x1, blocking collectives, body(): lax.all_to_all(analysed, 'member', split_axis=0, concat_axis=0, tiled=True)  19.2 us
    ppermute x7, starting transfers between devices, trade(): lax.ppermute(block, 'member', [(i, i ^ distance) for i in range(members)])  13.3 us
    ppermute x1, waiting for transfers between devices, swaps(): far = lax.ppermute(far, 'tile', pairs(1))  5.21 us
    ppermute x7, waiting for transfers between devices, trade(): lax.ppermute(block, 'member', [(i, i ^ distance) for i in range(members)])  3.86 us
    pallas_call x1, Pallas kernels, body(): pl.pallas_call(functools.partial(weight_kernel, members), out_shape=jax.S...  2.8 us
    ppermute x1, starting transfers between devices, swaps(): far = lax.ppermute(far, 'tile', pairs(1))  1.92 us
    pallas_call x1, Pallas kernels, body(): pl.pallas_call(functools.partial(forecast_kernel, (members, own_rows, hal...  1.88 us
    pallas_call x1, Pallas kernels, body(): pl.pallas_call(functools.partial(precision_kernel, (halo, rows, width, ra...  1.32 us
  transfers between devices with their start and end apart: 9, of which 3 were waited for; matrix products, arithmetic and copies ran while one was open for 0% of the time, Pallas kernels for 8%

profile of v10, /device:TPU:2, one launch (start us, length us, event | category | flops | bytes accessed | tf_op | source)
XLA Modules:
  0.0 52.5 jit_solution(12232729991970693037)
XLA Ops:
  0.0 1.2 %edges.1 = (f32[104,512]{1,0:T(8,128)S(1)}, f32[104,512]{1,0:T(8,128)S(1)}) custom-call(f32[4,64,512]{2,1,0:T(8,128)} %bitcast.11, f32[64,512]{1,0:T(8,128)} %depth_ref.1, s32[64,512]{1,0:T(8,128)} %mask_ref.1, s32[32,128]{1,0:T(8,128)} %bitcast.13, f32[32,128]{1,0:T(8,128)} %bitcast.15, f32[32,128]{1,0:T(8,128)} %bitcast.17, f32[32,128]{1,0:T(8,128)} %bitcast.19), custom_call_target="tpu_custom_call" | custom-call | tf_op jit(solution)/shard_map/edges/pallas_call | solution.py:420
  1.2 0.1 collective-permute-start
  1.3 1.9 %collective-permute-start.1 = (f32[104,512]{1,0:T(8,128)S(1)}, f32[104,512]{1,0:T(8,128)S(1)}, u32[]{:S(2)}, u32[]{:S(2)}) collective-permute-start(f32[104,512]{1,0:T(8,128)S(1)} %get-tuple-element.16), channel_id=1, source_target_pairs={{1,2},{2,1},{5,6},{6,5},{9,10},{10,9},{13,14},{14,13},{17,18},{18,... | collective-permute-start | bytes 638984 | tf_op jit(solution)/shard_map/ppermute | solution.py:389
  3.3 0.0 collective-permute-done.near_ref
  3.3 0.0 copy-start.1
  3.3 5.2 %collective-permute-done.1.far_ref = f32[104,512]{1,0:T(8,128)S(1)} collective-permute-done((f32[104,512]{1,0:T(8,128)S(1)}, f32[104,512]{1,0:T(8,128)S(1)}, u32[]{:S(2)}, u32[]{:S(2)}) %collective-permute-start.1) | collective-permute-done | bytes 213024 | tf_op jit(solution)/shard_map/ppermute | solution.py:389
  8.5 1.9 %forecast.1 = (f32[40,128]{1,0:T(8,128)S(1)}, f32[552,128]{1,0:T(8,128)S(1)}, f32[128,128]{1,0:T(8,128)S(1)}, f32[128,128]{1,0:T(8,128)S(1)}, f32[128,128]{1,0:T(8,128)S(1)}, /*index=5*/f32[128,128]{1,0:T(8,128)S(1)}) custom-call(f32[4,64,512]{2,1,0:T(8,128)S(1)} %bitcast.12, f32[64,512]{1,0:T(8,128)S(1)} %copy-done.3, s32[64,512]{1,0:T(8,128)S(1)} %copy-done.4, ...), custom_call_target="tpu_custom_call" | custom-call | tf_op jit(solution)/shard_map/forecast/pallas_call | solution.py:446
  10.4 1.6 %collective-permute-start.2 = (f32[552,128]{1,0:T(8,128)S(1)}, f32[552,128]{1,0:T(8,128)S(1)}, u32[]{:S(2)}, u32[]{:S(2)}) collective-permute-start(f32[552,128]{1,0:T(8,128)S(1)} %get-tuple-element.18), channel_id=1, source_target_pairs={{0,4},{4,0},{8,12},{12,8},{16,20},{20,16},{24,28},{28,24},{1,5},{5... | collective-permute-start | bytes 847880 | tf_op jit(solution)/shard_map/ppermute | solution.py:363
  12.0 2.6 %collective-permute-start.3 = (f32[40,128]{1,0:T(8,128)S(1)}, f32[40,128]{1,0:T(8,128)S(1)}, u32[]{:S(2)}, u32[]{:S(2)}) collective-permute-start(f32[40,128]{1,0:T(8,128)S(1)} %get-tuple-element.17), channel_id=1, source_target_pairs={{0,16},{4,20},{8,24},{12,28},{16,0},{20,4},{24,8},{28,12},{1,17},{... | collective-permute-start | bytes 61448 | tf_op jit(solution)/shard_map/ppermute | solution.py:363
  14.6 2.5 %collective-permute-done.2.refs_1_ = f32[552,128]{1,0:T(8,128)S(1)} collective-permute-done((f32[552,128]{1,0:T(8,128)S(1)}, f32[552,128]{1,0:T(8,128)S(1)}, u32[]{:S(2)}, u32[]{:S(2)}) %collective-permute-start.2) | collective-permute-done | bytes 282656 | tf_op jit(solution)/shard_map/ppermute | solution.py:363
  17.1 2.6 %collective-permute-start.4 = (f32[120,128]{1,0:T(8,128)S(1)}, f32[120,128]{1,0:T(8,128)S(1)}, u32[]{:S(2)}, u32[]{:S(2)}) collective-permute-start(f32[120,128]{1,0:T(8,128)S(1)} %pad_maximum_fusion.3.three_ref), channel_id=1, source_target_pairs={{0,8},{4,12},{8,0},{12,4},{16,24},{20,28},{24,16},{28,20},{1,9},{5... | collective-permute-start | bytes 184328 | tf_op jit(solution)/shard_map/ppermute | solution.py:363
  19.7 0.1 collective-permute-start.6
  19.8 3.6 %collective-permute-start.7 = (f32[256,128]{1,0:T(8,128)S(1)}, f32[256,128]{1,0:T(8,128)S(1)}, u32[]{:S(2)}, u32[]{:S(2)}) collective-permute-start(f32[256,128]{1,0:T(8,128)S(1)} %pad_maximum_fusion.1), channel_id=1, source_target_pairs={{0,16},{4,20},{8,24},{12,28},{16,0},{20,4},{24,8},{28,12},{1,17},{... | collective-permute-start | bytes 393224 | tf_op jit(solution)/shard_map/ppermute | solution.py:363
  23.4 1.5 %collective-permute-start.8 = (f32[256,128]{1,0:T(8,128)S(1)}, f32[256,128]{1,0:T(8,128)S(1)}, u32[]{:S(2)}, u32[]{:S(2)}) collective-permute-start(f32[256,128]{1,0:T(8,128)S(1)} %pad_maximum_fusion.2), channel_id=1, source_target_pairs={{0,24},{4,28},{8,16},{12,20},{16,8},{20,12},{24,0},{28,4},{1,25},{... | collective-permute-start | bytes 393224 | tf_op jit(solution)/shard_map/ppermute | solution.py:363
  24.9 0.0 collective-permute-done.4.refs_0_
  25.0 1.4 %collective-permute-start.5 = (f32[80,128]{1,0:T(8,128)S(1)}, f32[80,128]{1,0:T(8,128)S(1)}, u32[]{:S(2)}, u32[]{:S(2)}) collective-permute-start(f32[80,128]{1,0:T(8,128)S(1)} %pad_maximum_fusion.4), channel_id=1, source_target_pairs={{0,4},{4,0},{8,12},{12,8},{16,20},{20,16},{24,28},{28,24},{1,5},{5... | collective-permute-start | bytes 122888 | tf_op jit(solution)/shard_map/ppermute | solution.py:363
  26.3 1.3 %precision.1 = (f32[2,8,128]{2,1,0:T(8,128)S(1)}, s32[8,128]{1,0:T(8,128)S(1)}) custom-call(s32[16,64]{1,0:T(8,128)} %bitcast.21, s32[1,16]{1,0:T(1,128)} %count_ref.1, f32[32,128]{1,0:T(8,128)} %bitcast.18, f32[32,128]{1,0:T(8,128)} %bitcast.20, f32[104,512]{1,0:T(8,128)} %copy-done.1, f32[104,512]{1,0:T(8,128)} %copy-done.2), custom_call_target="tpu_custom_call" | custom-call | tf_op jit(solution)/shard_map/precision/pallas_call | solution.py:469
  27.7 1.4 %collective-permute-done.5.last_ref = f32[80,128]{1,0:T(8,128)S(1)} collective-permute-done((f32[80,128]{1,0:T(8,128)S(1)}, f32[80,128]{1,0:T(8,128)S(1)}, u32[]{:S(2)}, u32[]{:S(2)}) %collective-permute-start.5) | collective-permute-done | bytes 40992 | tf_op jit(solution)/shard_map/ppermute | solution.py:363
  29.0 2.8 %weights.1.mix_ref = f32[8,128]{1,0:T(8,128)S(1)} custom-call(f32[120,128]{1,0:T(8,128)S(1)} %pad_maximum_fusion.3.three_ref, f32[80,128]{1,0:T(8,128)S(1)} %collective-permute-done.5.last_ref, f32[120,128]{1,0:T(8,128)S(1)} %collective-permute-done.4.refs_0_, s32[8,128]{1,0:T(8,128)S(1)} %get-tuple-element.19.refs_1_, ...), custom_call_target="tpu_custom_call" | custom-call | tf_op jit(solution)/shard_map/weights/pallas_call | solution.py:484
  31.8 0.0 collective-permute-done.6.refs_2_
  31.8 0.0 collective-permute-done.7.refs_3_
  31.9 0.5 mix.1
  32.4 19.2 %all_to_all.5 = f32[8,4,8,512]{3,2,1,0:T(8,128)S(1)} all-to-all(f32[8,4,8,512]{3,2,1,0:T(8,128)S(1)} %mix.1), channel_id=1, replica_groups=mesh['member'=8,'tile'=4] {'member'}, dimensions={0} | all-to-all | bytes 1048576 | tf_op jit(solution)/shard_map/all_to_all | solution.py:502
  51.6 0.8 %copy_bitcast_fusion = f32[1,4,64,512]{3,2,1,0:T(8,128)} fusion(f32[8,4,8,512]{3,2,1,0:T(8,128)S(1)} %all_to_all.5), kind=kLoop, calls=%fused_computation | loop fusion | bytes 1048576 | tf_op jit(solution)/shard_map/reshape | solution.py:503
  (23 shorter events, 0.1 us)
Async XLA Ops:
  0.0 8.5 %copy-start = (f32[1,4,64,512]{3,2,1,0:T(8,128)S(1)}, f32[1,4,64,512]{3,2,1,0:T(8,128)}, u32[]{:S(2)}) copy-start(f32[1,4,64,512]{3,2,1,0:T(8,128)} %param.9) | copy-start | bytes 1572868
  0.0 8.5 %copy-start.3 = (f32[64,512]{1,0:T(8,128)S(1)}, f32[64,512]{1,0:T(8,128)}, u32[]{:S(2)}) copy-start(f32[64,512]{1,0:T(8,128)} %depth_ref.1) | copy-start | bytes 393220
  0.0 8.5 %copy-start.4 = (s32[64,512]{1,0:T(8,128)S(1)}, s32[64,512]{1,0:T(8,128)}, u32[]{:S(2)}) copy-start(s32[64,512]{1,0:T(8,128)} %mask_ref.1) | copy-start | bytes 393220
  0.0 8.5 %copy-start.5 = (s32[4096]{0:T(1024)S(1)}, s32[4096]{0:T(1024)}, u32[]{:S(2)}) copy-start(s32[4096]{0:T(1024)} %param.12) | copy-start | bytes 49156
  0.0 8.5 %copy-start.6 = (f32[4096]{0:T(1024)S(1)}, f32[4096]{0:T(1024)}, u32[]{:S(2)}) copy-start(f32[4096]{0:T(1024)} %param.15) | copy-start | bytes 49156
  1.2 2.0 %collective-permute-start = (f32[104,512]{1,0:T(8,128)S(1)}, f32[104,512]{1,0:T(8,128)S(1)}, u32[]{:S(2)}, u32[]{:S(2)}) collective-permute-start(f32[104,512]{1,0:T(8,128)S(1)} %get-tuple-element.15), channel_id=1, source_target_pairs={{0,1},{2,3},{1,0},{3,2},{4,5},{6,7},{5,4},{7,6},{8,9},{10,11},{9,8... | collective-permute-start | bytes 638984 | tf_op jit(solution)/shard_map/ppermute | solution.py:390
  1.3 7.2 %collective-permute-start.1 = (f32[104,512]{1,0:T(8,128)S(1)}, f32[104,512]{1,0:T(8,128)S(1)}, u32[]{:S(2)}, u32[]{:S(2)}) collective-permute-start(f32[104,512]{1,0:T(8,128)S(1)} %get-tuple-element.16), channel_id=1, source_target_pairs={{1,2},{2,1},{5,6},{6,5},{9,10},{10,9},{13,14},{14,13},{17,18},{18,... | collective-permute-start | bytes 638984 | tf_op jit(solution)/shard_map/ppermute | solution.py:389
  3.3 7.2 %copy-start.1 = (f32[104,512]{1,0:T(8,128)}, f32[104,512]{1,0:T(8,128)S(1)}, u32[]{:S(2)}) copy-start(f32[104,512]{1,0:T(8,128)S(1)} %collective-permute-done.near_ref) | copy-start | bytes 638980
  8.5 1.9 %copy-start.2 = (f32[104,512]{1,0:T(8,128)}, f32[104,512]{1,0:T(8,128)S(1)}, u32[]{:S(2)}) copy-start(f32[104,512]{1,0:T(8,128)S(1)} %collective-permute-done.1.far_ref) | copy-start | bytes 638980
  10.4 6.7 %collective-permute-start.2 = (f32[552,128]{1,0:T(8,128)S(1)}, f32[552,128]{1,0:T(8,128)S(1)}, u32[]{:S(2)}, u32[]{:S(2)}) collective-permute-start(f32[552,128]{1,0:T(8,128)S(1)} %get-tuple-element.18), channel_id=1, source_target_pairs={{0,4},{4,0},{8,12},{12,8},{16,20},{20,16},{24,28},{28,24},{1,5},{5... | collective-permute-start | bytes 847880 | tf_op jit(solution)/shard_map/ppermute | solution.py:363
  12.0 5.1 %collective-permute-start.3 = (f32[40,128]{1,0:T(8,128)S(1)}, f32[40,128]{1,0:T(8,128)S(1)}, u32[]{:S(2)}, u32[]{:S(2)}) collective-permute-start(f32[40,128]{1,0:T(8,128)S(1)} %get-tuple-element.17), channel_id=1, source_target_pairs={{0,16},{4,20},{8,24},{12,28},{16,0},{20,4},{24,8},{28,12},{1,17},{... | collective-permute-start | bytes 61448 | tf_op jit(solution)/shard_map/ppermute | solution.py:363
  17.1 7.8 %collective-permute-start.4 = (f32[120,128]{1,0:T(8,128)S(1)}, f32[120,128]{1,0:T(8,128)S(1)}, u32[]{:S(2)}, u32[]{:S(2)}) collective-permute-start(f32[120,128]{1,0:T(8,128)S(1)} %pad_maximum_fusion.3.three_ref), channel_id=1, source_target_pairs={{0,8},{4,12},{8,0},{12,4},{16,24},{20,28},{24,16},{28,20},{1,9},{5... | collective-permute-start | bytes 184328 | tf_op jit(solution)/shard_map/ppermute | solution.py:363
  19.7 12.1 %collective-permute-start.6 = (f32[256,128]{1,0:T(8,128)S(1)}, f32[256,128]{1,0:T(8,128)S(1)}, u32[]{:S(2)}, u32[]{:S(2)}) collective-permute-start(f32[256,128]{1,0:T(8,128)S(1)} %pad_maximum_fusion), channel_id=1, source_target_pairs={{0,8},{4,12},{8,0},{12,4},{16,24},{20,28},{24,16},{28,20},{1,9},{5... | collective-permute-start | bytes 393224 | tf_op jit(solution)/shard_map/ppermute | solution.py:363
  19.8 12.0 %collective-permute-start.7 = (f32[256,128]{1,0:T(8,128)S(1)}, f32[256,128]{1,0:T(8,128)S(1)}, u32[]{:S(2)}, u32[]{:S(2)}) collective-permute-start(f32[256,128]{1,0:T(8,128)S(1)} %pad_maximum_fusion.1), channel_id=1, source_target_pairs={{0,16},{4,20},{8,24},{12,28},{16,0},{20,4},{24,8},{28,12},{1,17},{... | collective-permute-start | bytes 393224 | tf_op jit(solution)/shard_map/ppermute | solution.py:363
  23.4 8.4 %collective-permute-start.8 = (f32[256,128]{1,0:T(8,128)S(1)}, f32[256,128]{1,0:T(8,128)S(1)}, u32[]{:S(2)}, u32[]{:S(2)}) collective-permute-start(f32[256,128]{1,0:T(8,128)S(1)} %pad_maximum_fusion.2), channel_id=1, source_target_pairs={{0,24},{4,28},{8,16},{12,20},{16,8},{20,12},{24,0},{28,4},{1,25},{... | collective-permute-start | bytes 393224 | tf_op jit(solution)/shard_map/ppermute | solution.py:363
  25.0 4.1 %collective-permute-start.5 = (f32[80,128]{1,0:T(8,128)S(1)}, f32[80,128]{1,0:T(8,128)S(1)}, u32[]{:S(2)}, u32[]{:S(2)}) collective-permute-start(f32[80,128]{1,0:T(8,128)S(1)} %pad_maximum_fusion.4), channel_id=1, source_target_pairs={{0,4},{4,0},{8,12},{12,8},{16,20},{20,16},{24,28},{28,24},{1,5},{5... | collective-permute-start | bytes 122888 | tf_op jit(solution)/shard_map/ppermute | solution.py:363

commit v11 on v9

--- a/solution.py
+++ b/solution.py
@@ -87,7 +87,7 @@
     half = members // 2
     out_ref, equiv_ref, across_ref = refs[:3]
     along_refs, scratch = refs[3 : half + 3], refs[half + 3 :]
-    s_ref, u_ref, v_ref, e_ref, h_ref, w_ref, flux_ref, part_ref, cell_win, gain_win = scratch
+    s_ref, u_ref, v_ref, e_ref, h_ref, w_ref, flux_ref, part_ref, cell_win, gain_win, pack_ref, sem = scratch
     even = lax.axis_index("tile") % 2 == 0
     rows, width = depth_ref.shape
     pieces = width // LANES
@@ -158,6 +158,17 @@
                     e = e_ref[q, here, :]
                     e_ref[q, here, :] = w * ((1.0 - UPWIND - DAMPING) * e + UPWIND * e_ref[q, above, :])
 
+    me = lax.axis_index("member")
+    for j in range(members):
+        source = first + j * own_rows
+        for i in range(PACKED):
+            for q in range(pieces):
+                target = (i * pieces + q) * own_rows
+                block = fields[i][q, source : source + own_rows, :]
+                pack_ref[j, target : target + own_rows, :] = block if i else block * (1.0 / PRESSURE)
+    sent = pltpu.make_async_copy(pack_ref, out_ref, sem)
+    sent.start()
+
     window = cell_win.shape[0]
     base = 6 * halo
     offsets = (cell_ref[...] % CELLS_PER_OBS).astype(jnp.float32)
@@ -190,14 +201,7 @@
     equiv_ref[...] = equiv
     across_ref[across_ref.shape[0] - window :, :] = equiv
 
-    me = lax.axis_index("member")
     for j in range(members):
-        source = first + j * own_rows
-        for i in range(PACKED):
-            for q in range(pieces):
-                target = (i * pieces + q) * own_rows
-                block = fields[i][q, source : source + own_rows, :]
-                out_ref[j, target : target + own_rows, :] = block if i else block * (1.0 / PRESSURE)
         source = pl.multiple_of(first + (me ^ j) * own_rows, min(own_rows, 8))
         for i in range(PACKED, 4):
             for q in range(pieces):
@@ -208,6 +212,7 @@
                     across_ref[target : target + own_rows, :] = block
                 else:
                     along_refs[j // 2][target : target + own_rows, :] = block
+    sent.wait()
 
 
 def group_columns(left, starts, members):
@@ -259,7 +264,7 @@
 def weight_kernel(members, three_ref, last_ref, *refs):
     half = members // 2
     near_refs, (spot_ref, known_ref, mix_ref, equiv_win) = refs[: half // 2 - 1], refs[half // 2 - 1 :]
-    window = equiv_win.shape[0] // members
+    window = equiv_win.shape[0] // (members + 1)
     for i, ref in enumerate((three_ref, *near_refs)):
         for j, place in enumerate((2 * i, 2 * i + 1, 2 * i + half)):
             equiv_win[place * window : (place + 1) * window, :] = ref[j * window : (j + 1) * window, :]
@@ -341,7 +346,7 @@
     rest_rows = (4 - PACKED) * pieces * own_rows
     stride = recv_ref.shape[0] // members
     me = lax.axis_index("member")
-    table_ref[...] = mix_ref[...].T
+    table_ref[0:LANES, :] = mix_ref[...].T
     bases = [pl.multiple_of((me ^ d) * stride, 8) for d in range(members)]
 
     def analyse(m, carry):
@@ -461,14 +466,16 @@
     sends, equiv, across, *along = pl.pallas_call(
         functools.partial(forecast_kernel, (members, own_rows, halo, radius)),
         out_shape=[
-            pltpu.VMEM((members, packet, LANES), jnp.float32),
+            jax.ShapeDtypeStruct((members, packet, LANES), jnp.float32),
             jax.ShapeDtypeStruct((window, LANES), jnp.float32),
             jax.ShapeDtypeStruct((half * rest_rows + window, LANES), jnp.float32),
         ]
         + [jax.ShapeDtypeStruct((rest_rows, LANES), jnp.float32)] * half,
         in_specs=vmem_specs(7),
-        out_specs=vmem_specs(3 + half),
-        scratch_shapes=[pltpu.VMEM(grid, jnp.float32)] * 8 + [pltpu.VMEM((window, LANES), jnp.float32)] * 2,
+        out_specs=[pl.BlockSpec(memory_space=pl.ANY)] + vmem_specs(2 + half),
+        scratch_shapes=[pltpu.VMEM(grid, jnp.float32)] * 8
+        + [pltpu.VMEM((window, LANES), jnp.float32)] * 2
+        + [pltpu.VMEM((members, packet, LANES), jnp.float32), pltpu.SemaphoreType.DMA],
         compiler_params=pltpu.CompilerParams(vmem_limit_bytes=24 * 2**20),
         name="forecast",
     )(
@@ -504,7 +511,7 @@
         out_shape=jax.ShapeDtypeStruct((members, LANES), jnp.float32),
         in_specs=vmem_specs(4 + len(near_equivs)),
         out_specs=vmem_specs(1)[0],
-        scratch_shapes=[pltpu.VMEM((members * window, LANES), jnp.float32)],
+        scratch_shapes=[pltpu.VMEM(((members + 1) * window, LANES), jnp.float32)],
         compiler_params=pltpu.CompilerParams(vmem_limit_bytes=24 * 2**20),
         name="weights",
     )(three, last, *near_equivs, spot, known)
@@ -513,7 +520,7 @@
         out_shape=jax.ShapeDtypeStruct((members, 4, own_rows, width), jnp.float32),
         in_specs=vmem_specs(3 + half),
         out_specs=vmem_specs(1)[0],
-        scratch_shapes=[pltpu.VMEM((LANES, members), jnp.float32)],
+        scratch_shapes=[pltpu.VMEM((LANES + 2 * members, members), jnp.float32)],
         compiler_params=pltpu.CompilerParams(vmem_limit_bytes=24 * 2**20),
         name="mix",
     )(received, mix, *rest)

time: 49.7 us -> 49.6 us (level)
  no operation moved by 1% of the time
where the time goes in v11:
time: 49.6 us; the launch traced here: 49.3 us
  starting transfers between devices  18.5 us (37%)
  blocking collectives  17.3 us (35%)
  Pallas kernels  8.13 us (16%)
  waiting for transfers between devices  4.24 us (9%)
  local copies, waits for them, and re-layouts  0.88 us (2%)
    all_to_all x1, blocking collectives, body(): lax.all_to_all(analysed, 'member', split_axis=0, concat_axis=0, tiled=True)  17.3 us
    ppermute x7, starting transfers between devices, trade(): lax.ppermute(block, 'member', [(i, i ^ distance) for i in range(members)])  10.5 us
    ppermute x1, starting transfers between devices, swaps(): far = lax.ppermute(far, 'tile', pairs(1))  4.48 us
    ppermute x1, waiting for transfers between devices, swaps(): far = lax.ppermute(far, 'tile', pairs(1))  3.79 us
    all_to_all x1, starting transfers between devices, body(): lax.all_to_all(sends, 'member', split_axis=0, concat_axis=0, tiled=True)  3.41 us
    pallas_call x1, Pallas kernels, body(): pl.pallas_call(functools.partial(weight_kernel, members), out_shape=jax.S...  2.8 us
    pallas_call x1, Pallas kernels, body(): pl.pallas_call(functools.partial(forecast_kernel, (members, own_rows, hal...  2.29 us
    pallas_call x1, Pallas kernels, body(): pl.pallas_call(functools.partial(precision_kernel, (halo, rows, width, ra...  1.32 us
  transfers between devices with their start and end apart: 10, of which 2 were waited for; matrix products, arithmetic and copies ran while one was open for 0% of the time, Pallas kernels for 8%

profile of v11, /device:TPU:1, one launch (start us, length us, event | category | flops | bytes accessed | tf_op | source)
XLA Modules:
  0.0 49.3 jit_solution(13166832988680910302)
XLA Ops:
  0.0 1.2 %edges.1 = (f32[104,512]{1,0:T(8,128)S(1)}, f32[104,512]{1,0:T(8,128)S(1)}) custom-call(f32[4,64,512]{2,1,0:T(8,128)} %bitcast.12, f32[64,512]{1,0:T(8,128)} %depth_ref.1, s32[64,512]{1,0:T(8,128)} %mask_ref.1, s32[32,128]{1,0:T(8,128)} %bitcast.15, f32[32,128]{1,0:T(8,128)} %bitcast.17, f32[32,128]{1,0:T(8,128)} %bitcast.19, f32[32,128]{1,0:T(8,128)} %bitcast.21), custom_call_target="tpu_custom_call" | custom-call | tf_op jit(solution)/shard_map/edges/pallas_call | solution.py:439
  1.2 0.1 collective-permute-start
  1.4 4.5 %collective-permute-start.1 = (f32[104,512]{1,0:T(8,128)S(1)}, f32[104,512]{1,0:T(8,128)S(1)}, u32[]{:S(2)}, u32[]{:S(2)}) collective-permute-start(f32[104,512]{1,0:T(8,128)S(1)} %get-tuple-element.17), channel_id=1, source_target_pairs={{1,2},{2,1},{5,6},{6,5},{9,10},{10,9},{13,14},{14,13},{17,18},{18,... | collective-permute-start | bytes 638984 | tf_op jit(solution)/shard_map/ppermute | solution.py:408
  5.8 0.0 collective-permute-done.near_ref
  5.9 3.8 %collective-permute-done.1.far_ref = f32[104,512]{1,0:T(8,128)S(1)} collective-permute-done((f32[104,512]{1,0:T(8,128)S(1)}, f32[104,512]{1,0:T(8,128)S(1)}, u32[]{:S(2)}, u32[]{:S(2)}) %collective-permute-start.1) | collective-permute-done | bytes 213024 | tf_op jit(solution)/shard_map/ppermute | solution.py:408
  9.7 2.3 %forecast.1 = (f32[8,64,128]{2,1,0:T(8,128)}, f32[40,128]{1,0:T(8,128)S(1)}, f32[296,128]{1,0:T(8,128)S(1)}, f32[64,128]{1,0:T(8,128)S(1)}, f32[64,128]{1,0:T(8,...) custom-call(f32[4,64,512]{2,1,0:T(8,128)S(1)} %bitcast.13, f32[64,512]{1,0:T(8,128)S(1)} %copy-done.3, ...), custom_call_target="tpu_custom_call" | custom-call | tf_op jit(solution)/shard_map/forecast/pallas_call | solution.py:466
  12.0 1.9 %collective-permute-start.2 = (f32[296,128]{1,0:T(8,128)S(1)}, f32[296,128]{1,0:T(8,128)S(1)}, u32[]{:S(2)}, u32[]{:S(2)}) collective-permute-start(f32[296,128]{1,0:T(8,128)S(1)} %get-tuple-element.20), channel_id=1, source_target_pairs={{0,4},{4,0},{8,12},{12,8},{16,20},{20,16},{24,28},{28,24},{1,5},{5... | collective-permute-start | bytes 454664 | tf_op jit(solution)/shard_map/ppermute | solution.py:382
  13.9 2.3 %collective-permute-start.3 = (f32[40,128]{1,0:T(8,128)S(1)}, f32[40,128]{1,0:T(8,128)S(1)}, u32[]{:S(2)}, u32[]{:S(2)}) collective-permute-start(f32[40,128]{1,0:T(8,128)S(1)} %get-tuple-element.19), channel_id=1, source_target_pairs={{0,16},{4,20},{8,24},{12,28},{16,0},{20,4},{24,8},{28,12},{1,17},{... | collective-permute-start | bytes 61448 | tf_op jit(solution)/shard_map/ppermute | solution.py:382
  16.2 3.4 %all-to-all-start = ((f32[8,64,128]{2,1,0:T(8,128)}), f32[8,64,128]{2,1,0:T(8,128)S(1)}, u32[]{:S(2)}, u32[]{:S(2)}) async-start(f32[8,64,128]{2,1,0:T(8,128)} %get-tuple-element.18), calls=%async_computation | async-start | bytes 524288 | tf_op jit(solution)/shard_map/all_to_all | solution.py:490
  19.7 0.0 collective-permute-done.2.refs_1_
  19.7 1.4 %collective-permute-start.4 = (f32[120,128]{1,0:T(8,128)S(1)}, f32[120,128]{1,0:T(8,128)S(1)}, u32[]{:S(2)}, u32[]{:S(2)}) collective-permute-start(f32[120,128]{1,0:T(8,128)S(1)} %pad_maximum_fusion.3.three_ref), channel_id=1, source_target_pairs={{0,8},{4,12},{8,0},{12,4},{16,24},{20,28},{24,16},{28,20},{1,9},{5... | collective-permute-start | bytes 184328 | tf_op jit(solution)/shard_map/ppermute | solution.py:382
  21.1 0.2 collective-permute-start.6
  21.3 2.3 %collective-permute-start.7 = (f32[128,128]{1,0:T(8,128)S(1)}, f32[128,128]{1,0:T(8,128)S(1)}, u32[]{:S(2)}, u32[]{:S(2)}) collective-permute-start(f32[128,128]{1,0:T(8,128)S(1)} %pad_maximum_fusion.1), channel_id=1, source_target_pairs={{0,16},{4,20},{8,24},{12,28},{16,0},{20,4},{24,8},{28,12},{1,17},{... | collective-permute-start | bytes 196616 | tf_op jit(solution)/shard_map/ppermute | solution.py:382
  23.6 1.2 %collective-permute-start.8 = (f32[128,128]{1,0:T(8,128)S(1)}, f32[128,128]{1,0:T(8,128)S(1)}, u32[]{:S(2)}, u32[]{:S(2)}) collective-permute-start(f32[128,128]{1,0:T(8,128)S(1)} %pad_maximum_fusion.2), channel_id=1, source_target_pairs={{0,24},{4,28},{8,16},{12,20},{16,8},{20,12},{24,0},{28,4},{1,25},{... | collective-permute-start | bytes 196616 | tf_op jit(solution)/shard_map/ppermute | solution.py:382
  24.8 0.0 collective-permute-done.4.refs_0_
  24.8 1.3 %collective-permute-start.5 = (f32[80,128]{1,0:T(8,128)S(1)}, f32[80,128]{1,0:T(8,128)S(1)}, u32[]{:S(2)}, u32[]{:S(2)}) collective-permute-start(f32[80,128]{1,0:T(8,128)S(1)} %pad_maximum_fusion.4), channel_id=1, source_target_pairs={{0,4},{4,0},{8,12},{12,8},{16,20},{20,16},{24,28},{28,24},{1,5},{5... | collective-permute-start | bytes 122888 | tf_op jit(solution)/shard_map/ppermute | solution.py:382
  26.0 1.3 %precision.1 = (f32[2,8,128]{2,1,0:T(8,128)S(1)}, s32[8,128]{1,0:T(8,128)S(1)}) custom-call(s32[16,64]{1,0:T(8,128)} %bitcast.23, s32[1,16]{1,0:T(1,128)} %count_ref.1, f32[32,128]{1,0:T(8,128)} %bitcast.20, f32[32,128]{1,0:T(8,128)} %bitcast.22, f32[104,512]{1,0:T(8,128)} %copy-done.1, f32[104,512]{1,0:T(8,128)} %copy-done.2), custom_call_target="tpu_custom_call" | custom-call | tf_op jit(solution)/shard_map/precision/pallas_call | solution.py:494
  27.4 0.4 collective-permute-done.5.last_ref
  27.8 2.8 %weights.1.mix_ref = f32[8,128]{1,0:T(8,128)S(1)} custom-call(f32[120,128]{1,0:T(8,128)S(1)} %pad_maximum_fusion.3.three_ref, f32[80,128]{1,0:T(8,128)S(1)} %collective-permute-done.5.last_ref, f32[120,128]{1,0:T(8,128)S(1)} %collective-permute-done.4.refs_0_, s32[8,128]{1,0:T(8,128)S(1)} %get-tuple-element.21.refs_1_, ...), custom_call_target="tpu_custom_call" | custom-call | tf_op jit(solution)/shard_map/weights/pallas_call | solution.py:509
  30.6 0.0 collective-permute-done.7.refs_3_
  30.6 0.0 collective-permute-done.8.refs_4_
  30.6 0.5 %mix.1 = f32[8,4,8,512]{3,2,1,0:T(8,128)S(1)} custom-call(f32[512,128]{1,0:T(8,128)S(1)} %bitcast.14, f32[8,128]{1,0:T(8,128)S(1)} %weights.1.mix_ref, f32[64,128]{1,0:T(8,128)S(1)} %get-tuple-element.23.refs_0_, f32[296,128]{1,0:T(8,128)S(1)} %collective-permute-done.2.refs_1_, f32[128,128]{1,0:T(8,128)S(1)} %collective-permute-done.6.refs_2_, ...), custom_call_target="tpu_custom_call" | custom-call | tf_op jit(solution)/shard_map/mix/pallas_call | solution.py:518
  31.2 17.3 %all_to_all.10 = f32[8,4,8,512]{3,2,1,0:T(8,128)S(1)} all-to-all(f32[8,4,8,512]{3,2,1,0:T(8,128)S(1)} %mix.1), channel_id=1, replica_groups=mesh['member'=8,'tile'=4] {'member'}, dimensions={0} | all-to-all | bytes 1048576 | tf_op jit(solution)/shard_map/all_to_all | solution.py:527
  48.5 0.8 %copy_bitcast_fusion = f32[1,4,64,512]{3,2,1,0:T(8,128)} fusion(f32[8,4,8,512]{3,2,1,0:T(8,128)S(1)} %all_to_all.10), kind=kLoop, calls=%fused_computation | loop fusion | bytes 1048576 | tf_op jit(solution)/shard_map/reshape | solution.py:528
  (25 shorter events, 0.1 us)
Async XLA Ops:
  0.0 9.7 %copy-start = (f32[1,4,64,512]{3,2,1,0:T(8,128)S(1)}, f32[1,4,64,512]{3,2,1,0:T(8,128)}, u32[]{:S(2)}) copy-start(f32[1,4,64,512]{3,2,1,0:T(8,128)} %param.9) | copy-start | bytes 1572868
  0.0 9.7 %copy-start.3 = (f32[64,512]{1,0:T(8,128)S(1)}, f32[64,512]{1,0:T(8,128)}, u32[]{:S(2)}) copy-start(f32[64,512]{1,0:T(8,128)} %depth_ref.1) | copy-start | bytes 393220
  0.0 9.7 %copy-start.4 = (s32[64,512]{1,0:T(8,128)S(1)}, s32[64,512]{1,0:T(8,128)}, u32[]{:S(2)}) copy-start(s32[64,512]{1,0:T(8,128)} %mask_ref.1) | copy-start | bytes 393220
  0.0 9.7 %copy-start.5 = (s32[4096]{0:T(1024)S(1)}, s32[4096]{0:T(1024)}, u32[]{:S(2)}) copy-start(s32[4096]{0:T(1024)} %param.12) | copy-start | bytes 49156
  0.0 9.7 %copy-start.6 = (f32[4096]{0:T(1024)S(1)}, f32[4096]{0:T(1024)}, u32[]{:S(2)}) copy-start(f32[4096]{0:T(1024)} %param.15) | copy-start | bytes 49156
  1.2 4.6 %collective-permute-start = (f32[104,512]{1,0:T(8,128)S(1)}, f32[104,512]{1,0:T(8,128)S(1)}, u32[]{:S(2)}, u32[]{:S(2)}) collective-permute-start(f32[104,512]{1,0:T(8,128)S(1)} %get-tuple-element.16), channel_id=1, source_target_pairs={{0,1},{2,3},{1,0},{3,2},{4,5},{6,7},{5,4},{7,6},{8,9},{10,11},{9,8... | collective-permute-start | bytes 638984 | tf_op jit(solution)/shard_map/ppermute | solution.py:409
  1.4 8.3 %collective-permute-start.1 = (f32[104,512]{1,0:T(8,128)S(1)}, f32[104,512]{1,0:T(8,128)S(1)}, u32[]{:S(2)}, u32[]{:S(2)}) collective-permute-start(f32[104,512]{1,0:T(8,128)S(1)} %get-tuple-element.17), channel_id=1, source_target_pairs={{1,2},{2,1},{5,6},{6,5},{9,10},{10,9},{13,14},{14,13},{17,18},{18,... | collective-permute-start | bytes 638984 | tf_op jit(solution)/shard_map/ppermute | solution.py:408
  5.9 6.1 %copy-start.1 = (f32[104,512]{1,0:T(8,128)}, f32[104,512]{1,0:T(8,128)S(1)}, u32[]{:S(2)}) copy-start(f32[104,512]{1,0:T(8,128)S(1)} %collective-permute-done.near_ref) | copy-start | bytes 638980
  9.7 2.3 %copy-start.2 = (f32[104,512]{1,0:T(8,128)}, f32[104,512]{1,0:T(8,128)S(1)}, u32[]{:S(2)}) copy-start(f32[104,512]{1,0:T(8,128)S(1)} %collective-permute-done.1.far_ref) | copy-start | bytes 638980
  12.0 7.7 %collective-permute-start.2 = (f32[296,128]{1,0:T(8,128)S(1)}, f32[296,128]{1,0:T(8,128)S(1)}, u32[]{:S(2)}, u32[]{:S(2)}) collective-permute-start(f32[296,128]{1,0:T(8,128)S(1)} %get-tuple-element.20), channel_id=1, source_target_pairs={{0,4},{4,0},{8,12},{12,8},{16,20},{20,16},{24,28},{28,24},{1,5},{5... | collective-permute-start | bytes 454664 | tf_op jit(solution)/shard_map/ppermute | solution.py:382
  13.9 5.8 %collective-permute-start.3 = (f32[40,128]{1,0:T(8,128)S(1)}, f32[40,128]{1,0:T(8,128)S(1)}, u32[]{:S(2)}, u32[]{:S(2)}) collective-permute-start(f32[40,128]{1,0:T(8,128)S(1)} %get-tuple-element.19), channel_id=1, source_target_pairs={{0,16},{4,20},{8,24},{12,28},{16,0},{20,4},{24,8},{28,12},{1,17},{... | collective-permute-start | bytes 61448 | tf_op jit(solution)/shard_map/ppermute | solution.py:382
  16.2 14.4 %all-to-all-start = ((f32[8,64,128]{2,1,0:T(8,128)}), f32[8,64,128]{2,1,0:T(8,128)S(1)}, u32[]{:S(2)}, u32[]{:S(2)}) async-start(f32[8,64,128]{2,1,0:T(8,128)} %get-tuple-element.18), calls=%async_computation | async-start | bytes 524288 | tf_op jit(solution)/shard_map/all_to_all | solution.py:490
  19.7 5.1 %collective-permute-start.4 = (f32[120,128]{1,0:T(8,128)S(1)}, f32[120,128]{1,0:T(8,128)S(1)}, u32[]{:S(2)}, u32[]{:S(2)}) collective-permute-start(f32[120,128]{1,0:T(8,128)S(1)} %pad_maximum_fusion.3.three_ref), channel_id=1, source_target_pairs={{0,8},{4,12},{8,0},{12,4},{16,24},{20,28},{24,16},{28,20},{1,9},{5... | collective-permute-start | bytes 184328 | tf_op jit(solution)/shard_map/ppermute | solution.py:382
  21.1 9.5 %collective-permute-start.6 = (f32[128,128]{1,0:T(8,128)S(1)}, f32[128,128]{1,0:T(8,128)S(1)}, u32[]{:S(2)}, u32[]{:S(2)}) collective-permute-start(f32[128,128]{1,0:T(8,128)S(1)} %pad_maximum_fusion), channel_id=1, source_target_pairs={{0,8},{4,12},{8,0},{12,4},{16,24},{20,28},{24,16},{28,20},{1,9},{5... | collective-permute-start | bytes 196616 | tf_op jit(solution)/shard_map/ppermute | solution.py:382
  21.3 9.3 %collective-permute-start.7 = (f32[128,128]{1,0:T(8,128)S(1)}, f32[128,128]{1,0:T(8,128)S(1)}, u32[]{:S(2)}, u32[]{:S(2)}) collective-permute-start(f32[128,128]{1,0:T(8,128)S(1)} %pad_maximum_fusion.1), channel_id=1, source_target_pairs={{0,16},{4,20},{8,24},{12,28},{16,0},{20,4},{24,8},{28,12},{1,17},{... | collective-permute-start | bytes 196616 | tf_op jit(solution)/shard_map/ppermute | solution.py:382
  23.6 7.0 %collective-permute-start.8 = (f32[128,128]{1,0:T(8,128)S(1)}, f32[128,128]{1,0:T(8,128)S(1)}, u32[]{:S(2)}, u32[]{:S(2)}) collective-permute-start(f32[128,128]{1,0:T(8,128)S(1)} %pad_maximum_fusion.2), channel_id=1, source_target_pairs={{0,24},{4,28},{8,16},{12,20},{16,8},{20,12},{24,0},{28,4},{1,25},{... | collective-permute-start | bytes 196616 | tf_op jit(solution)/shard_map/ppermute | solution.py:382
  24.8 3.0 %collective-permute-start.5 = (f32[80,128]{1,0:T(8,128)S(1)}, f32[80,128]{1,0:T(8,128)S(1)}, u32[]{:S(2)}, u32[]{:S(2)}) collective-permute-start(f32[80,128]{1,0:T(8,128)S(1)} %pad_maximum_fusion.4), channel_id=1, source_target_pairs={{0,4},{4,0},{8,12},{12,8},{16,20},{20,16},{24,28},{28,24},{1,5},{5... | collective-permute-start | bytes 122888 | tf_op jit(solution)/shard_map/ppermute | solution.py:382

commit v12 on v11

--- a/solution.py
+++ b/solution.py
@@ -390,11 +390,10 @@
     far = trade(equiv, half)
     three = jnp.concatenate([equiv, passed[half * size :], far], axis=0)
     near = [trade(three, 2 * i) for i in range(1, half // 2)]
+    pairs = [jnp.concatenate([along[i], passed[i * size : (i + 1) * size]], axis=0) for i in range(1, half)]
+    pairs[0], near[0] = lax.optimization_barrier((pairs[0], near[0]))
     last = trade(jnp.concatenate([far] + [x[2 * window :] for x in near], axis=0), 1)
-    pairs = [
-        trade(jnp.concatenate([along[i], passed[i * size : (i + 1) * size]], axis=0), 2 * i)
-        for i in range(1, half)
-    ]
+    pairs = [trade(pair, 2 * i) for i, pair in enumerate(pairs, 1)]
     return three, last, near, [along[0], passed, *pairs]
 
 

time: 49.6 us -> 50.3 us (1.014)
  waiting for transfers between devices: 4.24 us -> 6.59 us
  starting transfers between devices: 18.5 us -> 17.6 us
  blocking collectives: 17.3 us -> 16.5 us
    ppermute x7, waiting for transfers between devices: 0.44 us -> 2.8 us  [trade(): lax.ppermute(block, 'member', [(i, i ^ distance) for i in range(members)])]
    all_to_all x1, blocking collectives: 17.3 us -> 16.5 us  [body(): lax.all_to_all(analysed, 'member', split_axis=0, concat_axis=0, tiled=True)]
    ppermute x7, starting transfers between devices: 10.5 us -> 9.65 us  [trade(): lax.ppermute(block, 'member', [(i, i ^ distance) for i in range(members)])]
  transfers between devices with their start and end apart: 10 -> 10, of which waited for: 2 -> 3; matrix products, arithmetic and copies ran while one was open for 0% -> 0% of each run, Pallas kernels for 8% -> 8%
where the time goes in v12:
time: 50.3 us; the launch traced here: 50 us
  starting transfers between devices  17.6 us (35%)
  blocking collectives  16.5 us (33%)
  Pallas kernels  8.13 us (16%)
  waiting for transfers between devices  6.59 us (13%)
  local copies, waits for them, and re-layouts  0.88 us (2%)
    all_to_all x1, blocking collectives, body(): lax.all_to_all(analysed, 'member', split_axis=0, concat_axis=0, tiled=True)  16.5 us
    ppermute x7, starting transfers between devices, trade(): lax.ppermute(block, 'member', [(i, i ^ distance) for i in range(members)])  9.65 us
    ppermute x1, starting transfers between devices, swaps(): far = lax.ppermute(far, 'tile', pairs(1))  4.48 us
    ppermute x1, waiting for transfers between devices, swaps(): far = lax.ppermute(far, 'tile', pairs(1))  3.79 us
    all_to_all x1, starting transfers between devices, body(): lax.all_to_all(sends, 'member', split_axis=0, concat_axis=0, tiled=True)  3.41 us
    pallas_call x1, Pallas kernels, body(): pl.pallas_call(functools.partial(weight_kernel, members), out_shape=jax.S...  2.8 us
    ppermute x7, waiting for transfers between devices, trade(): lax.ppermute(block, 'member', [(i, i ^ distance) for i in range(members)])  2.8 us
    pallas_call x1, Pallas kernels, body(): pl.pallas_call(functools.partial(forecast_kernel, (members, own_rows, hal...  2.29 us
  transfers between devices with their start and end apart: 10, of which 3 were waited for; matrix products, arithmetic and copies ran while one was open for 0% of the time, Pallas kernels for 8%

profile of v12, /device:TPU:1, one launch (start us, length us, event | category | flops | bytes accessed | tf_op | source)
XLA Modules:
  0.0 50.0 jit_solution(8233206648065776711)
XLA Ops:
  0.0 1.2 %edges.1 = (f32[104,512]{1,0:T(8,128)S(1)}, f32[104,512]{1,0:T(8,128)S(1)}) custom-call(f32[4,64,512]{2,1,0:T(8,128)} %bitcast.12, f32[64,512]{1,0:T(8,128)} %depth_ref.1, s32[64,512]{1,0:T(8,128)} %mask_ref.1, s32[32,128]{1,0:T(8,128)} %bitcast.15, f32[32,128]{1,0:T(8,128)} %bitcast.17, f32[32,128]{1,0:T(8,128)} %bitcast.19, f32[32,128]{1,0:T(8,128)} %bitcast.21), custom_call_target="tpu_custom_call" | custom-call | tf_op jit(solution)/shard_map/edges/pallas_call | solution.py:438
  1.2 0.1 collective-permute-start
  1.4 4.5 %collective-permute-start.1 = (f32[104,512]{1,0:T(8,128)S(1)}, f32[104,512]{1,0:T(8,128)S(1)}, u32[]{:S(2)}, u32[]{:S(2)}) collective-permute-start(f32[104,512]{1,0:T(8,128)S(1)} %get-tuple-element.19), channel_id=1, source_target_pairs={{1,2},{2,1},{5,6},{6,5},{9,10},{10,9},{13,14},{14,13},{17,18},{18,... | collective-permute-start | bytes 638984 | tf_op jit(solution)/shard_map/ppermute | solution.py:407
  5.8 0.0 collective-permute-done.near_ref
  5.9 3.8 %collective-permute-done.1.far_ref = f32[104,512]{1,0:T(8,128)S(1)} collective-permute-done((f32[104,512]{1,0:T(8,128)S(1)}, f32[104,512]{1,0:T(8,128)S(1)}, u32[]{:S(2)}, u32[]{:S(2)}) %collective-permute-start.1) | collective-permute-done | bytes 213024 | tf_op jit(solution)/shard_map/ppermute | solution.py:407
  9.7 2.3 %forecast.1 = (f32[8,64,128]{2,1,0:T(8,128)}, f32[40,128]{1,0:T(8,128)S(1)}, f32[296,128]{1,0:T(8,128)S(1)}, f32[64,128]{1,0:T(8,128)S(1)}, f32[64,128]{1,0:T(8,...) custom-call(f32[4,64,512]{2,1,0:T(8,128)S(1)} %bitcast.13, f32[64,512]{1,0:T(8,128)S(1)} %copy-done.3, ...), custom_call_target="tpu_custom_call" | custom-call | tf_op jit(solution)/shard_map/forecast/pallas_call | solution.py:465
  12.0 1.9 %collective-permute-start.2 = (f32[296,128]{1,0:T(8,128)S(1)}, f32[296,128]{1,0:T(8,128)S(1)}, u32[]{:S(2)}, u32[]{:S(2)}) collective-permute-start(f32[296,128]{1,0:T(8,128)S(1)} %get-tuple-element.22), channel_id=1, source_target_pairs={{0,4},{4,0},{8,12},{12,8},{16,20},{20,16},{24,28},{28,24},{1,5},{5... | collective-permute-start | bytes 454664 | tf_op jit(solution)/shard_map/ppermute | solution.py:382
  13.9 2.3 %collective-permute-start.3 = (f32[40,128]{1,0:T(8,128)S(1)}, f32[40,128]{1,0:T(8,128)S(1)}, u32[]{:S(2)}, u32[]{:S(2)}) collective-permute-start(f32[40,128]{1,0:T(8,128)S(1)} %get-tuple-element.21), channel_id=1, source_target_pairs={{0,16},{4,20},{8,24},{12,28},{16,0},{20,4},{24,8},{28,12},{1,17},{... | collective-permute-start | bytes 61448 | tf_op jit(solution)/shard_map/ppermute | solution.py:382
  16.2 3.4 %all-to-all-start = ((f32[8,64,128]{2,1,0:T(8,128)}), f32[8,64,128]{2,1,0:T(8,128)S(1)}, u32[]{:S(2)}, u32[]{:S(2)}) async-start(f32[8,64,128]{2,1,0:T(8,128)} %get-tuple-element.20), calls=%async_computation | async-start | bytes 524288 | tf_op jit(solution)/shard_map/all_to_all | solution.py:489
  19.7 0.0 collective-permute-done.3
  19.7 1.4 %collective-permute-start.4 = (f32[120,128]{1,0:T(8,128)S(1)}, f32[120,128]{1,0:T(8,128)S(1)}, u32[]{:S(2)}, u32[]{:S(2)}) collective-permute-start(f32[120,128]{1,0:T(8,128)S(1)} %pad_maximum_fusion.3.three_ref), channel_id=1, source_target_pairs={{0,8},{4,12},{8,0},{12,4},{16,24},{20,28},{24,16},{28,20},{1,9},{5... | collective-permute-start | bytes 184328 | tf_op jit(solution)/shard_map/ppermute | solution.py:382
  21.1 2.2 %collective-permute-start.7 = (f32[128,128]{1,0:T(8,128)S(1)}, f32[128,128]{1,0:T(8,128)S(1)}, u32[]{:S(2)}, u32[]{:S(2)}) collective-permute-start(f32[128,128]{1,0:T(8,128)S(1)} %pad_maximum_fusion.1), channel_id=1, source_target_pairs={{0,16},{4,20},{8,24},{12,28},{16,0},{20,4},{24,8},{28,12},{1,17},{... | collective-permute-start | bytes 196616 | tf_op jit(solution)/shard_map/ppermute | solution.py:382
  23.3 0.1 collective-permute-start.8
  23.4 2.7 %collective-permute-done.4.refs_0_ = f32[120,128]{1,0:T(8,128)S(1)} collective-permute-done((f32[120,128]{1,0:T(8,128)S(1)}, f32[120,128]{1,0:T(8,128)S(1)}, u32[]{:S(2)}, u32[]{:S(2)}) %collective-permute-start.4) | collective-permute-done | bytes 61472 | tf_op jit(solution)/shard_map/ppermute | solution.py:382
  26.1 0.1 collective-permute-start.6
  26.3 1.6 %collective-permute-start.5 = (f32[80,128]{1,0:T(8,128)S(1)}, f32[80,128]{1,0:T(8,128)S(1)}, u32[]{:S(2)}, u32[]{:S(2)}) collective-permute-start(f32[80,128]{1,0:T(8,128)S(1)} %pad_maximum_fusion.4), channel_id=1, source_target_pairs={{0,4},{4,0},{8,12},{12,8},{16,20},{20,16},{24,28},{28,24},{1,5},{5... | collective-permute-start | bytes 122888 | tf_op jit(solution)/shard_map/ppermute | solution.py:382
  27.9 1.3 %precision.1 = (f32[2,8,128]{2,1,0:T(8,128)S(1)}, s32[8,128]{1,0:T(8,128)S(1)}) custom-call(s32[16,64]{1,0:T(8,128)} %bitcast.23, s32[1,16]{1,0:T(1,128)} %count_ref.1, f32[32,128]{1,0:T(8,128)} %bitcast.20, f32[32,128]{1,0:T(8,128)} %bitcast.22, f32[104,512]{1,0:T(8,128)} %copy-done.1, f32[104,512]{1,0:T(8,128)} %copy-done.2), custom_call_target="tpu_custom_call" | custom-call | tf_op jit(solution)/shard_map/precision/pallas_call | solution.py:493
  29.2 0.1 collective-permute-done.5.last_ref
  29.3 2.8 %weights.1.mix_ref = f32[8,128]{1,0:T(8,128)S(1)} custom-call(f32[120,128]{1,0:T(8,128)S(1)} %pad_maximum_fusion.3.three_ref, f32[80,128]{1,0:T(8,128)S(1)} %collective-permute-done.5.last_ref, f32[120,128]{1,0:T(8,128)S(1)} %collective-permute-done.4.refs_0_, s32[8,128]{1,0:T(8,128)S(1)} %get-tuple-element.25.refs_1_, ...), custom_call_target="tpu_custom_call" | custom-call | tf_op jit(solution)/shard_map/weights/pallas_call | solution.py:508
  32.1 0.0 collective-permute-done.7.refs_3_
  32.1 0.0 collective-permute-done.6.refs_2_
  32.1 0.5 %mix.1 = f32[8,4,8,512]{3,2,1,0:T(8,128)S(1)} custom-call(f32[512,128]{1,0:T(8,128)S(1)} %bitcast.14, f32[8,128]{1,0:T(8,128)S(1)} %weights.1.mix_ref, f32[64,128]{1,0:T(8,128)S(1)} %get-tuple-element.27.refs_0_, f32[296,128]{1,0:T(8,128)S(1)} %collective-permute-done.2.refs_1_, f32[128,128]{1,0:T(8,128)S(1)} %collective-permute-done.6.refs_2_, ...), custom_call_target="tpu_custom_call" | custom-call | tf_op jit(solution)/shard_map/mix/pallas_call | solution.py:517
  32.6 16.5 %all_to_all.10 = f32[8,4,8,512]{3,2,1,0:T(8,128)S(1)} all-to-all(f32[8,4,8,512]{3,2,1,0:T(8,128)S(1)} %mix.1), channel_id=1, replica_groups=mesh['member'=8,'tile'=4] {'member'}, dimensions={0} | all-to-all | bytes 1048576 | tf_op jit(solution)/shard_map/all_to_all | solution.py:526
  49.1 0.8 %copy_bitcast_fusion = f32[1,4,64,512]{3,2,1,0:T(8,128)} fusion(f32[8,4,8,512]{3,2,1,0:T(8,128)S(1)} %all_to_all.10), kind=kLoop, calls=%fused_computation | loop fusion | bytes 1048576 | tf_op jit(solution)/shard_map/reshape | solution.py:527
  (25 shorter events, 0.1 us)
Async XLA Ops:
  0.0 9.7 %copy-start = (f32[1,4,64,512]{3,2,1,0:T(8,128)S(1)}, f32[1,4,64,512]{3,2,1,0:T(8,128)}, u32[]{:S(2)}) copy-start(f32[1,4,64,512]{3,2,1,0:T(8,128)} %param.9) | copy-start | bytes 1572868
  0.0 9.7 %copy-start.3 = (f32[64,512]{1,0:T(8,128)S(1)}, f32[64,512]{1,0:T(8,128)}, u32[]{:S(2)}) copy-start(f32[64,512]{1,0:T(8,128)} %depth_ref.1) | copy-start | bytes 393220
  0.0 9.7 %copy-start.4 = (s32[64,512]{1,0:T(8,128)S(1)}, s32[64,512]{1,0:T(8,128)}, u32[]{:S(2)}) copy-start(s32[64,512]{1,0:T(8,128)} %mask_ref.1) | copy-start | bytes 393220
  0.0 9.7 %copy-start.5 = (s32[4096]{0:T(1024)S(1)}, s32[4096]{0:T(1024)}, u32[]{:S(2)}) copy-start(s32[4096]{0:T(1024)} %param.12) | copy-start | bytes 49156
  0.0 9.7 %copy-start.6 = (f32[4096]{0:T(1024)S(1)}, f32[4096]{0:T(1024)}, u32[]{:S(2)}) copy-start(f32[4096]{0:T(1024)} %param.15) | copy-start | bytes 49156
  1.2 4.6 %collective-permute-start = (f32[104,512]{1,0:T(8,128)S(1)}, f32[104,512]{1,0:T(8,128)S(1)}, u32[]{:S(2)}, u32[]{:S(2)}) collective-permute-start(f32[104,512]{1,0:T(8,128)S(1)} %get-tuple-element.18), channel_id=1, source_target_pairs={{0,1},{2,3},{1,0},{3,2},{4,5},{6,7},{5,4},{7,6},{8,9},{10,11},{9,8... | collective-permute-start | bytes 638984 | tf_op jit(solution)/shard_map/ppermute | solution.py:408
  1.4 8.3 %collective-permute-start.1 = (f32[104,512]{1,0:T(8,128)S(1)}, f32[104,512]{1,0:T(8,128)S(1)}, u32[]{:S(2)}, u32[]{:S(2)}) collective-permute-start(f32[104,512]{1,0:T(8,128)S(1)} %get-tuple-element.19), channel_id=1, source_target_pairs={{1,2},{2,1},{5,6},{6,5},{9,10},{10,9},{13,14},{14,13},{17,18},{18,... | collective-permute-start | bytes 638984 | tf_op jit(solution)/shard_map/ppermute | solution.py:407
  5.9 6.1 %copy-start.1 = (f32[104,512]{1,0:T(8,128)}, f32[104,512]{1,0:T(8,128)S(1)}, u32[]{:S(2)}) copy-start(f32[104,512]{1,0:T(8,128)S(1)} %collective-permute-done.near_ref) | copy-start | bytes 638980
  9.7 2.3 %copy-start.2 = (f32[104,512]{1,0:T(8,128)}, f32[104,512]{1,0:T(8,128)S(1)}, u32[]{:S(2)}) copy-start(f32[104,512]{1,0:T(8,128)S(1)} %collective-permute-done.1.far_ref) | copy-start | bytes 638980
  12.0 7.7 %collective-permute-start.2 = (f32[296,128]{1,0:T(8,128)S(1)}, f32[296,128]{1,0:T(8,128)S(1)}, u32[]{:S(2)}, u32[]{:S(2)}) collective-permute-start(f32[296,128]{1,0:T(8,128)S(1)} %get-tuple-element.22), channel_id=1, source_target_pairs={{0,4},{4,0},{8,12},{12,8},{16,20},{20,16},{24,28},{28,24},{1,5},{5... | collective-permute-start | bytes 454664 | tf_op jit(solution)/shard_map/ppermute | solution.py:382
  13.9 5.8 %collective-permute-start.3 = (f32[40,128]{1,0:T(8,128)S(1)}, f32[40,128]{1,0:T(8,128)S(1)}, u32[]{:S(2)}, u32[]{:S(2)}) collective-permute-start(f32[40,128]{1,0:T(8,128)S(1)} %get-tuple-element.21), channel_id=1, source_target_pairs={{0,16},{4,20},{8,24},{12,28},{16,0},{20,4},{24,8},{28,12},{1,17},{... | collective-permute-start | bytes 61448 | tf_op jit(solution)/shard_map/ppermute | solution.py:382
  16.2 15.9 %all-to-all-start = ((f32[8,64,128]{2,1,0:T(8,128)}), f32[8,64,128]{2,1,0:T(8,128)S(1)}, u32[]{:S(2)}, u32[]{:S(2)}) async-start(f32[8,64,128]{2,1,0:T(8,128)} %get-tuple-element.20), calls=%async_computation | async-start | bytes 524288 | tf_op jit(solution)/shard_map/all_to_all | solution.py:489
  19.7 6.4 %collective-permute-start.4 = (f32[120,128]{1,0:T(8,128)S(1)}, f32[120,128]{1,0:T(8,128)S(1)}, u32[]{:S(2)}, u32[]{:S(2)}) collective-permute-start(f32[120,128]{1,0:T(8,128)S(1)} %pad_maximum_fusion.3.three_ref), channel_id=1, source_target_pairs={{0,8},{4,12},{8,0},{12,4},{16,24},{20,28},{24,16},{28,20},{1,9},{5... | collective-permute-start | bytes 184328 | tf_op jit(solution)/shard_map/ppermute | solution.py:382
  21.1 10.9 %collective-permute-start.7 = (f32[128,128]{1,0:T(8,128)S(1)}, f32[128,128]{1,0:T(8,128)S(1)}, u32[]{:S(2)}, u32[]{:S(2)}) collective-permute-start(f32[128,128]{1,0:T(8,128)S(1)} %pad_maximum_fusion.1), channel_id=1, source_target_pairs={{0,16},{4,20},{8,24},{12,28},{16,0},{20,4},{24,8},{28,12},{1,17},{... | collective-permute-start | bytes 196616 | tf_op jit(solution)/shard_map/ppermute | solution.py:382
  23.3 8.8 %collective-permute-start.8 = (f32[128,128]{1,0:T(8,128)S(1)}, f32[128,128]{1,0:T(8,128)S(1)}, u32[]{:S(2)}, u32[]{:S(2)}) collective-permute-start(f32[128,128]{1,0:T(8,128)S(1)} %pad_maximum_fusion.2), channel_id=1, source_target_pairs={{0,24},{4,28},{8,16},{12,20},{16,8},{20,12},{24,0},{28,4},{1,25},{... | collective-permute-start | bytes 196616 | tf_op jit(solution)/shard_map/ppermute | solution.py:382
  26.1 6.0 %collective-permute-start.6 = (f32[128,128]{1,0:T(8,128)S(1)}, f32[128,128]{1,0:T(8,128)S(1)}, u32[]{:S(2)}, u32[]{:S(2)}) collective-permute-start(f32[128,128]{1,0:T(8,128)S(1)} %pad_maximum_fusion), channel_id=1, source_target_pairs={{0,8},{4,12},{8,0},{12,4},{16,24},{20,28},{24,16},{28,20},{1,9},{5... | collective-permute-start | bytes 196616 | tf_op jit(solution)/shard_map/ppermute | solution.py:382
  26.3 3.0 %collective-permute-start.5 = (f32[80,128]{1,0:T(8,128)S(1)}, f32[80,128]{1,0:T(8,128)S(1)}, u32[]{:S(2)}, u32[]{:S(2)}) collective-permute-start(f32[80,128]{1,0:T(8,128)S(1)} %pad_maximum_fusion.4), channel_id=1, source_target_pairs={{0,4},{4,0},{8,12},{12,8},{16,20},{20,16},{24,28},{28,24},{1,5},{5... | collective-permute-start | bytes 122888 | tf_op jit(solution)/shard_map/ppermute | solution.py:382

commit v13 on v11

--- a/solution.py
+++ b/solution.py
@@ -299,20 +299,22 @@
             [jnp.where(left_half, x, 0.0) for x in weighted] + [jnp.where(left_half, 0.0, x) for x in weighted],
             axis=0,
         ),
-        jnp.concatenate(spreads + spreads + innovations + innovations, axis=0),
+        jnp.concatenate(spreads + innovations, axis=0),
         (((1,), (1,)), ((), ())),
         preferred_element_type=jnp.float32,
         precision=HIGH,
     )
     lane_at = iota((members, LANES), 1)
-    patch_at = lane_at // members
-    gram = jnp.zeros((members, LANES), jnp.float32)
-    proj = jnp.zeros((members, LANES), jnp.float32)
-    for p in range(2 * pairs):
-        mine = patch_at == p
-        block = every[p * members : (p + 1) * members, :]
-        gram = jnp.where(mine, block[:, :LANES], gram)
-        proj = jnp.where(mine, block[:, LANES:], proj)
+    pair_at = lane_at // members % pairs
+    sides = []
+    for side in range(2):
+        total = jnp.zeros((members, LANES), jnp.float32)
+        for i in range(pairs):
+            start = (side * pairs + i) * members
+            total = jnp.where(pair_at == i, every[start : start + members, :], total)
+        sides.append(total)
+    gram = jnp.where(left_half, sides[0], pltpu.roll(sides[1], LANES // 2, 1))
+    proj = jnp.where(left_half, pltpu.roll(sides[0], LANES // 2, 1), sides[1])
 
     starts = lane_at - lane_at % members
     eye = (lane_at % members == iota((members, LANES), 0)).astype(jnp.float32)

time: 49.6 us -> 49.6 us (level)
  no operation moved by 1% of the time
where the time goes in v13:
time: 49.6 us; the launch traced here: 49.3 us
  starting transfers between devices  18.5 us (37%)
  blocking collectives  17.3 us (35%)
  Pallas kernels  8.19 us (17%)
  waiting for transfers between devices  4.24 us (9%)
  local copies, waits for them, and re-layouts  0.88 us (2%)
    all_to_all x1, blocking collectives, body(): lax.all_to_all(analysed, 'member', split_axis=0, concat_axis=0, tiled=True)  17.3 us
    ppermute x7, starting transfers between devices, trade(): lax.ppermute(block, 'member', [(i, i ^ distance) for i in range(members)])  10.5 us
    ppermute x1, starting transfers between devices, swaps(): far = lax.ppermute(far, 'tile', pairs(1))  4.48 us
    ppermute x1, waiting for transfers between devices, swaps(): far = lax.ppermute(far, 'tile', pairs(1))  3.79 us
    all_to_all x1, starting transfers between devices, body(): lax.all_to_all(sends, 'member', split_axis=0, concat_axis=0, tiled=True)  3.41 us
    pallas_call x1, Pallas kernels, body(): pl.pallas_call(functools.partial(weight_kernel, members), out_shape=jax.S...  2.85 us
    pallas_call x1, Pallas kernels, body(): pl.pallas_call(functools.partial(forecast_kernel, (members, own_rows, hal...  2.29 us
    pallas_call x1, Pallas kernels, body(): pl.pallas_call(functools.partial(precision_kernel, (halo, rows, width, ra...  1.32 us
  transfers between devices with their start and end apart: 10, of which 2 were waited for; matrix products, arithmetic and copies ran while one was open for 0% of the time, Pallas kernels for 8%

profile of v13, /device:TPU:1, one launch (start us, length us, event | category | flops | bytes accessed | tf_op | source)
XLA Modules:
  0.0 49.3 jit_solution(12181457653639659405)
XLA Ops:
  0.0 1.2 %edges.1 = (f32[104,512]{1,0:T(8,128)S(1)}, f32[104,512]{1,0:T(8,128)S(1)}) custom-call(f32[4,64,512]{2,1,0:T(8,128)} %bitcast.12, f32[64,512]{1,0:T(8,128)} %depth_ref.1, s32[64,512]{1,0:T(8,128)} %mask_ref.1, s32[32,128]{1,0:T(8,128)} %bitcast.15, f32[32,128]{1,0:T(8,128)} %bitcast.17, f32[32,128]{1,0:T(8,128)} %bitcast.19, f32[32,128]{1,0:T(8,128)} %bitcast.21), custom_call_target="tpu_custom_call" | custom-call | tf_op jit(solution)/shard_map/edges/pallas_call | solution.py:441
  1.2 0.1 collective-permute-start
  1.4 4.5 %collective-permute-start.1 = (f32[104,512]{1,0:T(8,128)S(1)}, f32[104,512]{1,0:T(8,128)S(1)}, u32[]{:S(2)}, u32[]{:S(2)}) collective-permute-start(f32[104,512]{1,0:T(8,128)S(1)} %get-tuple-element.17), channel_id=1, source_target_pairs={{1,2},{2,1},{5,6},{6,5},{9,10},{10,9},{13,14},{14,13},{17,18},{18,... | collective-permute-start | bytes 638984 | tf_op jit(solution)/shard_map/ppermute | solution.py:410
  5.9 3.8 %collective-permute-done.1.far_ref = f32[104,512]{1,0:T(8,128)S(1)} collective-permute-done((f32[104,512]{1,0:T(8,128)S(1)}, f32[104,512]{1,0:T(8,128)S(1)}, u32[]{:S(2)}, u32[]{:S(2)}) %collective-permute-start.1) | collective-permute-done | bytes 213024 | tf_op jit(solution)/shard_map/ppermute | solution.py:410
  9.7 2.3 %forecast.1 = (f32[8,64,128]{2,1,0:T(8,128)}, f32[40,128]{1,0:T(8,128)S(1)}, f32[296,128]{1,0:T(8,128)S(1)}, f32[64,128]{1,0:T(8,128)S(1)}, f32[64,128]{1,0:T(8,...) custom-call(f32[4,64,512]{2,1,0:T(8,128)S(1)} %bitcast.13, f32[64,512]{1,0:T(8,128)S(1)} %copy-done.3, ...), custom_call_target="tpu_custom_call" | custom-call | tf_op jit(solution)/shard_map/forecast/pallas_call | solution.py:468
  12.0 1.9 %collective-permute-start.2 = (f32[296,128]{1,0:T(8,128)S(1)}, f32[296,128]{1,0:T(8,128)S(1)}, u32[]{:S(2)}, u32[]{:S(2)}) collective-permute-start(f32[296,128]{1,0:T(8,128)S(1)} %get-tuple-element.20), channel_id=1, source_target_pairs={{0,4},{4,0},{8,12},{12,8},{16,20},{20,16},{24,28},{28,24},{1,5},{5... | collective-permute-start | bytes 454664 | tf_op jit(solution)/shard_map/ppermute | solution.py:384
  13.9 2.3 %collective-permute-start.3 = (f32[40,128]{1,0:T(8,128)S(1)}, f32[40,128]{1,0:T(8,128)S(1)}, u32[]{:S(2)}, u32[]{:S(2)}) collective-permute-start(f32[40,128]{1,0:T(8,128)S(1)} %get-tuple-element.19), channel_id=1, source_target_pairs={{0,16},{4,20},{8,24},{12,28},{16,0},{20,4},{24,8},{28,12},{1,17},{... | collective-permute-start | bytes 61448 | tf_op jit(solution)/shard_map/ppermute | solution.py:384
  16.2 3.4 %all-to-all-start = ((f32[8,64,128]{2,1,0:T(8,128)}), f32[8,64,128]{2,1,0:T(8,128)S(1)}, u32[]{:S(2)}, u32[]{:S(2)}) async-start(f32[8,64,128]{2,1,0:T(8,128)} %get-tuple-element.18), calls=%async_computation | async-start | bytes 524288 | tf_op jit(solution)/shard_map/all_to_all | solution.py:492
  19.7 0.0 collective-permute-done.2.refs_1_
  19.7 0.0 collective-permute-done.3
  19.7 1.4 %collective-permute-start.4 = (f32[120,128]{1,0:T(8,128)S(1)}, f32[120,128]{1,0:T(8,128)S(1)}, u32[]{:S(2)}, u32[]{:S(2)}) collective-permute-start(f32[120,128]{1,0:T(8,128)S(1)} %pad_maximum_fusion.3.three_ref), channel_id=1, source_target_pairs={{0,8},{4,12},{8,0},{12,4},{16,24},{20,28},{24,16},{28,20},{1,9},{5... | collective-permute-start | bytes 184328 | tf_op jit(solution)/shard_map/ppermute | solution.py:384
  21.1 0.2 collective-permute-start.6
  21.3 2.3 %collective-permute-start.7 = (f32[128,128]{1,0:T(8,128)S(1)}, f32[128,128]{1,0:T(8,128)S(1)}, u32[]{:S(2)}, u32[]{:S(2)}) collective-permute-start(f32[128,128]{1,0:T(8,128)S(1)} %pad_maximum_fusion.1), channel_id=1, source_target_pairs={{0,16},{4,20},{8,24},{12,28},{16,0},{20,4},{24,8},{28,12},{1,17},{... | collective-permute-start | bytes 196616 | tf_op jit(solution)/shard_map/ppermute | solution.py:384
  23.6 1.2 %collective-permute-start.8 = (f32[128,128]{1,0:T(8,128)S(1)}, f32[128,128]{1,0:T(8,128)S(1)}, u32[]{:S(2)}, u32[]{:S(2)}) collective-permute-start(f32[128,128]{1,0:T(8,128)S(1)} %pad_maximum_fusion.2), channel_id=1, source_target_pairs={{0,24},{4,28},{8,16},{12,20},{16,8},{20,12},{24,0},{28,4},{1,25},{... | collective-permute-start | bytes 196616 | tf_op jit(solution)/shard_map/ppermute | solution.py:384
  24.8 0.0 collective-permute-done.4.refs_0_
  24.8 1.3 %collective-permute-start.5 = (f32[80,128]{1,0:T(8,128)S(1)}, f32[80,128]{1,0:T(8,128)S(1)}, u32[]{:S(2)}, u32[]{:S(2)}) collective-permute-start(f32[80,128]{1,0:T(8,128)S(1)} %pad_maximum_fusion.4), channel_id=1, source_target_pairs={{0,4},{4,0},{8,12},{12,8},{16,20},{20,16},{24,28},{28,24},{1,5},{5... | collective-permute-start | bytes 122888 | tf_op jit(solution)/shard_map/ppermute | solution.py:384
  26.0 1.3 %precision.1 = (f32[2,8,128]{2,1,0:T(8,128)S(1)}, s32[8,128]{1,0:T(8,128)S(1)}) custom-call(s32[16,64]{1,0:T(8,128)} %bitcast.23, s32[1,16]{1,0:T(1,128)} %count_ref.1, f32[32,128]{1,0:T(8,128)} %bitcast.20, f32[32,128]{1,0:T(8,128)} %bitcast.22, f32[104,512]{1,0:T(8,128)} %copy-done.1, f32[104,512]{1,0:T(8,128)} %copy-done.2), custom_call_target="tpu_custom_call" | custom-call | tf_op jit(solution)/shard_map/precision/pallas_call | solution.py:496
  27.4 0.4 collective-permute-done.5.last_ref
  27.8 2.9 %weights.1.mix_ref = f32[8,128]{1,0:T(8,128)S(1)} custom-call(f32[120,128]{1,0:T(8,128)S(1)} %pad_maximum_fusion.3.three_ref, f32[80,128]{1,0:T(8,128)S(1)} %collective-permute-done.5.last_ref, f32[120,128]{1,0:T(8,128)S(1)} %collective-permute-done.4.refs_0_, s32[8,128]{1,0:T(8,128)S(1)} %get-tuple-element.21.refs_1_, ...), custom_call_target="tpu_custom_call" | custom-call | tf_op jit(solution)/shard_map/weights/pallas_call | solution.py:511
  30.7 0.0 collective-permute-done.6.refs_2_
  30.7 0.0 all-to-all-done
  30.7 0.5 %mix.1 = f32[8,4,8,512]{3,2,1,0:T(8,128)S(1)} custom-call(f32[512,128]{1,0:T(8,128)S(1)} %bitcast.14, f32[8,128]{1,0:T(8,128)S(1)} %weights.1.mix_ref, f32[64,128]{1,0:T(8,128)S(1)} %get-tuple-element.23.refs_0_, f32[296,128]{1,0:T(8,128)S(1)} %collective-permute-done.2.refs_1_, f32[128,128]{1,0:T(8,128)S(1)} %collective-permute-done.6.refs_2_, ...), custom_call_target="tpu_custom_call" | custom-call | tf_op jit(solution)/shard_map/mix/pallas_call | solution.py:520
  31.2 17.3 %all_to_all.10 = f32[8,4,8,512]{3,2,1,0:T(8,128)S(1)} all-to-all(f32[8,4,8,512]{3,2,1,0:T(8,128)S(1)} %mix.1), channel_id=1, replica_groups=mesh['member'=8,'tile'=4] {'member'}, dimensions={0} | all-to-all | bytes 1048576 | tf_op jit(solution)/shard_map/all_to_all | solution.py:529
  48.5 0.8 %copy_bitcast_fusion = f32[1,4,64,512]{3,2,1,0:T(8,128)} fusion(f32[8,4,8,512]{3,2,1,0:T(8,128)S(1)} %all_to_all.10), kind=kLoop, calls=%fused_computation | loop fusion | bytes 1048576 | tf_op jit(solution)/shard_map/reshape | solution.py:530
  (25 shorter events, 0.1 us)
Async XLA Ops:
  0.0 9.7 %copy-start = (f32[1,4,64,512]{3,2,1,0:T(8,128)S(1)}, f32[1,4,64,512]{3,2,1,0:T(8,128)}, u32[]{:S(2)}) copy-start(f32[1,4,64,512]{3,2,1,0:T(8,128)} %param.9) | copy-start | bytes 1572868
  0.0 9.7 %copy-start.3 = (f32[64,512]{1,0:T(8,128)S(1)}, f32[64,512]{1,0:T(8,128)}, u32[]{:S(2)}) copy-start(f32[64,512]{1,0:T(8,128)} %depth_ref.1) | copy-start | bytes 393220
  0.0 9.7 %copy-start.4 = (s32[64,512]{1,0:T(8,128)S(1)}, s32[64,512]{1,0:T(8,128)}, u32[]{:S(2)}) copy-start(s32[64,512]{1,0:T(8,128)} %mask_ref.1) | copy-start | bytes 393220
  0.0 9.7 %copy-start.5 = (s32[4096]{0:T(1024)S(1)}, s32[4096]{0:T(1024)}, u32[]{:S(2)}) copy-start(s32[4096]{0:T(1024)} %param.12) | copy-start | bytes 49156
  0.0 9.7 %copy-start.6 = (f32[4096]{0:T(1024)S(1)}, f32[4096]{0:T(1024)}, u32[]{:S(2)}) copy-start(f32[4096]{0:T(1024)} %param.15) | copy-start | bytes 49156
  1.2 4.6 %collective-permute-start = (f32[104,512]{1,0:T(8,128)S(1)}, f32[104,512]{1,0:T(8,128)S(1)}, u32[]{:S(2)}, u32[]{:S(2)}) collective-permute-start(f32[104,512]{1,0:T(8,128)S(1)} %get-tuple-element.16), channel_id=1, source_target_pairs={{0,1},{2,3},{1,0},{3,2},{4,5},{6,7},{5,4},{7,6},{8,9},{10,11},{9,8... | collective-permute-start | bytes 638984 | tf_op jit(solution)/shard_map/ppermute | solution.py:411
  1.4 8.3 %collective-permute-start.1 = (f32[104,512]{1,0:T(8,128)S(1)}, f32[104,512]{1,0:T(8,128)S(1)}, u32[]{:S(2)}, u32[]{:S(2)}) collective-permute-start(f32[104,512]{1,0:T(8,128)S(1)} %get-tuple-element.17), channel_id=1, source_target_pairs={{1,2},{2,1},{5,6},{6,5},{9,10},{10,9},{13,14},{14,13},{17,18},{18,... | collective-permute-start | bytes 638984 | tf_op jit(solution)/shard_map/ppermute | solution.py:410
  5.9 6.1 %copy-start.1 = (f32[104,512]{1,0:T(8,128)}, f32[104,512]{1,0:T(8,128)S(1)}, u32[]{:S(2)}) copy-start(f32[104,512]{1,0:T(8,128)S(1)} %collective-permute-done.near_ref) | copy-start | bytes 638980
  9.7 2.3 %copy-start.2 = (f32[104,512]{1,0:T(8,128)}, f32[104,512]{1,0:T(8,128)S(1)}, u32[]{:S(2)}) copy-start(f32[104,512]{1,0:T(8,128)S(1)} %collective-permute-done.1.far_ref) | copy-start | bytes 638980
  12.0 7.7 %collective-permute-start.2 = (f32[296,128]{1,0:T(8,128)S(1)}, f32[296,128]{1,0:T(8,128)S(1)}, u32[]{:S(2)}, u32[]{:S(2)}) collective-permute-start(f32[296,128]{1,0:T(8,128)S(1)} %get-tuple-element.20), channel_id=1, source_target_pairs={{0,4},{4,0},{8,12},{12,8},{16,20},{20,16},{24,28},{28,24},{1,5},{5... | collective-permute-start | bytes 454664 | tf_op jit(solution)/shard_map/ppermute | solution.py:384
  13.9 5.8 %collective-permute-start.3 = (f32[40,128]{1,0:T(8,128)S(1)}, f32[40,128]{1,0:T(8,128)S(1)}, u32[]{:S(2)}, u32[]{:S(2)}) collective-permute-start(f32[40,128]{1,0:T(8,128)S(1)} %get-tuple-element.19), channel_id=1, source_target_pairs={{0,16},{4,20},{8,24},{12,28},{16,0},{20,4},{24,8},{28,12},{1,17},{... | collective-permute-start | bytes 61448 | tf_op jit(solution)/shard_map/ppermute | solution.py:384
  16.2 14.5 %all-to-all-start = ((f32[8,64,128]{2,1,0:T(8,128)}), f32[8,64,128]{2,1,0:T(8,128)S(1)}, u32[]{:S(2)}, u32[]{:S(2)}) async-start(f32[8,64,128]{2,1,0:T(8,128)} %get-tuple-element.18), calls=%async_computation | async-start | bytes 524288 | tf_op jit(solution)/shard_map/all_to_all | solution.py:492
  19.7 5.1 %collective-permute-start.4 = (f32[120,128]{1,0:T(8,128)S(1)}, f32[120,128]{1,0:T(8,128)S(1)}, u32[]{:S(2)}, u32[]{:S(2)}) collective-permute-start(f32[120,128]{1,0:T(8,128)S(1)} %pad_maximum_fusion.3.three_ref), channel_id=1, source_target_pairs={{0,8},{4,12},{8,0},{12,4},{16,24},{20,28},{24,16},{28,20},{1,9},{5... | collective-permute-start | bytes 184328 | tf_op jit(solution)/shard_map/ppermute | solution.py:384
  21.1 9.5 %collective-permute-start.6 = (f32[128,128]{1,0:T(8,128)S(1)}, f32[128,128]{1,0:T(8,128)S(1)}, u32[]{:S(2)}, u32[]{:S(2)}) collective-permute-start(f32[128,128]{1,0:T(8,128)S(1)} %pad_maximum_fusion), channel_id=1, source_target_pairs={{0,8},{4,12},{8,0},{12,4},{16,24},{20,28},{24,16},{28,20},{1,9},{5... | collective-permute-start | bytes 196616 | tf_op jit(solution)/shard_map/ppermute | solution.py:384
  21.3 9.3 %collective-permute-start.7 = (f32[128,128]{1,0:T(8,128)S(1)}, f32[128,128]{1,0:T(8,128)S(1)}, u32[]{:S(2)}, u32[]{:S(2)}) collective-permute-start(f32[128,128]{1,0:T(8,128)S(1)} %pad_maximum_fusion.1), channel_id=1, source_target_pairs={{0,16},{4,20},{8,24},{12,28},{16,0},{20,4},{24,8},{28,12},{1,17},{... | collective-permute-start | bytes 196616 | tf_op jit(solution)/shard_map/ppermute | solution.py:384
  23.6 7.1 %collective-permute-start.8 = (f32[128,128]{1,0:T(8,128)S(1)}, f32[128,128]{1,0:T(8,128)S(1)}, u32[]{:S(2)}, u32[]{:S(2)}) collective-permute-start(f32[128,128]{1,0:T(8,128)S(1)} %pad_maximum_fusion.2), channel_id=1, source_target_pairs={{0,24},{4,28},{8,16},{12,20},{16,8},{20,12},{24,0},{28,4},{1,25},{... | collective-permute-start | bytes 196616 | tf_op jit(solution)/shard_map/ppermute | solution.py:384
  24.8 3.0 %collective-permute-start.5 = (f32[80,128]{1,0:T(8,128)S(1)}, f32[80,128]{1,0:T(8,128)S(1)}, u32[]{:S(2)}, u32[]{:S(2)}) collective-permute-start(f32[80,128]{1,0:T(8,128)S(1)} %pad_maximum_fusion.4), channel_id=1, source_target_pairs={{0,4},{4,0},{8,12},{12,8},{16,20},{20,16},{24,28},{28,24},{1,5},{5... | collective-permute-start | bytes 122888 | tf_op jit(solution)/shard_map/ppermute | solution.py:384
